TPU v7x, 32 devices: a whole 2x2x4 slice. The times are simulated.
32 devices in a mesh: brick: 8 (over y, x, core), scan: 4 (over z).
Axes of the slice: x: 2, y: 2, z: 4, core: 2. Of those that a mesh axis runs over, the one named last changes fastest.
Arguments:
- tomogram: bfloat16 [256, 128, 128], P(('brick', 'scan')), may hold values from -6 to 6
- deformed: bfloat16 [4, 256, 128, 128], P('scan', 'brick'), may hold values from -6 to 6
- subvoxel: float32 [4, 3, 8, 25], P('scan', None, 'brick'), may hold values from 0 to 0.99
- offsets: int32 [4, 3, 128], P('scan', None, 'brick'), may hold values from -15 to 15, as said below
Outputs:
- residual_map: bfloat16 [4, 256, 128, 128], P('scan', 'brick')
- node_rhs: float32 [4, 3, 8, 25], P('scan', None, 'brick')
Inputs may be any that keep to these rules, and one draw needn't show every extreme that they name: offsets[k, c, e] lies in -(15) .. 15 and both ends occur.
All inputs are finite; a program needn't handle non-finite values.
Results may differ from a plain program's by a relative error of at most 0.0095.
Values may be sent and summed in bfloat16 or wider, within the bound.
No kernel may reach another device: no remote copies, remote signals or barrier semaphores. Data moves between devices by JAX's collectives and lax.ppermute only.
A program may use at most 128 MiB of HBM per device.

v0:
```python
import jax
import jax.numpy as jnp
from jax import lax
from jax.sharding import PartitionSpec as P

E = 32
HALO = 16
RADIUS = 3


gauss_sigma = 1.0


def padded_2(cells, sides, width):
    for axis, dim in sides:
        count = lax.axis_size(axis)
        ends = count - 1
        head = lax.slice_in_dim(cells, 0, width, axis=dim)
        tail = lax.slice_in_dim(cells, cells.shape[dim] - width, cells.shape[dim], axis=dim)
        cells = jnp.concatenate(
            [
                lax.ppermute(tail, axis, [(i, (i + 1) % count) for i in range(ends)]),
                cells,
                lax.ppermute(head, axis, [((i + 1) % count, i) for i in range(ends)]),
            ],
            axis=dim,
        )
    return cells


def passed_along(block, axis, distance):
    devices = range(lax.axis_size(axis))
    route = [(i - distance, i) for i in devices if i - distance in devices]
    return lax.ppermute(block, axis, route)


def filter_taps():
    tap_pos = jnp.arange(-RADIUS, RADIUS + 1).astype(jnp.float32)
    gaussian = jnp.exp(-tap_pos * tap_pos / (2.0 * gauss_sigma * gauss_sigma))
    smooth_taps = gaussian / jnp.sum(gaussian)
    slope_taps = tap_pos * gaussian / jnp.sum(tap_pos * tap_pos * gaussian)
    return (smooth_taps.astype(jnp.bfloat16), slope_taps.astype(jnp.bfloat16))


def band_matrix(coeff, cross_width):
    distance = jnp.arange(cross_width)[:, None] - jnp.arange(cross_width)[None, :]
    band_table = jnp.zeros((cross_width, cross_width), jnp.float32)
    for tap in range(2 * RADIUS + 1):
        band_table = band_table + jnp.where(
            distance == tap - RADIUS, coeff[tap].astype(jnp.float32), jnp.float32(0.0)
        )
    return band_table.astype(jnp.bfloat16)


def z_stencil(field, coeff, planes):
    stencil_sum = jnp.zeros((planes,) + field.shape[1:], jnp.float32)
    for tap in range(2 * RADIUS + 1):
        stencil_sum = stencil_sum + coeff[tap].astype(jnp.float32) * field[
            tap : tap + planes
        ].astype(jnp.float32)
    return stencil_sum.astype(jnp.bfloat16)


def gradients(extended):
    smooth_taps, slope_taps = filter_taps()
    cross_width = extended.shape[2]
    planes = extended.shape[0] - 2 * RADIUS
    along_s = band_matrix(smooth_taps, cross_width)
    along_d = band_matrix(slope_taps, cross_width)
    both_bands = jnp.concatenate([along_s, along_d], axis=1)
    x_filtered = jnp.dot(
        extended.reshape(-1, cross_width), both_bands, preferred_element_type=jnp.float32
    )
    x_filtered = x_filtered.astype(jnp.bfloat16).reshape(
        extended.shape[0], extended.shape[1], 2 * cross_width
    )
    y_smoothed = jnp.einsum(
        "zyx,yw->zwx", x_filtered, along_s, preferred_element_type=jnp.float32
    ).astype(jnp.bfloat16)
    y_slope = jnp.einsum(
        "zyx,yw->zwx", x_filtered[:, :, :cross_width], along_d, preferred_element_type=jnp.float32
    ).astype(jnp.bfloat16)
    grad_z = z_stencil(y_smoothed[:, :, :cross_width], slope_taps, planes)
    grad_y = z_stencil(y_slope, smooth_taps, planes)
    grad_x = z_stencil(y_smoothed[:, :, cross_width:], smooth_taps, planes)
    return (grad_z, grad_y, grad_x)


def shape_table(edge_len):
    position = (jnp.arange(edge_len).astype(jnp.float32) + 0.5) / edge_len
    return jnp.stack([1.0 - position, position], axis=1)


def layer_terms(padded, z_start, ref_layer, grad_layer, node_pair, layer_offsets):
    edge_len = ref_layer.shape[0]
    cross_width = ref_layer.shape[1]
    per_row = cross_width // edge_len
    ref_blocks = ref_layer.reshape(edge_len, per_row, edge_len, per_row, edge_len).transpose(
        1, 3, 0, 2, 4
    )
    ref_blocks = ref_blocks.reshape(per_row * per_row, edge_len, edge_len, edge_len)
    grad_blocks = grad_layer.reshape(3, edge_len, per_row, edge_len, per_row, edge_len).transpose(
        2, 4, 0, 1, 3, 5
    )
    grad_blocks = grad_blocks.reshape(per_row * per_row, 3, edge_len, edge_len, edge_len)
    picked_nodes = []
    for j in range(2):
        for k in range(2):
            picked_nodes.append(node_pair[:, :, j : j + per_row, k : k + per_row])
    corner_nodes = jnp.stack(picked_nodes, axis=2).reshape(3, 2, 2, 2, per_row, per_row)
    corner_nodes = corner_nodes.transpose(4, 5, 0, 1, 2, 3).reshape(per_row * per_row, 3, 2, 2, 2)
    element_ids = jnp.arange(per_row * per_row, dtype=jnp.int32)
    starts_z = z_start + layer_offsets[0] + HALO
    starts_y = element_ids // per_row * edge_len + layer_offsets[1] + HALO
    starts_x = element_ids % per_row * edge_len + layer_offsets[2] + HALO

    def cut_window(start_z, start_y, start_x):
        return lax.dynamic_slice(
            padded, (start_z, start_y, start_x), (edge_len + 1, edge_len + 1, edge_len + 1)
        )

    windows = jax.vmap(cut_window)(starts_z, starts_y, starts_x).astype(jnp.float32)
    shapes = shape_table(edge_len)
    subvoxel_field = jnp.einsum(
        "enijk,ai,bj,ck->enabc",
        corner_nodes,
        shapes,
        shapes,
        shapes,
        precision=lax.Precision.HIGHEST,
    )
    warped = jnp.zeros((per_row * per_row, edge_len, edge_len, edge_len), jnp.float32)
    for corner_z in range(2):
        weight_z = subvoxel_field[:, 0] if corner_z else 1.0 - subvoxel_field[:, 0]
        for corner_y in range(2):
            weight_y = subvoxel_field[:, 1] if corner_y else 1.0 - subvoxel_field[:, 1]
            for corner_x in range(2):
                weight_x = subvoxel_field[:, 2] if corner_x else 1.0 - subvoxel_field[:, 2]
                sample = windows[
                    :,
                    corner_z : corner_z + edge_len,
                    corner_y : corner_y + edge_len,
                    corner_x : corner_x + edge_len,
                ]
                warped = warped + weight_z * weight_y * weight_x * sample
    misfit = warped - ref_blocks.astype(jnp.float32)
    products = grad_blocks.astype(jnp.float32) * misfit[:, None]
    element_rhs = jnp.einsum(
        "enabc,ai,bj,ck->enijk", products, shapes, shapes, shapes, precision=lax.Precision.HIGHEST
    ) * (1.0 / edge_len)
    misfit_layer = misfit.reshape(per_row, per_row, edge_len, edge_len, edge_len).transpose(
        2, 0, 3, 1, 4
    )
    misfit_layer = misfit_layer.reshape(edge_len, cross_width, cross_width)
    corner_sums = element_rhs.reshape(per_row, per_row, 3, 2, 2, 2)
    planes = jnp.zeros((3, 2, per_row + 1, per_row + 1), jnp.float32)
    for j in range(2):
        for k in range(2):
            placed = corner_sums[:, :, :, :, j, k].transpose(2, 3, 0, 1)
            planes = planes + jnp.pad(placed, ((0, 0), (0, 0), (j, 1 - j), (k, 1 - k)))
    return (misfit_layer, planes.reshape(3, 2, (per_row + 1) * (per_row + 1)))


def body(tomogram, deformed, subvoxel, offsets):
    ref_slab = lax.all_gather(tomogram, "scan", axis=0, tiled=True)
    extended = padded_2(ref_slab, (("brick", 0),), RADIUS)
    grad_z, grad_y, grad_x = gradients(extended)
    gradient_all = jnp.stack([grad_z, grad_y, grad_x])
    node_above = passed_along(subvoxel, "brick", -1)
    nodes_all = jnp.concatenate([subvoxel, node_above], axis=2)
    rimmed = padded_2(deformed, (("brick", 1),), HALO)
    padded_all = jnp.pad(rimmed, ((0, 0), (0, 0), (HALO, HALO), (HALO, HALO)))
    cross_width = tomogram.shape[1]
    per_row = cross_width // E
    layers = ref_slab.shape[0] // E

    def one_scan(scan_items):
        padded, node_values, scan_offsets = scan_items
        node_grid = node_values.reshape(3, layers + 1, per_row + 1, per_row + 1)

        def one_layer(layer_index):
            return layer_terms(
                padded, layer_index * E, ref_slab, gradient_all, node_grid, scan_offsets
            )

        misfits, planes = lax.map(one_layer, jnp.arange(layers, dtype=jnp.int32))
        residual_scan = misfits.reshape(layers * E, cross_width, cross_width).astype(jnp.bfloat16)
        zero_plane = jnp.zeros((1, 3, planes.shape[-1]), jnp.float32)
        stacked = jnp.concatenate([planes[:, :, 0], zero_plane], axis=0) + jnp.concatenate(
            [zero_plane, planes[:, :, 1]], axis=0
        )
        return (residual_scan, stacked.transpose(1, 0, 2))

    residual_map, local_rhs = lax.map(one_scan, (padded_all, nodes_all, offsets))
    passed = passed_along(local_rhs[:, :, layers:], "brick", 1)
    node_rhs = local_rhs[:, :, :layers] + jnp.concatenate(
        [passed, jnp.zeros_like(local_rhs[:, :, 1:layers])], axis=2
    )
    return (residual_map, node_rhs)


def solution(mesh):
    return jax.shard_map(
        body,
        mesh=mesh,
        in_specs=(
            P(("brick", "scan"), None, None),
            P("scan", "brick", None, None),
            P("scan", None, "brick", None),
            P("scan", None, "brick"),
        ),
        out_specs=(P("scan", "brick", None, None), P("scan", None, "brick", None)),
        check_vma=False,
    )
```

profile of v0, /device:TPU:11, one launch (start us, length us, event | category | flops | bytes accessed | tf_op | source)
XLA Modules:
  0.0 348.7 jit_solution(670476737531864867)
XLA Ops:
  35.4 42.8 %convolution_bitcast_fusion = f32[16,3,32,32,32]{4,3,1,0,2:T(8,128)} fusion(f32[32,16,3,2,32]{4,0,3,2,1:T(8,128)S(1)} %fusion.24, f32[32,1]{0,1:T(1,128)S(1)} %get-tuple-element.110, f32[32,1]{0,1:T(1,128)S(1)} %get-tuple-element.111), kind=kOutput, calls=%fused_computation.13 | convolution fusion | flops 37748800 | bytes 6684928 | tf_op jit(solution)/shard_map/while/body/eval_jaxpr/while/body/eval_jaxpr/enijk,ai,bj,ck->enabc/dot_general | solution.py:124
  78.2 8.3 %fusion.13 = bf16[64,160,160]{2,1,0:T(8,128)(2,1)} fusion(bf16[1,16,128,128]{3,2,1,0:T(8,128)(2,1)S(1)} %collective-permute-done.2, bf16[1,32,128,128]{3,2,1,0:T(8,128)(2,1)S(1)} %copy-done.1, bf16[1,16,128,128]{3,2,1,0:T(8,128)(2,1)S(1)} %collective-permute-done.1), kind=kLoop, calls=%fused_computation.37 | loop fusion | flops 31129600 | bytes 5373952 | tf_op jit(solution)/shard_map/while/body/jit(dynamic_index_in_dim)/squeeze | solution.py:194
  86.5 77.1 %while.4 = (s32[]{:T(128)}, bf16[64,160,160]{2,1,0:T(8,128)(2,1)}, s32[16,3]{0,1:T(4,128)S(1)}, bf16[16,33,33,33]{3,2,0,1:T(8,128)(2,1)}, s32[]{:T(128)}) while((s32[]{:T(128)}, bf16[64,160,160]{2,1,0:T(8,128)(2,1)}, s32[16,3]{0,1:T(4,128)S(1)}, bf16[16,33,33,33]{3,2,0,1:T(8,128)(2,1)}, s32[]{:T(128)}) %tuple.55), condition=%wide.while_cond, body=%wide.while_body.sunk | while | flops 2 | bytes 677501 | solution.py:118
  87.2 4.2 %bitcast_dynamic-update-slice_fusion.2 = bf16[16,33,33,33]{3,2,0,1:T(8,128)(2,1)} fusion(bf16[16,33,33,33]{3,2,0,1:T(8,128)(2,1)} %get-tuple-element.153, s32[]{:T(128)S(6)} %copy.86, bf16[64,160,160]{2,1,0:T(8,128)(2,1)} %get-tuple-element.156, s32[]{:T(128)} %bitcast.159, s32[]{:T(128)} %bitcast.160, s32[]{:T(128)} %bitcast.161), kind=kLoop, calls=%fused_computation.clone.1 | loop fusion | bytes 677380 | tf_op jit(solution)/shard_map/while/body/eval_jaxpr/while/body/eval_jaxpr/vmap()/gather
  101.6 4.2 %bitcast_dynamic-update-slice_fusion.2 = bf16[16,33,33,33]{3,2,0,1:T(8,128)(2,1)} fusion(bf16[16,33,33,33]{3,2,0,1:T(8,128)(2,1)} %get-tuple-element.153, s32[]{:T(128)S(6)} %copy.86, bf16[64,160,160]{2,1,0:T(8,128)(2,1)} %get-tuple-element.156, s32[]{:T(128)} %bitcast.159, s32[]{:T(128)} %bitcast.160, s32[]{:T(128)} %bitcast.161), kind=kLoop, calls=%fused_computation.clone.1 | loop fusion | bytes 677380 | tf_op jit(solution)/shard_map/while/body/eval_jaxpr/while/body/eval_jaxpr/vmap()/gather
  111.3 4.2 %bitcast_dynamic-update-slice_fusion.2 = bf16[16,33,33,33]{3,2,0,1:T(8,128)(2,1)} fusion(bf16[16,33,33,33]{3,2,0,1:T(8,128)(2,1)} %get-tuple-element.153, s32[]{:T(128)S(6)} %copy.86, bf16[64,160,160]{2,1,0:T(8,128)(2,1)} %get-tuple-element.156, s32[]{:T(128)} %bitcast.159, s32[]{:T(128)} %bitcast.160, s32[]{:T(128)} %bitcast.161), kind=kLoop, calls=%fused_computation.clone.1 | loop fusion | bytes 677380 | tf_op jit(solution)/shard_map/while/body/eval_jaxpr/while/body/eval_jaxpr/vmap()/gather
  135.3 4.1 %bitcast_dynamic-update-slice_fusion.2 = bf16[16,33,33,33]{3,2,0,1:T(8,128)(2,1)} fusion(bf16[16,33,33,33]{3,2,0,1:T(8,128)(2,1)} %get-tuple-element.153, s32[]{:T(128)S(6)} %copy.86, bf16[64,160,160]{2,1,0:T(8,128)(2,1)} %get-tuple-element.156, s32[]{:T(128)} %bitcast.159, s32[]{:T(128)} %bitcast.160, s32[]{:T(128)} %bitcast.161), kind=kLoop, calls=%fused_computation.clone.1 | loop fusion | bytes 677380 | tf_op jit(solution)/shard_map/while/body/eval_jaxpr/while/body/eval_jaxpr/vmap()/gather
  140.1 4.2 %bitcast_dynamic-update-slice_fusion.2 = bf16[16,33,33,33]{3,2,0,1:T(8,128)(2,1)} fusion(bf16[16,33,33,33]{3,2,0,1:T(8,128)(2,1)} %get-tuple-element.153, s32[]{:T(128)S(6)} %copy.86, bf16[64,160,160]{2,1,0:T(8,128)(2,1)} %get-tuple-element.156, s32[]{:T(128)} %bitcast.159, s32[]{:T(128)} %bitcast.160, s32[]{:T(128)} %bitcast.161), kind=kLoop, calls=%fused_computation.clone.1 | loop fusion | bytes 677380 | tf_op jit(solution)/shard_map/while/body/eval_jaxpr/while/body/eval_jaxpr/vmap()/gather
  145.0 4.2 %bitcast_dynamic-update-slice_fusion.2 = bf16[16,33,33,33]{3,2,0,1:T(8,128)(2,1)} fusion(bf16[16,33,33,33]{3,2,0,1:T(8,128)(2,1)} %get-tuple-element.153, s32[]{:T(128)S(6)} %copy.86, bf16[64,160,160]{2,1,0:T(8,128)(2,1)} %get-tuple-element.156, s32[]{:T(128)} %bitcast.159, s32[]{:T(128)} %bitcast.160, s32[]{:T(128)} %bitcast.161), kind=kLoop, calls=%fused_computation.clone.1 | loop fusion | bytes 677380 | tf_op jit(solution)/shard_map/while/body/eval_jaxpr/while/body/eval_jaxpr/vmap()/gather
  154.6 4.1 %bitcast_dynamic-update-slice_fusion.2 = bf16[16,33,33,33]{3,2,0,1:T(8,128)(2,1)} fusion(bf16[16,33,33,33]{3,2,0,1:T(8,128)(2,1)} %get-tuple-element.153, s32[]{:T(128)S(6)} %copy.86, bf16[64,160,160]{2,1,0:T(8,128)(2,1)} %get-tuple-element.156, s32[]{:T(128)} %bitcast.159, s32[]{:T(128)} %bitcast.160, s32[]{:T(128)} %bitcast.161), kind=kLoop, calls=%fused_computation.clone.1 | loop fusion | bytes 677380 | tf_op jit(solution)/shard_map/while/body/eval_jaxpr/while/body/eval_jaxpr/vmap()/gather
  159.4 4.2 %bitcast_dynamic-update-slice_fusion.2 = bf16[16,33,33,33]{3,2,0,1:T(8,128)(2,1)} fusion(bf16[16,33,33,33]{3,2,0,1:T(8,128)(2,1)} %get-tuple-element.153, s32[]{:T(128)S(6)} %copy.86, bf16[64,160,160]{2,1,0:T(8,128)(2,1)} %get-tuple-element.156, s32[]{:T(128)} %bitcast.159, s32[]{:T(128)} %bitcast.160, s32[]{:T(128)} %bitcast.161), kind=kLoop, calls=%fused_computation.clone.1 | loop fusion | bytes 677380 | tf_op jit(solution)/shard_map/while/body/eval_jaxpr/while/body/eval_jaxpr/vmap()/gather
  163.6 7.9 %convert_element_type.294 = f32[16,33,33,33]{3,2,0,1:T(8,128)} convert(bf16[16,33,33,33]{3,2,0,1:T(8,128)(2,1)} %get-tuple-element.65) | non-fusion elementwise | flops 574992 | bytes 3449952 | tf_op jit(solution)/shard_map/while/body/eval_jaxpr/while/body/eval_jaxpr/convert_element_type | solution.py:122
  171.5 7.1 %reshape.306 = f32[32,4,32,4,32]{4,3,2,1,0:T(4,128)} reshape(bf16[32,128,128]{2,1,0:T(8,128)(2,1)} %all-gather.2.cloned.1.call-done) | data formatting | bytes 3145728 | tf_op jit(solution)/shard_map/while/body/eval_jaxpr/while/body/eval_jaxpr/convert_element_type | solution.py:146
  178.6 8.0 %copy.37 = f32[32,4,32,4,32]{4,2,3,1,0:T(8,128)} copy(f32[32,4,32,4,32]{4,3,2,1,0:T(4,128)} %reshape.306) | data formatting | bytes 4194304 | tf_op jit(solution)/shard_map/while/body/eval_jaxpr/while/body/eval_jaxpr/convert_element_type | solution.py:146
  188.5 4.5 %collective-permute-start.3 = (bf16[3,128,128]{2,1,0:T(8,128)(2,1)S(1)}, bf16[3,128,128]{2,1,0:T(8,128)(2,1)S(1)}, u32[]{:S(2)}, u32[]{:S(2)}) collective-permute-start(bf16[3,128,128]{2,1,0:T(8,128)(2,1)S(1)} %get-tuple-element.79), channel_id=1, source_target_pairs={{0,4},{4,8},{8,12},{12,16},{16,20},{20,24},{24,28},{1,5},{5,9},{9,... | collective-permute-start | bytes 294920 | tf_op jit(solution)/shard_map/ppermute | solution.py:22
  193.1 43.0 %fusion.63 = (bf16[16,32,32,32]{3,2,0,1:T(8,128)(2,1)}, f32[16,32,32,32]{3,2,0,1:T(8,128)}) fusion(f32[16,32,32,32]{3,2,0,1:T(8,128)} %bitcast.164, f32[16,33,33,33]{3,2,0,1:T(8,128)} %convert_element_type.294, f32[16,3,32,32,32]{4,3,1,0,2:T(8,128)} %convolution_bitcast_fusion), kind=kLoop, calls=%fused_computation.131 | loop fusion | flops 16777216 | bytes 28311552 | tf_op jit(solution)/shard_map/while/body/eval_jaxpr/convert_element_type | solution.py:187
  244.7 5.0 %copy.41 = bf16[1,32,4,32,4,32]{5,3,1,0,4,2:T(8,128)(2,1)} copy(bf16[1,32,4,32,4,32]{5,4,3,2,1,0:T(4,128)(2,1)} %stack.56) | data formatting | bytes 2097152 | tf_op jit(solution)/shard_map/stack | solution.py:168
  254.6 4.9 %copy.40 = bf16[1,32,4,32,4,32]{5,3,1,0,4,2:T(8,128)(2,1)} copy(bf16[1,32,4,32,4,32]{5,4,3,2,1,0:T(4,128)(2,1)} %stack.55) | data formatting | bytes 2097152 | tf_op jit(solution)/shard_map/stack | solution.py:168
  262.8 5.1 %copy.39 = bf16[1,32,4,32,4,32]{5,3,1,0,4,2:T(8,128)(2,1)} copy(bf16[1,32,4,32,4,32]{5,4,3,2,1,0:T(4,128)(2,1)} %stack.54) | data formatting | bytes 2097152 | tf_op jit(solution)/shard_map/stack | solution.py:168
  267.9 7.9 %maximum_convert_fusion = f32[3,32,4,32,4,32]{5,3,1,0,4,2:T(8,128)S(1)} fusion(bf16[1,32,4,32,4,32]{5,3,1,0,4,2:T(8,128)(2,1)} %copy.41, bf16[1,32,4,32,4,32]{5,3,1,0,4,2:T(8,128)(2,1)} %copy.40, bf16[1,32,4,32,4,32]{5,3,1,0,4,2:T(8,128)(2,1)} %copy.39), kind=kLoop, calls=%fused_computation.9 | loop fusion | flops 4718592 | bytes 9437184 | tf_op jit(solution)/shard_map/while/body/eval_jaxpr/while/body/eval_jaxpr/convert_element_type | solution.py:147
  275.8 13.3 %bitcast_multiply_fusion = f32[16,3,32,32,32]{4,3,2,1,0:T(8,128)} fusion(f32[3,32,4,32,4,32]{5,3,1,0,4,2:T(8,128)S(1)} %maximum_convert_fusion, f32[16,32,32,32]{3,2,0,1:T(8,128)S(1)} %bitcast.163), kind=kLoop, calls=%fused_computation.2 | loop fusion | flops 1572864 | bytes 14680064 | tf_op jit(solution)/shard_map/while/body/eval_jaxpr/while/body/eval_jaxpr/mul | solution.py:147
  289.1 32.8 %fusion = f32[2,16,3,32,32]{4,0,3,2,1:T(2,128)S(1)} fusion(f32[16,3,32,32,32]{4,3,2,1,0:T(8,128)} %bitcast_multiply_fusion, f32[32,1]{0,1:T(1,128)S(1)} %get-tuple-element.110, f32[32,1]{0,1:T(1,128)S(1)} %get-tuple-element.111), kind=kOutput, calls=%fused_computation.3 | convolution fusion | flops 37748800 | bytes 6684928 | tf_op jit(solution)/shard_map/while/body/eval_jaxpr/while/body/eval_jaxpr/enabc,ai,bj,ck->enijk/dot_general | solution.py:148
  326.6 8.4 %copy.38 = bf16[32,4,32,4,32]{4,3,2,1,0:T(4,128)(2,1)} copy(bf16[32,4,32,4,32]{4,2,3,1,0:T(8,128)(2,1)} %bitcast.167) | data formatting | bytes 2097152 | tf_op jit(solution)/shard_map/while/body/eval_jaxpr/convert_element_type | solution.py:187
  335.0 6.0 %convert_element_type.302 = bf16[1,32,128,128]{3,2,1,0:T(8,128)(2,1)} reshape(bf16[32,4,32,4,32]{4,3,2,1,0:T(4,128)(2,1)} %copy.38) | data formatting | bytes 2097152 | tf_op jit(solution)/shard_map/while/body/eval_jaxpr/convert_element_type | solution.py:187
  (108 shorter events, 86.8 us)
Async XLA Ops:
  7.2 164.4 %all-gather.2.cloned.1.call-start = ((), (), s32[]{:S(2)}) async-start(), calls=%async_computation | async-start | bytes 1310720 | tf_op jit(solution)/shard_map/all_gather | solution.py:165
  9.2 69.0 %collective-permute-start.2 = (bf16[1,16,128,128]{3,2,1,0:T(8,128)(2,1)S(1)}, bf16[1,16,128,128]{3,2,1,0:T(8,128)(2,1)S(1)}, u32[]{:S(2)}, u32[]{:S(2)}) collective-permute-start(bf16[1,16,128,128]{3,2,1,0:T(8,128)(2,1)S(1)} %get-tuple-element.82), channel_id=1, source_target_pairs={{4,0},{8,4},{12,8},{16,12},{20,16},{24,20},{28,24},{5,1},{9,5},{13... | collective-permute-start | bytes 1572872 | tf_op jit(solution)/shard_map/ppermute | solution.py:24
  11.8 66.4 %collective-permute-start.1 = (bf16[1,16,128,128]{3,2,1,0:T(8,128)(2,1)S(1)}, bf16[1,16,128,128]{3,2,1,0:T(8,128)(2,1)S(1)}, u32[]{:S(2)}, u32[]{:S(2)}) collective-permute-start(bf16[1,16,128,128]{3,2,1,0:T(8,128)(2,1)S(1)} %get-tuple-element.81), channel_id=1, source_target_pairs={{0,4},{4,8},{8,12},{12,16},{16,20},{20,24},{24,28},{1,5},{5,9},{9,... | collective-permute-start | bytes 1572872 | tf_op jit(solution)/shard_map/ppermute | solution.py:22
  15.7 15.7 %collective-permute-start = (f32[1,3,1,25]{3,2,1,0:T(1,128)}, f32[1,3,1,25]{3,2,1,0:T(1,128)S(1)}, u32[]{:S(2)}, u32[]{:S(2)}) collective-permute-start(f32[1,3,1,25]{3,2,1,0:T(1,128)} %param.6), channel_id=1, source_target_pairs={{4,0},{8,4},{12,8},{16,12},{20,16},{24,20},{28,24},{5,1},{9,5},{13... | collective-permute-start | bytes 908 | tf_op jit(solution)/shard_map/ppermute | solution.py:34
  35.4 42.8 %copy-start.1 = (bf16[1,32,128,128]{3,2,1,0:T(8,128)(2,1)S(1)}, bf16[1,32,128,128]{3,2,1,0:T(8,128)(2,1)}, u32[]{:S(2)}) copy-start(bf16[1,32,128,128]{3,2,1,0:T(8,128)(2,1)} %param.5) | copy-start | bytes 3145732
  178.6 8.0 %copy-start = (bf16[32,128,128]{2,1,0:T(8,128)(2,1)S(1)}, bf16[32,128,128]{2,1,0:T(8,128)(2,1)}, u32[]{:S(2)}) copy-start(bf16[32,128,128]{2,1,0:T(8,128)(2,1)} %all-gather.2.cloned.1.call-done) | copy-start | bytes 3145732
  186.6 49.5 %collective-permute-start.4 = (bf16[3,128,128]{2,1,0:T(8,128)(2,1)S(1)}, bf16[3,128,128]{2,1,0:T(8,128)(2,1)S(1)}, u32[]{:S(2)}, u32[]{:S(2)}) collective-permute-start(bf16[3,128,128]{2,1,0:T(8,128)(2,1)S(1)} %get-tuple-element.80), channel_id=1, source_target_pairs={{4,0},{8,4},{12,8},{16,12},{20,16},{24,20},{28,24},{5,1},{9,5},{13... | collective-permute-start | bytes 294920 | tf_op jit(solution)/shard_map/ppermute | solution.py:24
  188.5 47.6 %collective-permute-start.3 = (bf16[3,128,128]{2,1,0:T(8,128)(2,1)S(1)}, bf16[3,128,128]{2,1,0:T(8,128)(2,1)S(1)}, u32[]{:S(2)}, u32[]{:S(2)}) collective-permute-start(bf16[3,128,128]{2,1,0:T(8,128)(2,1)S(1)} %get-tuple-element.79), channel_id=1, source_target_pairs={{0,4},{4,8},{8,12},{12,16},{16,20},{20,24},{24,28},{1,5},{5,9},{9,... | collective-permute-start | bytes 294920 | tf_op jit(solution)/shard_map/ppermute | solution.py:22
  262.8 12.9 %slice-start = ((s8[8388608]{0:T(1024)(128)(4,1)}), s8[4194304]{0:T(1024)(128)(4,1)S(1)}, s32[]{:S(2)}) async-start(s8[8388608]{0:T(1024)(128)(4,1)} %bitcast.162), calls=%async_computation.1 | async-start | bytes 8388608
  267.9 7.9 %slice-start.1 = ((s8[8388608]{0:T(1024)(128)(4,1)}), s8[4194304]{0:T(1024)(128)(4,1)S(1)}, s32[]{:S(2)}) async-start(s8[8388608]{0:T(1024)(128)(4,1)} %bitcast.162), calls=%async_computation.2 | async-start | bytes 8388608
  324.0 17.0 %collective-permute-start.5 = (f32[1,3,1,25]{3,2,1,0:T(1,128)S(1)}, f32[1,3,1,25]{3,2,1,0:T(1,128)S(1)}, u32[]{:S(2)}, u32[]{:S(2)}) collective-permute-start(f32[1,3,1,25]{3,2,1,0:T(1,128)S(1)} %slice.422), channel_id=1, source_target_pairs={{0,4},{4,8},{8,12},{12,16},{16,20},{20,24},{24,28},{1,5},{5,9},{9,... | collective-permute-start | bytes 908 | tf_op jit(solution)/shard_map/ppermute | solution.py:34
Sparse Core Ops, SparseCore 0:
  9.6 28.8 all-gather.1
where the time goes:
time: 354 us; the launch traced here: 349 us
  local copies, waits for them, and re-layouts  135 us (38%)
  other arithmetic  89.9 us (25%)
  matrix products  82.5 us (23%)
  between operations  23.5 us (7%)
  starting transfers between devices  17.5 us (5%)
    gather x48, local copies, waits for them, and re-layouts  77.1 us
    dot_general x3, matrix products, layer_terms(): jnp.einsum('enijk,ai,bj,ck->enabc', corner_nodes, shapes, shapes, shapes,...  45.8 us
    convert_element_type x1, other arithmetic, one_scan(): misfits.reshape(layers * E, cross_width, cross_width).astype(jnp.bfloat16)  43 us
    dot_general x3, matrix products, layer_terms(): jnp.einsum('enabc,ai,bj,ck->enijk', products, shapes, shapes, shapes, pre...  34.5 us
    another operation x6, local copies, waits for them, and re-layouts, body(): gradient_all = jnp.stack([grad_z, grad_y, grad_x])  24.8 us
    convert_element_type x2, local copies, waits for them, and re-layouts, layer_terms(): misfit = warped - ref_blocks.astype(jnp.float32)  15.1 us
    convert_element_type x2, local copies, waits for them, and re-layouts, one_scan(): misfits.reshape(layers * E, cross_width, cross_width).astype(jnp.bfloat16)  14.4 us
    mul x1, other arithmetic, layer_terms(): products = grad_blocks.astype(jnp.float32) * misfit[:, None]  13.3 us
  transfers between devices with their start and end apart: 7, of which 0 were waited for; matrix products, arithmetic and copies ran while one was open for 58% of the time, Pallas kernels for 0%

commit v1 on v0

v1 whole, which is shorter than its diff:
```python
import functools

import jax
import jax.numpy as jnp
import numpy as np
from jax import lax
from jax.experimental import pallas as pl
from jax.experimental.pallas import tpu as pltpu
from jax.sharding import PartitionSpec as P

E = 32
HALO = 16
RADIUS = 3
N = 128
ROW = N // E
WIN = 48
ROWS = HALO + N + E


def taps():
    t = np.arange(-RADIUS, RADIUS + 1).astype(np.float32)
    g = np.exp(-t * t / np.float32(2.0))
    smooth = g / np.sum(g)
    slope = t * g / np.sum(t * t * g)
    return [np.asarray(v, jnp.bfloat16).astype(np.float32) for v in (smooth, slope)]


def band(coeff):
    out = np.zeros((N, N), np.float32)
    for tap in range(2 * RADIUS + 1):
        out += coeff[tap] * np.eye(N, k=RADIUS - tap, dtype=np.float32)
    return out


SMOOTH, SLOPE = taps()
BAND_S, BAND_D = band(SMOOTH), band(SLOPE)
X_BANDS = np.concatenate([BAND_S, BAND_D], axis=1)
Y_BANDS = np.concatenate([BAND_S.T, BAND_D.T], axis=0)


def hat_rows():
    out = np.zeros((8, N), np.float32)
    for v in range(N):
        p = np.float32((v % E + 0.5) / E)
        out[v // E, v] = 1 - p
        out[v // E + 1, v] = p
    return out


HATS = hat_rows()


def lane_position(shape, dim):
    v = lax.broadcasted_iota(jnp.int32, shape, dim)
    return ((v % E).astype(jnp.float32) + 0.5) * (1.0 / E)


def warp_kernel(offs, nodes, own, low, high, hats, warped, vol, lhs, s_val, s_dif, w_base, w_step):
    zero_top = jnp.zeros((HALO, N), jnp.float32)
    zero_end = jnp.zeros((E, N), jnp.float32)

    def fill(src, first, count):
        def step(i, c):
            vol[first + i, 0:HALO] = zero_top
            vol[first + i, HALO : HALO + N] = src[i].astype(jnp.float32)
            vol[first + i, HALO + N : ROWS] = zero_end
            return c

        lax.fori_loop(0, count, step, 0, unroll=2)

    fill(low, 0, HALO)
    fill(own, HALO, E)
    fill(high, HALO + E, HALO)

    py = lane_position((E, N), 0)
    for c in range(3):
        line = []
        for iz in range(2):
            rows = []
            for iy in range(ROW + 1):
                acc = None
                for ix in range(ROW + 1):
                    term = nodes[c, iz * 25 + iy * (ROW + 1) + ix] * hats[ix : ix + 1, :]
                    acc = term if acc is None else acc + term
                rows.append(acc)
            line.append(rows)
        for ey in range(ROW):
            lo = line[0][ey] + py * (line[0][ey + 1] - line[0][ey])
            up = line[1][ey] + py * (line[1][ey + 1] - line[1][ey])
            w_base[c, ey * E : (ey + 1) * E] = lo
            w_step[c, ey * E : (ey + 1) * E] = up - lo

    src_lane = lax.broadcasted_iota(jnp.int32, (N, N), 0)
    out_lane = lax.broadcasted_iota(jnp.int32, (N, N), 1)
    shift = src_lane - out_lane
    block = out_lane // E

    def element_row(ey, carry):
        mats = []
        for ex in range(ROW):
            e = ey * ROW + ex
            oz, oy, ox = offs[0, e], offs[1, e], offs[2, e]
            mine = block == ex
            here = jnp.where(mine & (shift == ox), 1.0, 0.0)
            after = jnp.where(mine & (shift == ox + 1), 1.0, 0.0)
            mats.append(jnp.concatenate([here, after - here], axis=1).astype(jnp.bfloat16))
            first_z = oz + HALO
            first_y = ey * E + oy + HALO

            def copy_plane(z, c, ex=ex, first_z=first_z, first_y=first_y):
                lhs[z, :, ex * N : (ex + 1) * N] = vol[
                    first_z + z, pl.ds(first_y, WIN), :
                ].astype(jnp.bfloat16)
                return c

            lax.fori_loop(0, E + 1, copy_plane, 0, unroll=3)
        select = jnp.concatenate(mats, axis=0)

        def product(i, c):
            out = jnp.dot(
                lhs[pl.ds(i * 11, 11)].reshape(11 * WIN, ROW * N),
                select,
                preferred_element_type=jnp.float32,
            )
            s_val[pl.ds(i * 11, 11)] = out[:, :N].reshape(11, WIN, N)
            s_dif[pl.ds(i * 11, 11)] = out[:, N:].reshape(11, WIN, N)
            return c

        lax.fori_loop(0, 3, product, 0)

        def rows_of(r, c):
            base = pl.multiple_of(r * 8, 8)
            at = pl.multiple_of(ey * E + r * 8, 8)
            wz0, wy0, wx0 = [w_base[k, pl.ds(at, 8)] for k in range(3)]
            wz1, wy1, wx1 = [w_step[k, pl.ds(at, 8)] for k in range(3)]

            def corners(z):
                return (
                    s_val[z, pl.ds(base, 8)],
                    s_dif[z, pl.ds(base, 8)],
                    s_val[z, pl.ds(base + 1, 8)],
                    s_dif[z, pl.ds(base + 1, 8)],
                )

            below = corners(0)
            for z in range(E):
                above = corners(z + 1)
                p = (z + 0.5) / E
                wz = wz0 + p * wz1
                wy = wy0 + p * wy1
                wx = wx0 + p * wx1
                lines = []
                for v0, d0, v1, d1 in (below, above):
                    a0 = v0 + wx * d0
                    a1 = v1 + wx * d1
                    lines.append(a0 + wy * (a1 - a0))
                warped[z, pl.ds(at, 8)] = lines[0] + wz * (lines[1] - lines[0])
                below = above
            return c

        lax.fori_loop(0, E // 8, rows_of, 0)
        return carry

    lax.fori_loop(0, ROW, element_row, 0)


def warp(offs, nodes, own, low, high):
    vmem = pl.BlockSpec(memory_space=pltpu.VMEM)
    smem = pl.BlockSpec(memory_space=pltpu.SMEM)
    return pl.pallas_call(
        warp_kernel,
        out_shape=jax.ShapeDtypeStruct((E, N, N), jnp.float32),
        in_specs=[smem, smem, vmem, vmem, vmem, vmem],
        out_specs=vmem,
        scratch_shapes=[
            pltpu.VMEM((E + 2 * HALO, ROWS, N), jnp.float32),
            pltpu.VMEM((E + 1, WIN, ROW * N), jnp.bfloat16),
            pltpu.VMEM((E + 1, WIN, N), jnp.float32),
            pltpu.VMEM((E + 1, WIN, N), jnp.float32),
            pltpu.VMEM((3, N, N), jnp.float32),
            pltpu.VMEM((3, N, N), jnp.float32),
        ],
        compiler_params=pltpu.CompilerParams(vmem_limit_bytes=48 * 1024 * 1024),
        name="warp",
    )(offs, nodes, own, low, high, jnp.asarray(HATS))


def rhs_kernel(
    place, b0, b1, b2, b3, low, high, warped, x_bands, y_bands, hats,
    residual, bottom, top,
    y_z, y_y, y_x, misfit, sums,
):
    me = place[0]
    bands = x_bands[...]
    rows_s = y_bands[0:N]
    rows_d = y_bands[N : 2 * N]

    def filtered(src, count, at):
        flat = src[...].reshape(count * N, N)
        xf = jnp.dot(flat, bands, preferred_element_type=jnp.float32).astype(jnp.bfloat16)
        for i in range(count):
            plane = xf[i * N : (i + 1) * N]
            both = jnp.dot(rows_s, plane, preferred_element_type=jnp.float32)
            y_z[at + i] = both[:, :N]
            y_x[at + i] = both[:, N:]
            y_y[at + i] = jnp.dot(rows_d, plane[:, :N], preferred_element_type=jnp.float32)

    blocks = (b0, b1, b2, b3)
    depth = b0.shape[0]
    for j in range(4):
        first = (me ^ j) * depth
        filtered(blocks[j], depth, first + RADIUS)

        def differences(i, c, j=j, first=first):
            m = warped[first + i] - blocks[j][i].astype(jnp.float32)
            misfit[first + i] = m
            residual[first + i] = m.astype(jnp.bfloat16)
            return c

        lax.fori_loop(0, depth, differences, 0)
    filtered(low, RADIUS, 0)
    filtered(high, RADIUS, E + RADIUS)

    sums[...] = jnp.zeros_like(sums)
    smooth = [float(SMOOTH[RADIUS + t] / SMOOTH[RADIUS]) for t in range(RADIUS + 1)]
    slope = [float(SLOPE[RADIUS + t] / SLOPE[RADIUS + 1]) for t in range(RADIUS + 1)]

    def rows_of(r, carry):
        at = pl.multiple_of(r * 8, 8)
        ey = r // (E // 8)
        fields = (y_z, y_y, y_x)
        window = [[f[i, pl.ds(at, 8)] for i in range(2 * RADIUS)] for f in fields]
        zero = jnp.zeros((8, N), jnp.float32)
        plain = [zero] * 3
        running = [zero] * 3
        for z in range(E):
            for k in range(3):
                window[k] = window[k] + [fields[k][z + 2 * RADIUS, pl.ds(at, 8)]]
            m = misfit[z, pl.ds(at, 8)]
            w = window[0]
            grads = [
                (w[4] - w[2]) + slope[2] * (w[5] - w[1]) + slope[3] * (w[6] - w[0])
            ]
            for k in (1, 2):
                w = window[k]
                grads.append(
                    w[3]
                    + smooth[1] * (w[4] + w[2])
                    + smooth[2] * (w[5] + w[1])
                    + smooth[3] * (w[6] + w[0])
                )
            for k in range(3):
                plain[k] = plain[k] + grads[k] * m
                running[k] = running[k] + plain[k]
                window[k] = window[k][1:]
        row = lax.broadcasted_iota(jnp.int32, (8, N), 0) + (r % (E // 8)) * 8
        py = (row.astype(jnp.float32) + 0.5) * (1.0 / E)
        for k in range(3):
            gain = float(SLOPE[RADIUS + 1] if k == 0 else SMOOTH[RADIUS]) / E
            upper = (plain[k] * (1.0 + 0.5 / E) - running[k] * (1.0 / E)) * gain
            lower = plain[k] * gain - upper
            for iz, part in enumerate((lower, upper)):
                right = jnp.sum(part * py, axis=0, keepdims=True)
                left = jnp.sum(part, axis=0, keepdims=True) - right
                q = iz * 3 + k
                sums[q, pl.ds(ey, 1)] += left
                sums[q, pl.ds(ey + 1, 1)] += right
        return carry

    lax.fori_loop(0, N // 8, rows_of, 0)
    out = lax.dot_general(
        sums[...].reshape(48, N),
        hats[...],
        (((1,), (1,)), ((), ())),
        precision=lax.Precision.HIGHEST,
        preferred_element_type=jnp.float32,
    ).reshape(6, 8, 8)
    bottom[...] = out[:3]
    top[...] = out[3:]


def assemble(place, blocks, low, high, warped):
    vmem = pl.BlockSpec(memory_space=pltpu.VMEM)
    smem = pl.BlockSpec(memory_space=pltpu.SMEM)
    small = jax.ShapeDtypeStruct((3, 8, 8), jnp.float32)
    return pl.pallas_call(
        rhs_kernel,
        out_shape=(jax.ShapeDtypeStruct((E, N, N), jnp.bfloat16), small, small),
        in_specs=[smem] + [vmem] * 10,
        out_specs=(vmem, vmem, vmem),
        scratch_shapes=[pltpu.VMEM((E + 2 * RADIUS, N, N), jnp.float32)] * 3
        + [pltpu.VMEM((E, N, N), jnp.float32), pltpu.VMEM((6, 8, N), jnp.float32)],
        compiler_params=pltpu.CompilerParams(vmem_limit_bytes=48 * 1024 * 1024),
        name="rhs",
    )(
        place, *blocks, low, high, warped,
        jnp.asarray(X_BANDS, jnp.bfloat16), jnp.asarray(Y_BANDS, jnp.bfloat16), jnp.asarray(HATS),
    )


def chain(count, distance):
    return [(i, i + distance) for i in range(count) if 0 <= i + distance < count]


def body(tomogram, deformed, subvoxel, offsets):
    bricks = lax.axis_size("brick")
    me = lax.axis_index("scan")
    up, down = chain(bricks, 1), chain(bricks, -1)

    across = lax.ppermute(tomogram, "scan", [(0, 2), (1, 3), (2, 0), (3, 1)])
    beside = lax.ppermute(tomogram, "scan", [(0, 1), (1, 0), (2, 3), (3, 2)])
    slab = deformed[0]
    low = lax.ppermute(slab[E - HALO :], "brick", up)
    high = lax.ppermute(slab[:HALO], "brick", down)
    node_above = lax.ppermute(subvoxel, "brick", down)
    middle = lax.ppermute(tomogram, "scan", [(1, 2), (2, 1)])
    relayed = lax.ppermute(across, "scan", [(2, 3), (1, 0)])
    inner = (me == 1) | (me == 2)
    last = jnp.where(inner, middle, relayed)
    blocks = (tomogram, beside, across, last)

    nodes = jnp.concatenate([subvoxel[0, :, 0], node_above[0, :, 0]], axis=1)
    warped = warp(offsets[0], nodes, slab, low, high)

    def pick(index, part):
        out = part(blocks[0])
        for j in range(1, 4):
            out = jnp.where((me ^ j) == index, part(blocks[j]), out)
        return out

    low_ref = lax.ppermute(pick(3, lambda b: b[-RADIUS:]), "brick", up)
    high_ref = lax.ppermute(pick(0, lambda b: b[:RADIUS]), "brick", down)
    residual, bottom, top = assemble(me.reshape(1), blocks, low_ref, high_ref, warped)
    total = bottom + lax.ppermute(top, "brick", up)
    node_rhs = total[:, : ROW + 1, : ROW + 1].reshape(1, 3, 1, (ROW + 1) ** 2)
    return residual[None], node_rhs


def solution(mesh):
    return jax.shard_map(
        body,
        mesh=mesh,
        in_specs=(
            P(("brick", "scan"), None, None),
            P("scan", "brick", None, None),
            P("scan", None, "brick", None),
            P("scan", None, "brick"),
        ),
        out_specs=(P("scan", "brick", None, None), P("scan", None, "brick", None)),
        check_vma=False,
    )
```

time: 354 us -> 61.2 us (0.17)
  the two profiles are of different devices: /device:TPU:11 before, /device:TPU:12 now
where the time goes in v1:
time: 61.2 us; the launch traced here: 60.9 us
  starting transfers between devices  24.2 us (40%)
  waiting for transfers between devices  16.6 us (27%)
  Pallas kernels  16.1 us (26%)
  local copies, waits for them, and re-layouts  1.95 us (3%)
  other arithmetic  1.13 us (2%)
  between operations  0.9 us (1%)
    pallas_call x1, Pallas kernels, warp(): pl.pallas_call(warp_kernel, out_shape=jax.ShapeDtypeStruct((E, N, N), jnp...  8.77 us
    pallas_call x1, Pallas kernels, assemble(): pl.pallas_call(rhs_kernel, out_shape=(jax.ShapeDtypeStruct((E, N, N), jnp...  7.33 us
    ppermute x1, waiting for transfers between devices, body(): across = lax.ppermute(tomogram, 'scan', [(0, 2), (1, 3), (2, 0), (3, 1)])  7.02 us
    ppermute x1, waiting for transfers between devices, body(): low = lax.ppermute(slab[E - HALO:], 'brick', up)  5.56 us
    ppermute x1, starting transfers between devices, body(): relayed = lax.ppermute(across, 'scan', [(2, 3), (1, 0)])  4.87 us
    ppermute x1, starting transfers between devices, body(): high_ref = lax.ppermute(pick(0, lambda b: b[:RADIUS]), 'brick', down)  4.06 us
    ppermute x1, waiting for transfers between devices, body(): total = bottom + lax.ppermute(top, 'brick', up)  3.98 us
    ppermute x1, starting transfers between devices, body(): across = lax.ppermute(tomogram, 'scan', [(0, 2), (1, 3), (2, 0), (3, 1)])  2.65 us
  transfers between devices with their start and end apart: 10, of which 3 were waited for; matrix products, arithmetic and copies ran while one was open for 4% of the time, Pallas kernels for 14%

profile of v1, /device:TPU:12, one launch (start us, length us, event | category | flops | bytes accessed | tf_op | source)
XLA Modules:
  0.0 60.9 jit_solution(14082015807898364121)
XLA Ops:
  0.6 0.0 copy-start.4
  0.7 2.7 %collective-permute-start.1 = (bf16[8,128,128]{2,1,0:T(8,128)(2,1)}, bf16[8,128,128]{2,1,0:T(8,128)(2,1)S(1)}, u32[]{:S(2)}, u32[]{:S(2)}) collective-permute-start(bf16[8,128,128]{2,1,0:T(8,128)(2,1)} %b0.1), channel_id=1, source_target_pairs={{0,2},{1,3},{2,0},{3,1},{4,6},{5,7},{6,4},{7,5},{8,10},{9,11},{10,... | collective-permute-start | bytes 786440 | tf_op jit(solution)/shard_map/ppermute | solution.py:310
  3.3 1.9 %collective-permute-start.2 = (bf16[8,128,128]{2,1,0:T(8,128)(2,1)}, bf16[8,128,128]{2,1,0:T(8,128)(2,1)}, u32[]{:S(2)}, u32[]{:S(2)}) collective-permute-start(bf16[8,128,128]{2,1,0:T(8,128)(2,1)} %b0.1), channel_id=1, source_target_pairs={{1,2},{2,1},{5,6},{6,5},{9,10},{10,9},{13,14},{14,13},{17,18},{18,... | collective-permute-start | bytes 786440 | tf_op jit(solution)/shard_map/ppermute | solution.py:316
  5.3 0.1 collective-permute-start
  5.3 2.5 %collective-permute-start.6 = (f32[1,3,1,25]{3,2,1,0:T(1,128)}, f32[1,3,1,25]{3,2,1,0:T(1,128)S(1)}, u32[]{:S(2)}, u32[]{:S(2)}) collective-permute-start(f32[1,3,1,25]{3,2,1,0:T(1,128)} %param.9), channel_id=1, source_target_pairs={{4,0},{8,4},{12,8},{16,12},{20,16},{24,20},{28,24},{5,1},{9,5},{13... | collective-permute-start | bytes 908 | tf_op jit(solution)/shard_map/ppermute | solution.py:315
  7.8 7.0 %collective-permute-done.1.b2 = bf16[8,128,128]{2,1,0:T(8,128)(2,1)S(1)} collective-permute-done((bf16[8,128,128]{2,1,0:T(8,128)(2,1)}, bf16[8,128,128]{2,1,0:T(8,128)(2,1)S(1)}, u32[]{:S(2)}, u32[]{:S(2)}) %collective-permute-start.1) | collective-permute-done | bytes 262176 | tf_op jit(solution)/shard_map/ppermute | solution.py:310
  14.9 4.9 %collective-permute-start.3 = (bf16[8,128,128]{2,1,0:T(8,128)(2,1)S(1)}, bf16[8,128,128]{2,1,0:T(8,128)(2,1)}, u32[]{:S(2)}, u32[]{:S(2)}) collective-permute-start(bf16[8,128,128]{2,1,0:T(8,128)(2,1)S(1)} %collective-permute-done.1.b2), channel_id=1, source_target_pairs={{2,3},{1,0},{6,7},{5,4},{10,11},{9,8},{14,15},{13,12},{18,19},{17,... | collective-permute-start | bytes 786440 | tf_op jit(solution)/shard_map/ppermute | solution.py:317
  19.7 1.3 %slice_bitcast_fusion = (bf16[16,128,128]{2,1,0:T(8,128)(2,1)S(1)}, bf16[16,128,128]{2,1,0:T(8,128)(2,1)S(1)}) fusion(bf16[1,32,128,128]{3,2,1,0:T(8,128)(2,1)} %param.8), kind=kLoop, calls=%fused_computation | loop fusion | bytes 2097152 | tf_op jit(solution)/shard_map/slice | solution.py:314
  21.0 1.9 %collective-permute-start.8 = (bf16[16,128,128]{2,1,0:T(8,128)(2,1)S(1)}, bf16[16,128,128]{2,1,0:T(8,128)(2,1)S(1)}, u32[]{:S(2)}, u32[]{:S(2)}) collective-permute-start(bf16[16,128,128]{2,1,0:T(8,128)(2,1)S(1)} %get-tuple-element.12), channel_id=1, source_target_pairs={{4,0},{8,4},{12,8},{16,12},{20,16},{24,20},{28,24},{5,1},{9,5},{13... | collective-permute-start | bytes 1572872 | tf_op jit(solution)/shard_map/ppermute | solution.py:314
  23.0 2.4 %collective-permute-start.7 = (bf16[16,128,128]{2,1,0:T(8,128)(2,1)S(1)}, bf16[16,128,128]{2,1,0:T(8,128)(2,1)S(1)}, u32[]{:S(2)}, u32[]{:S(2)}) collective-permute-start(bf16[16,128,128]{2,1,0:T(8,128)(2,1)S(1)} %get-tuple-element.13), channel_id=1, source_target_pairs={{0,4},{4,8},{8,12},{12,16},{16,20},{20,24},{24,28},{1,5},{5,9},{9,... | collective-permute-start | bytes 1572872 | tf_op jit(solution)/shard_map/ppermute | solution.py:313
  25.4 0.0 collective-permute-done.2
  25.5 0.0 collective-permute-done.3
  25.5 1.0 %broadcast_select_fusion.b3 = bf16[8,128,128]{2,1,0:T(8,128)(2,1)S(1)} fusion(bf16[8,128,128]{2,1,0:T(8,128)(2,1)} %collective-permute-done.2, bf16[8,128,128]{2,1,0:T(8,128)(2,1)} %collective-permute-done.3, pred[]{:T(512)S(6)} %or.3), kind=kLoop, calls=%fused_computation.2 | loop fusion | flops 131072 | bytes 786433 | tf_op jit(solution)/shard_map/jit(_where)/select_n | solution.py:319
  26.5 0.1 fusion.1
  26.5 4.1 %collective-permute-start.5 = (bf16[3,128,128]{2,1,0:T(8,128)(2,1)S(1)}, bf16[3,128,128]{2,1,0:T(8,128)(2,1)S(1)}, u32[]{:S(2)}, u32[]{:S(2)}) collective-permute-start(bf16[3,128,128]{2,1,0:T(8,128)(2,1)S(1)} %get-tuple-element.14), channel_id=1, source_target_pairs={{4,0},{8,4},{12,8},{16,12},{20,16},{24,20},{28,24},{5,1},{9,5},{13... | collective-permute-start | bytes 294920 | tf_op jit(solution)/shard_map/ppermute | solution.py:332
  30.6 1.9 %collective-permute-start.4 = (bf16[3,128,128]{2,1,0:T(8,128)(2,1)S(1)}, bf16[3,128,128]{2,1,0:T(8,128)(2,1)S(1)}, u32[]{:S(2)}, u32[]{:S(2)}) collective-permute-start(bf16[3,128,128]{2,1,0:T(8,128)(2,1)S(1)} %get-tuple-element.15), channel_id=1, source_target_pairs={{0,4},{4,8},{8,12},{12,16},{16,20},{20,24},{24,28},{1,5},{5,9},{9,... | collective-permute-start | bytes 294920 | tf_op jit(solution)/shard_map/ppermute | solution.py:331
  32.5 0.1 pad_maximum_fusion.nodes
  32.6 0.0 collective-permute-done.8.high
  32.6 5.6 %collective-permute-done.7.low = bf16[16,128,128]{2,1,0:T(8,128)(2,1)S(1)} collective-permute-done((bf16[16,128,128]{2,1,0:T(8,128)(2,1)S(1)}, bf16[16,128,128]{2,1,0:T(8,128)(2,1)S(1)}, u32[]{:S(2)}, u32[]{:S(2)}) %collective-permute-start.7) | collective-permute-done | bytes 524320 | tf_op jit(solution)/shard_map/ppermute | solution.py:313
  38.2 8.8 %warp.1.warped = f32[32,128,128]{2,1,0:T(8,128)S(1)} custom-call(s32[3,16]{1,0:T(4,128)S(1)} %bitcast.17, f32[3,50]{1,0:T(4,128)S(1)} %pad_maximum_fusion.nodes, bf16[32,128,128]{2,1,0:T(8,128)(2,1)S(1)} %bitcast.16, bf16[16,128,128]{2,1,0:T(8,128)(2,1)S(1)} %collective-permute-done.7.low, bf16[16,128,128]{2,1,0:T(8,128)(2,1)S(1)} %collective-permute-done.8.high, ...), custom_call_target="tpu_custom_call" | custom-call | tf_op jit(solution)/shard_map/warp/pallas_call | solution.py:170
  47.0 7.3 %rhs.1 = (bf16[32,128,128]{2,1,0:T(8,128)(2,1)}, f32[3,8,8]{2,1,0:T(8,128)S(1)}, f32[3,8,8]{2,1,0:T(8,128)S(1)}) custom-call(s32[1]{0:T(128)} %bitcast.place, bf16[8,128,128]{2,1,0:T(8,128)(2,1)S(1)} %copy-done.1, bf16[8,128,128]{2,1,0:T(8,128)(2,1)S(1)} %collective-permute-done.b1, bf16[8,128,128]{2,1,0:T(8,128)(2,1)S(1)} %collective-permute-done.1.b2, ...), custom_call_target="tpu_custom_call" | custom-call | tf_op jit(solution)/shard_map/rhs/pallas_call | solution.py:286
  54.3 1.9 %collective-permute-start.9 = (f32[3,8,8]{2,1,0:T(8,128)S(1)}, f32[3,8,8]{2,1,0:T(8,128)S(1)}, u32[]{:S(2)}, u32[]{:S(2)}) collective-permute-start(f32[3,8,8]{2,1,0:T(8,128)S(1)} %get-tuple-element.7), channel_id=1, source_target_pairs={{0,4},{4,8},{8,12},{12,16},{16,20},{20,24},{24,28},{1,5},{5,9},{9,... | collective-permute-start | bytes 2312 | tf_op jit(solution)/shard_map/ppermute | solution.py:334
  56.3 4.0 %collective-permute-done.9 = f32[3,8,8]{2,1,0:T(8,128)S(1)} collective-permute-done((f32[3,8,8]{2,1,0:T(8,128)S(1)}, f32[3,8,8]{2,1,0:T(8,128)S(1)}, u32[]{:S(2)}, u32[]{:S(2)}) %collective-permute-start.9) | collective-permute-done | bytes 800 | tf_op jit(solution)/shard_map/ppermute | solution.py:334
  60.2 0.6 %reshape.14 = f32[1,3,1,25]{3,2,1,0:T(1,128)} reshape(f32[3,5,5]{2,1,0:T(8,128)S(1)} %slice_add_fusion) | data formatting | bytes 600 | tf_op jit(solution)/shard_map/reshape | solution.py:335
  (21 shorter events, 0.0 us)
Async XLA Ops:
  0.6 37.5 %copy-start.4 = (f32[8,128]{1,0:T(8,128)S(1)}, f32[8,128]{1,0:T(8,128)}, u32[]{:S(2)}) copy-start(f32[8,128]{1,0:T(8,128)} %constant.18.clone.hats) | copy-start | bytes 12292
  0.6 25.8 %copy-start.1 = (bf16[8,128,128]{2,1,0:T(8,128)(2,1)S(1)}, bf16[8,128,128]{2,1,0:T(8,128)(2,1)}, u32[]{:S(2)}) copy-start(bf16[8,128,128]{2,1,0:T(8,128)(2,1)} %b0.1) | copy-start | bytes 786436
  0.7 22.3 %copy-start.6 = (f32[1,3,1,25]{3,2,1,0:T(1,128)S(1)}, f32[1,3,1,25]{3,2,1,0:T(1,128)}, u32[]{:S(2)}) copy-start(f32[1,3,1,25]{3,2,1,0:T(1,128)} %param.9) | copy-start | bytes 904
  0.7 37.5 %copy-start = (bf16[1,32,128,128]{3,2,1,0:T(8,128)(2,1)S(1)}, bf16[1,32,128,128]{3,2,1,0:T(8,128)(2,1)}, u32[]{:S(2)}) copy-start(bf16[1,32,128,128]{3,2,1,0:T(8,128)(2,1)} %param.8) | copy-start | bytes 3145732
  0.7 22.3 %copy-start.5 = (s32[1,3,16]{2,0,1:T(1,128)S(1)}, s32[1,3,16]{2,0,1:T(1,128)}, u32[]{:S(2)}) copy-start(s32[1,3,16]{2,0,1:T(1,128)} %param.10) | copy-start | bytes 580
  0.7 14.2 %collective-permute-start.1 = (bf16[8,128,128]{2,1,0:T(8,128)(2,1)}, bf16[8,128,128]{2,1,0:T(8,128)(2,1)S(1)}, u32[]{:S(2)}, u32[]{:S(2)}) collective-permute-start(bf16[8,128,128]{2,1,0:T(8,128)(2,1)} %b0.1), channel_id=1, source_target_pairs={{0,2},{1,3},{2,0},{3,1},{4,6},{5,7},{6,4},{7,5},{8,10},{9,11},{10,... | collective-permute-start | bytes 786440 | tf_op jit(solution)/shard_map/ppermute | solution.py:310
  3.3 22.1 %collective-permute-start.2 = (bf16[8,128,128]{2,1,0:T(8,128)(2,1)}, bf16[8,128,128]{2,1,0:T(8,128)(2,1)}, u32[]{:S(2)}, u32[]{:S(2)}) collective-permute-start(bf16[8,128,128]{2,1,0:T(8,128)(2,1)} %b0.1), channel_id=1, source_target_pairs={{1,2},{2,1},{5,6},{6,5},{9,10},{10,9},{13,14},{14,13},{17,18},{18,... | collective-permute-start | bytes 786440 | tf_op jit(solution)/shard_map/ppermute | solution.py:316
  5.3 21.2 %collective-permute-start = (bf16[8,128,128]{2,1,0:T(8,128)(2,1)}, bf16[8,128,128]{2,1,0:T(8,128)(2,1)S(1)}, u32[]{:S(2)}, u32[]{:S(2)}) collective-permute-start(bf16[8,128,128]{2,1,0:T(8,128)(2,1)} %b0.1), channel_id=1, source_target_pairs={{0,1},{1,0},{2,3},{3,2},{4,5},{5,4},{6,7},{7,6},{8,9},{9,8},{10,11... | collective-permute-start | bytes 786440 | tf_op jit(solution)/shard_map/ppermute | solution.py:311
  5.3 17.7 %collective-permute-start.6 = (f32[1,3,1,25]{3,2,1,0:T(1,128)}, f32[1,3,1,25]{3,2,1,0:T(1,128)S(1)}, u32[]{:S(2)}, u32[]{:S(2)}) collective-permute-start(f32[1,3,1,25]{3,2,1,0:T(1,128)} %param.9), channel_id=1, source_target_pairs={{4,0},{8,4},{12,8},{16,12},{20,16},{24,20},{28,24},{5,1},{9,5},{13... | collective-permute-start | bytes 908 | tf_op jit(solution)/shard_map/ppermute | solution.py:315
  14.9 10.6 %collective-permute-start.3 = (bf16[8,128,128]{2,1,0:T(8,128)(2,1)S(1)}, bf16[8,128,128]{2,1,0:T(8,128)(2,1)}, u32[]{:S(2)}, u32[]{:S(2)}) collective-permute-start(bf16[8,128,128]{2,1,0:T(8,128)(2,1)S(1)} %collective-permute-done.1.b2), channel_id=1, source_target_pairs={{2,3},{1,0},{6,7},{5,4},{10,11},{9,8},{14,15},{13,12},{18,19},{17,... | collective-permute-start | bytes 786440 | tf_op jit(solution)/shard_map/ppermute | solution.py:317
  21.0 11.6 %collective-permute-start.8 = (bf16[16,128,128]{2,1,0:T(8,128)(2,1)S(1)}, bf16[16,128,128]{2,1,0:T(8,128)(2,1)S(1)}, u32[]{:S(2)}, u32[]{:S(2)}) collective-permute-start(bf16[16,128,128]{2,1,0:T(8,128)(2,1)S(1)} %get-tuple-element.12), channel_id=1, source_target_pairs={{4,0},{8,4},{12,8},{16,12},{20,16},{24,20},{28,24},{5,1},{9,5},{13... | collective-permute-start | bytes 1572872 | tf_op jit(solution)/shard_map/ppermute | solution.py:314
  23.0 15.2 %collective-permute-start.7 = (bf16[16,128,128]{2,1,0:T(8,128)(2,1)S(1)}, bf16[16,128,128]{2,1,0:T(8,128)(2,1)S(1)}, u32[]{:S(2)}, u32[]{:S(2)}) collective-permute-start(bf16[16,128,128]{2,1,0:T(8,128)(2,1)S(1)} %get-tuple-element.13), channel_id=1, source_target_pairs={{0,4},{4,8},{8,12},{12,16},{16,20},{20,24},{24,28},{1,5},{5,9},{9,... | collective-permute-start | bytes 1572872 | tf_op jit(solution)/shard_map/ppermute | solution.py:313
  26.5 20.4 %collective-permute-start.5 = (bf16[3,128,128]{2,1,0:T(8,128)(2,1)S(1)}, bf16[3,128,128]{2,1,0:T(8,128)(2,1)S(1)}, u32[]{:S(2)}, u32[]{:S(2)}) collective-permute-start(bf16[3,128,128]{2,1,0:T(8,128)(2,1)S(1)} %get-tuple-element.14), channel_id=1, source_target_pairs={{4,0},{8,4},{12,8},{16,12},{20,16},{24,20},{28,24},{5,1},{9,5},{13... | collective-permute-start | bytes 294920 | tf_op jit(solution)/shard_map/ppermute | solution.py:332
  30.6 16.4 %collective-permute-start.4 = (bf16[3,128,128]{2,1,0:T(8,128)(2,1)S(1)}, bf16[3,128,128]{2,1,0:T(8,128)(2,1)S(1)}, u32[]{:S(2)}, u32[]{:S(2)}) collective-permute-start(bf16[3,128,128]{2,1,0:T(8,128)(2,1)S(1)} %get-tuple-element.15), channel_id=1, source_target_pairs={{0,4},{4,8},{8,12},{12,16},{16,20},{20,24},{24,28},{1,5},{5,9},{9,... | collective-permute-start | bytes 294920 | tf_op jit(solution)/shard_map/ppermute | solution.py:331
  38.2 8.8 %copy-start.2 = (bf16[256,128]{1,0:T(8,128)(2,1)S(1)}, bf16[256,128]{1,0:T(8,128)(2,1)}, u32[]{:S(2)}) copy-start(bf16[256,128]{1,0:T(8,128)(2,1)} %constant.20.clone.y_bands) | copy-start | bytes 196612
  38.2 8.8 %copy-start.3 = (bf16[128,256]{1,0:T(8,128)(2,1)S(1)}, bf16[128,256]{1,0:T(8,128)(2,1)}, u32[]{:S(2)}) copy-start(bf16[128,256]{1,0:T(8,128)(2,1)} %constant.19.clone.x_bands) | copy-start | bytes 196612
  54.3 5.9 %collective-permute-start.9 = (f32[3,8,8]{2,1,0:T(8,128)S(1)}, f32[3,8,8]{2,1,0:T(8,128)S(1)}, u32[]{:S(2)}, u32[]{:S(2)}) collective-permute-start(f32[3,8,8]{2,1,0:T(8,128)S(1)} %get-tuple-element.7), channel_id=1, source_target_pairs={{0,4},{4,8},{8,12},{12,16},{16,20},{20,24},{24,28},{1,5},{5,9},{9,... | collective-permute-start | bytes 2312 | tf_op jit(solution)/shard_map/ppermute | solution.py:334

commit v2 on v1

v2 whole, which is shorter than its diff:
```python
import functools

import jax
import jax.numpy as jnp
import numpy as np
from jax import lax
from jax.experimental import pallas as pl
from jax.experimental.pallas import tpu as pltpu
from jax.sharding import PartitionSpec as P

E = 32
HALO = 16
RADIUS = 3
N = 128
ROW = N // E
WIN = 48
HALF = E // 2
HALF_HALO = HALO // 2
ROWS = HALO + N + E


def taps():
    t = np.arange(-RADIUS, RADIUS + 1).astype(np.float32)
    g = np.exp(-t * t / np.float32(2.0))
    smooth = g / np.sum(g)
    slope = t * g / np.sum(t * t * g)
    return [np.asarray(v, jnp.bfloat16).astype(np.float32) for v in (smooth, slope)]


def band(coeff):
    out = np.zeros((N, N), np.float32)
    for tap in range(2 * RADIUS + 1):
        out += coeff[tap] * np.eye(N, k=RADIUS - tap, dtype=np.float32)
    return out


SMOOTH, SLOPE = taps()
BAND_S, BAND_D = band(SMOOTH), band(SLOPE)
X_BANDS = np.concatenate([BAND_S, BAND_D], axis=1)
Y_BANDS = np.concatenate([BAND_S.T, BAND_D.T], axis=0)


def rhs_hats():
    at = (np.arange(N, dtype=np.float32) + 0.5) / E
    hats = np.maximum(0.0, 1.0 - np.abs(at[:, None] - np.arange(ROW + 1, dtype=np.float32)))
    out = np.zeros((ROW + 1, N, N), np.float32)
    for iy in range(ROW + 1):
        out[iy, :, iy * (ROW + 1) : (iy + 1) * (ROW + 1)] = hats
    return out


RHS_HATS = rhs_hats()


def lane_position(shape, dim):
    v = lax.broadcasted_iota(jnp.int32, shape, dim)
    return ((v % E).astype(jnp.float32) + 0.5) * (1.0 / E)


def split_kernel(place, nodes_in, slab, near, far, far_end, nodes, wide, sems):
    odd = place[1]
    parts = ((1 - odd, 0, HALO, near), (odd, 0, HALF_HALO, far), (odd, HALF_HALO, HALF_HALO, far_end))
    copies = [
        pltpu.make_async_copy(
            slab.at[0, pl.ds(HALO * first + skip, count)], out.at[pl.ds(0, count)], sems.at[i]
        )
        for i, (first, skip, count, out) in enumerate(parts)
    ]
    fetch = pltpu.make_async_copy(nodes_in, nodes, sems.at[3])
    fetch.start()
    for c in copies:
        c.start()
    fetch.wait()
    wide[...] = jnp.zeros_like(wide)
    for c in range(3):
        wide[c : c + 1, 0 : (ROW + 1) ** 2] = nodes[0, c]
    rest = wide[...]
    rows = []
    for _ in range(3):
        rows.append(rest.astype(jnp.bfloat16).astype(jnp.float32))
        rest = rest - rows[-1]
    rows = jnp.concatenate(rows + [rest], axis=0).astype(jnp.bfloat16)
    for out, last in ((near, HALO), (far_end, HALF_HALO)):
        out[last, 0 : 4 * 8] = rows
        out[last, 4 * 8 : N] = jnp.zeros((N - 4 * 8, N), jnp.bfloat16)
    for c in copies:
        c.wait()


def shifted(below, offs, middle, other, halo, vol, lhs, store):
    zero_top = jnp.zeros((HALO, N), jnp.float32)
    zero_end = jnp.zeros((E, N), jnp.float32)

    def fill(srcs, first):
        count = HALO // len(srcs)
        for part, src in enumerate(srcs):

            def step(i, c, src=src, at=first + part * count):
                vol[at + i, 0:HALO] = zero_top
                vol[at + i, HALO : HALO + N] = src[i].astype(jnp.float32)
                vol[at + i, HALO + N : ROWS] = zero_end
                return c

            lax.fori_loop(0, count, step, 0, unroll=4)

    fill(halo, jnp.where(below, 0, E))
    fill(middle, HALO)
    fill(other, jnp.where(below, E, 0))

    lane = lax.broadcasted_iota(jnp.int32, (WIN, N), 1)
    src_lane = lax.broadcasted_iota(jnp.int32, (N, N), 0)
    out_lane = lax.broadcasted_iota(jnp.int32, (N, N), 1)
    distance = src_lane - out_lane
    block = out_lane // E

    def element_row(ey, carry):
        first_z, first_y, shift = [], [], []
        for ex in range(ROW):
            e = ey * ROW + ex
            first_z.append(offs[0, 0, e] + HALO)
            first_y.append(ey * E + offs[1, 0, e] + HALO)
            shift.append(offs[2, 0, e])
        mats = []
        for ex in range(2):
            moved = jnp.where(block == ex, distance - shift[ex], N)
            moved = jnp.where(block == ex + 2, distance - shift[ex + 2], moved)
            here = jnp.where(moved == 0, 1.0, 0.0)
            mats.append(jnp.concatenate([here, jnp.where(moved == 1, 1.0, 0.0) - here], axis=1))
        select = jnp.concatenate(mats, axis=0).astype(jnp.bfloat16)

        for z in range(HALF + 1):
            part = [vol[first_z[ex] + z, pl.ds(first_y[ex], WIN), :] for ex in range(ROW)]
            lhs[z, :, :N] = jnp.where(lane < E + HALO, part[0], part[2]).astype(jnp.bfloat16)
            lhs[z, :, N:] = jnp.where(lane < 2 * E + HALO, part[1], part[3]).astype(jnp.bfloat16)

        out = jnp.dot(
            lhs[...].reshape((HALF + 1) * WIN, 2 * N), select, preferred_element_type=jnp.float32
        )
        store(ey, out.reshape(HALF + 1, WIN, 2 * N))
        return carry

    lax.fori_loop(0, ROW, element_row, 0)


def window_kernel(
    place, offs, near, far, far_end, halo, val_out, dif_out, vol, lhs, s_val, s_dif, sems
):
    def copies(ey):
        return [
            pltpu.make_async_copy(src.at[ey], out.at[ey], sems.at[i, ey])
            for i, (src, out) in enumerate(((s_val, val_out), (s_dif, dif_out)))
        ]

    def store(ey, out):
        s_val[ey] = out[:, : E + 8, :N]
        s_dif[ey] = out[:, : E + 8, N:]
        for c in copies(ey):
            c.start()

    shifted(place[1] == 1, offs, (near,), (far, far_end), (halo,), vol, lhs, store)
    for ey in range(ROW):
        for c in copies(ey):
            c.wait()


def node_rows(plane, hats):
    row = lax.broadcasted_iota(jnp.int32, (16, N), 0)
    mine = lax.broadcasted_iota(jnp.int32, (16, N), 1) // (ROW + 1) == row % (ROW + 1)
    component = row // (ROW + 1)
    out = jnp.zeros((16, N), jnp.float32)
    values = plane[0 : 4 * 8].astype(jnp.float32)
    for piece in range(3):
        v = values[piece * 8 : piece * 8 + 8]
        line = jnp.where(component == 0, v[0:1], jnp.where(component == 1, v[1:2], v[2:3]))
        line = jnp.where(mine, line, 0.0).astype(jnp.bfloat16)
        out = out + jnp.dot(line, hats, preferred_element_type=jnp.float32)
    return out


def warp_kernel(
    place, offs, near, far, far_end, near_halo, far_halo, far_halo_end, val_in, dif_in,
    warped, vol, lhs, s_val, s_dif, w_base, w_step, val_a, dif_a, sems,
):
    odd = place[1] == 1
    earlier = [
        pltpu.make_async_copy(src, out, sems.at[i])
        for i, (src, out) in enumerate(((val_in, val_a), (dif_in, dif_a)))
    ]
    for c in earlier:
        c.start()

    def store(ey, out):
        s_val[ey] = out[:, : E + 8, :N]
        s_dif[ey] = out[:, : E + 8, N:]

    halo = (far_halo, far_halo_end)
    shifted(jnp.logical_not(odd), offs, (far, far_end), (near,), halo, vol, lhs, store)

    node = lax.broadcasted_iota(jnp.int32, (N, N), 0)
    at = (lax.broadcasted_iota(jnp.int32, (N, N), 1).astype(jnp.float32) + 0.5) * (1.0 / E)
    hat = jnp.maximum(0.0, 1.0 - jnp.abs(at - (node % (ROW + 1)).astype(jnp.float32)))
    hats = jnp.where(node < (ROW + 1) ** 2, hat, 0.0).astype(jnp.bfloat16)
    lower = node_rows(near[HALO], hats)
    upper = jnp.where(
        odd, node_rows(far_halo_end[HALF_HALO], hats), node_rows(near_halo[HALO], hats)
    )
    py = lane_position((E, N), 0)
    for c in range(3):
        for ey in range(ROW):
            q = c * (ROW + 1) + ey
            lo = lower[q : q + 1] + py * (lower[q + 1 : q + 2] - lower[q : q + 1])
            up = upper[q : q + 1] + py * (upper[q + 1 : q + 2] - upper[q : q + 1])
            w_step[c, ey * E : (ey + 1) * E] = up - lo
            w_base[c, ey * E : (ey + 1) * E] = lo

    def interpolate(val, dif, first_plane):
        start = first_plane.astype(jnp.float32) * (1.0 / E)

        def rows_of(r, carry):
            ey = r // (E // 8)
            base = (r % (E // 8)) * 8
            at = pl.multiple_of(r * 8, 8)
            wz1, wy1, wx1 = [w_step[k, pl.ds(at, 8)] for k in range(3)]
            wz0, wy0, wx0 = [
                w_base[k, pl.ds(at, 8)] + start * w for k, w in enumerate((wz1, wy1, wx1))
            ]

            def corners(z):
                return (
                    val[ey, z, pl.ds(base, 8)],
                    dif[ey, z, pl.ds(base, 8)],
                    val[ey, z, pl.ds(base + 1, 8)],
                    dif[ey, z, pl.ds(base + 1, 8)],
                )

            lower = corners(0)
            for z in range(HALF):
                upper = corners(z + 1)
                p = (z + 0.5) / E
                wz = wz0 + p * wz1
                wy = wy0 + p * wy1
                wx = wx0 + p * wx1
                lines = []
                for v0, d0, v1, d1 in (lower, upper):
                    a0 = v0 + wx * d0
                    a1 = v1 + wx * d1
                    lines.append(a0 + wy * (a1 - a0))
                warped[first_plane + z, pl.ds(at, 8)] = lines[0] + wz * (lines[1] - lines[0])
                lower = upper
            return carry

        lax.fori_loop(0, N // 8, rows_of, 0)

    interpolate(s_val, s_dif, jnp.where(odd, HALF, 0))
    for c in earlier:
        c.wait()
    interpolate(val_a, dif_a, jnp.where(odd, 0, HALF))


VMEM = pl.BlockSpec(memory_space=pltpu.VMEM)
SMEM = pl.BlockSpec(memory_space=pltpu.SMEM)
HBM = pl.BlockSpec(memory_space=pltpu.HBM)
VOLUME = jax.ShapeDtypeStruct((E, N, N), jnp.float32)
SAMPLES = (ROW, HALF + 1, E + 8, N)
RESIDUAL = jax.ShapeDtypeStruct((E, N, N), jnp.bfloat16)
FILTERED = jax.ShapeDtypeStruct((3, E, N, N), jnp.float32)
SMALL = jax.ShapeDtypeStruct((3, 1, (ROW + 1) ** 2), jnp.float32)


def call(kernel, name, outs, smem, vmem, scratch, mib, hbm=(), out_spec=VMEM):
    specs = [SMEM] * len(smem) + [VMEM] * len(vmem)
    return pl.pallas_call(
        kernel,
        out_shape=outs,
        in_specs=specs + [HBM] * len(hbm),
        out_specs=jax.tree.map(lambda _: out_spec, outs),
        scratch_shapes=scratch,
        compiler_params=pltpu.CompilerParams(vmem_limit_bytes=mib * 1024 * 1024),
        name=name,
    )(*smem, *vmem, *hbm)


def split(place, nodes, slab):
    return call(
        split_kernel,
        "split",
        tuple(jax.ShapeDtypeStruct((n, N, N), jnp.bfloat16) for n in (HALO + 1, HALF_HALO, HALF_HALO + 1)),
        [place],
        [],
        [
            pltpu.VMEM((1, 3, 1, (ROW + 1) ** 2), jnp.float32),
            pltpu.VMEM((8, N), jnp.float32),
            pltpu.SemaphoreType.DMA((4,)),
        ],
        4,
        hbm=[nodes, slab],
    )


WINDOW_SCRATCH = [
    pltpu.VMEM((E + HALO, ROWS, N), jnp.float32),
    pltpu.VMEM((HALF + 1, WIN, 2 * N), jnp.bfloat16),
    pltpu.VMEM(SAMPLES, jnp.float32),
    pltpu.VMEM(SAMPLES, jnp.float32),
]


def windows(place, offs, *planes):
    samples = pltpu.HBM(SAMPLES, jnp.float32)
    return call(
        window_kernel,
        "windows",
        (samples, samples),
        [place, offs],
        planes,
        WINDOW_SCRATCH + [pltpu.SemaphoreType.DMA((2, ROW))],
        12,
        out_spec=HBM,
    )


def warp(place, offs, planes, samples):
    return call(
        warp_kernel,
        "warp",
        VOLUME,
        [place, offs],
        planes,
        WINDOW_SCRATCH
        + [pltpu.VMEM((3, N, N), jnp.float32)] * 2
        + [pltpu.VMEM(SAMPLES, jnp.float32)] * 2
        + [pltpu.SemaphoreType.DMA((2,))],
        16,
        hbm=samples,
    )


def filter_into(y, planes, at, x_bands, y_bands):
    smoothed, slopes = [], []
    for i in range(0, len(planes), 2):
        pair = planes[i : i + 2]
        both = jnp.concatenate(pair, axis=1) if len(pair) == 2 else pair[0]
        along_y = jnp.dot(y_bands[...], both, preferred_element_type=jnp.float32)
        along_y = along_y.astype(jnp.bfloat16)
        for k in range(len(pair)):
            smoothed.append(along_y[:N, k * N : (k + 1) * N])
            slopes.append(along_y[N:, k * N : (k + 1) * N])
    rows = pl.ds(at, len(planes))
    out = jnp.dot(jnp.concatenate(smoothed), x_bands[...], preferred_element_type=jnp.float32)
    y[0, rows] = out[:, :N].reshape(-1, N, N)
    y[2, rows] = out[:, N:].reshape(-1, N, N)
    out = jnp.dot(jnp.concatenate(slopes), x_bands[:, :N], preferred_element_type=jnp.float32)
    y[1, rows] = out.reshape(-1, N, N)


def filter_kernel(
    place, warped, x_bands, y_bands, b0, b1, b2, b3, misfit, residual, y, held, sems
):
    me = place[0]
    depth = b0.shape[0]
    copies = [
        pltpu.make_async_copy(b, held.at[j], sems.at[j]) for j, b in enumerate((b0, b1, b2, b3))
    ]
    for c in copies:
        c.start()
    for j in range(4):
        copies[j].wait()
        filter_into(y, [held[j, i] for i in range(depth)], j * depth, x_bands, y_bands)
        first = (me ^ j) * depth
        for i in range(depth):
            m = warped[first + i] - held[j, i].astype(jnp.float32)
            misfit[first + i] = m
            residual[first + i] = m.astype(jnp.bfloat16)


def filtered(place, blocks, warped):
    return call(
        filter_kernel,
        "filters",
        (VOLUME, RESIDUAL, FILTERED),
        [place],
        [warped, jnp.asarray(X_BANDS, jnp.bfloat16), jnp.asarray(Y_BANDS, jnp.bfloat16)],
        [pltpu.VMEM((4, E // 4, N, N), jnp.bfloat16), pltpu.SemaphoreType.DMA((4,))],
        24,
        hbm=blocks,
    )


def rhs_kernel(
    place, edge_a, edge_b, misfit, y, x_bands, y_bands, hats, bottom, top, edges, sums
):
    me, odd = place[0], place[1]
    depth = E // 4
    planes = [edge[i] for edge in (edge_a, edge_b) for i in range(RADIUS)]
    filter_into(edges, planes, 0, x_bands, y_bands)

    sums[...] = jnp.zeros_like(sums)
    smooth = [float(SMOOTH[RADIUS + t] / SMOOTH[RADIUS]) for t in range(RADIUS + 1)]
    slope = [float(SLOPE[RADIUS + t] / SLOPE[RADIUS + 1]) for t in range(RADIUS + 1)]
    below = RADIUS * (1 - odd)
    above = RADIUS * odd
    starts = [(me ^ j) * depth for j in range(4)]

    def plane(k, z, rows):
        if z < 0:
            return edges[k, below + RADIUS + z, rows]
        if z >= E:
            return edges[k, above + z - E, rows]
        return y[k, starts[z // depth] + z % depth, rows]

    def rows_of(r, carry):
        at = pl.multiple_of(r * 8, 8)
        ey = r // (E // 8)
        rows = pl.ds(at, 8)
        window = [[plane(k, z, rows) for z in range(-RADIUS, RADIUS)] for k in range(3)]
        zero = jnp.zeros((8, N), jnp.float32)
        plain = [zero] * 3
        running = [zero] * 3
        for z in range(E):
            for k in range(3):
                window[k] = window[k] + [plane(k, z + RADIUS, rows)]
            m = misfit[z, rows]
            w = window[0]
            grads = [(w[4] - w[2]) + slope[2] * (w[5] - w[1]) + slope[3] * (w[6] - w[0])]
            for k in (1, 2):
                w = window[k]
                grads.append(
                    w[3]
                    + smooth[1] * (w[4] + w[2])
                    + smooth[2] * (w[5] + w[1])
                    + smooth[3] * (w[6] + w[0])
                )
            for k in range(3):
                plain[k] = plain[k] + grads[k] * m
                running[k] = running[k] + plain[k]
                window[k] = window[k][1:]
        row = lax.broadcasted_iota(jnp.int32, (8, N), 0) + (r % (E // 8)) * 8
        py = (row.astype(jnp.float32) + 0.5) * (1.0 / E)
        for k in range(3):
            gain = float(SLOPE[RADIUS + 1] if k == 0 else SMOOTH[RADIUS]) / E
            upper = (plain[k] * (1.0 + 0.5 / E) - running[k] * (1.0 / E)) * gain
            lower = plain[k] * gain - upper
            for iz, part in enumerate((lower, upper)):
                right = jnp.sum(part * py, axis=0, keepdims=True)
                left = jnp.sum(part, axis=0, keepdims=True) - right
                q = iz * 3 + k
                sums[ey, q : q + 1] += left
                sums[ey + 1, q : q + 1] += right
        return carry

    lax.fori_loop(0, N // 8, rows_of, 0)
    out = jnp.zeros((8, N), jnp.float32)
    for iy in range(ROW + 1):
        rest = sums[iy]
        for piece in range(3):
            part = rest.astype(jnp.bfloat16)
            rest = rest - part.astype(jnp.float32)
            out = out + jnp.dot(part, hats[iy], preferred_element_type=jnp.float32)
    for k in range(3):
        bottom[k] = out[k : k + 1, : (ROW + 1) ** 2]
        top[k] = out[3 + k : 4 + k, : (ROW + 1) ** 2]


def assemble(place, edges, misfit, y):
    return call(
        rhs_kernel,
        "rhs",
        (SMALL, SMALL),
        [place],
        [
            *edges, misfit, y,
            jnp.asarray(X_BANDS, jnp.bfloat16), jnp.asarray(Y_BANDS, jnp.bfloat16),
            jnp.asarray(RHS_HATS, jnp.bfloat16),
        ],
        [
            pltpu.VMEM((3, 2 * RADIUS, N, N), jnp.float32),
            pltpu.VMEM((ROW + 1, 8, N), jnp.float32),
        ],
        24,
    )


def body(tomogram, deformed, subvoxel, offsets):
    bricks = lax.axis_size("brick")
    me = lax.axis_index("scan")
    odd = lax.axis_index("brick") % 2
    place = jnp.stack([me, odd]).astype(jnp.int32)
    up = [(i, i + 1) for i in range(bricks - 1)]
    inside = [r for i in range(0, bricks - 1, 2) for r in ((i, i + 1), (i + 1, i))]
    outside = [r for i in range(1, bricks - 1, 2) for r in ((i, i + 1), (i + 1, i))]
    pairs = [(0, 1), (1, 0), (2, 3), (3, 2)]

    slab = pltpu.with_memory_space_constraint(deformed, pltpu.HBM)
    across = lax.ppermute(tomogram, "scan", [(0, 2), (1, 3), (2, 0), (3, 1)])
    near, far, far_end = split(place, pltpu.with_memory_space_constraint(subvoxel, pltpu.HBM), slab)
    offs = offsets.reshape(3, 1, -1)
    halo_a = lax.ppermute(near, "brick", inside)
    halo_b = lax.ppermute(far, "brick", outside)
    halo_c = lax.ppermute(far_end, "brick", outside)
    late = tomogram
    beside = lax.ppermute(late, "scan", pairs)
    samples = windows(place, offs, near, far, far_end, halo_a)
    across, samples = lax.optimization_barrier((across, samples))
    samples = [pltpu.with_memory_space_constraint(x, pltpu.HBM) for x in samples]
    relayed = lax.ppermute(across, "scan", pairs)
    blocks = (tomogram, beside, across, relayed)
    warped = warp(place, offs, (near, far, far_end, halo_a, halo_b, halo_c), samples)

    def pick(index, part):
        out = part(blocks[0])
        for j in range(1, 4):
            out = jnp.where((me ^ j) == index, part(blocks[j]), out)
        return out

    tail, head = pick(3, lambda b: b[-RADIUS:]), pick(0, lambda b: b[:RADIUS])
    send_a, send_b, warped = lax.optimization_barrier(
        (jnp.where(odd == 1, head, tail), jnp.where(odd == 1, tail, head), warped)
    )
    edges = (lax.ppermute(send_a, "brick", inside), lax.ppermute(send_b, "brick", outside))
    misfit, residual, y = filtered(place, blocks, warped)
    bottom, top = assemble(place, edges, misfit, y)
    node_rhs = bottom + lax.ppermute(top, "brick", up)
    return residual[None], node_rhs[None]


def solution(mesh):
    return jax.shard_map(
        body,
        mesh=mesh,
        in_specs=(
            P(("brick", "scan"), None, None),
            P("scan", "brick", None, None),
            P("scan", None, "brick", None),
            P("scan", None, "brick"),
        ),
        out_specs=(P("scan", "brick", None, None), P("scan", None, "brick", None)),
        check_vma=False,
    )
```

time: 61.2 us -> 45.5 us (0.74)
  the two profiles are of different devices: /device:TPU:12 before, /device:TPU:4 now
where the time goes in v2:
time: 45.5 us; the launch traced here: 45.2 us
  Pallas kernels  17.6 us (39%)
  starting transfers between devices  16.3 us (36%)
  waiting for transfers between devices  9.12 us (20%)
  between operations  0.82 us (2%)
  other arithmetic  0.71 us (2%)
  local copies, waits for them, and re-layouts  0.7 us (2%)
    pallas_call x5, Pallas kernels, call(): pl.pallas_call(kernel, out_shape=outs, in_specs=specs + [HBM] * len(hbm),...  17.6 us
    ppermute x1, waiting for transfers between devices, body(): node_rhs = bottom + lax.ppermute(top, 'brick', up)  3.87 us
    ppermute x1, waiting for transfers between devices, body(): halo_b = lax.ppermute(far, 'brick', outside)  3.47 us
    ppermute x1, starting transfers between devices, body(): halo_c = lax.ppermute(far_end, 'brick', outside)  3.1 us
    ppermute x1, starting transfers between devices, body(): lax.ppermute(send_b, 'brick', outside)  3.07 us
    ppermute x1, starting transfers between devices, body(): halo_b = lax.ppermute(far, 'brick', outside)  3.06 us
    ppermute x1, starting transfers between devices, body(): across = lax.ppermute(tomogram, 'scan', [(0, 2), (1, 3), (2, 0), (3, 1)])  2.65 us
    ppermute x1, starting transfers between devices, body(): node_rhs = bottom + lax.ppermute(top, 'brick', up)  1.92 us
  transfers between devices with their start and end apart: 9, of which 4 were waited for; matrix products, arithmetic and copies ran while one was open for 0% of the time, Pallas kernels for 25%

profile of v2, /device:TPU:4, one launch (start us, length us, event | category | flops | bytes accessed | tf_op | source)
XLA Modules:
  0.0 45.2 jit_solution(5478534708714044873)
XLA Ops:
  0.7 0.1 pad_add_fusion.place
  0.7 1.8 %split.1 = (bf16[17,128,128]{2,1,0:T(8,128)(2,1)S(1)}, bf16[8,128,128]{2,1,0:T(8,128)(2,1)S(1)}, bf16[9,128,128]{2,1,0:T(8,128)(2,1)S(1)}) custom-call(s32[2]{0:T(128)S(1)} %pad_add_fusion.place, f32[1,3,1,25]{3,2,1,0:T(1,128)} %nodes_in.1, bf16[1,32,128,128]{3,2,1,0:T(8,128)(2,1)} %slab.1), custom_call_target="tpu_custom_call" | custom-call | tf_op jit(solution)/shard_map/split/pallas_call | solution.py:272
  2.5 0.1 collective-permute-start.1
  2.6 2.7 %collective-permute-start = (bf16[8,128,128]{2,1,0:T(8,128)(2,1)}, bf16[8,128,128]{2,1,0:T(8,128)(2,1)S(1)}, u32[]{:S(2)}, u32[]{:S(2)}) collective-permute-start(bf16[8,128,128]{2,1,0:T(8,128)(2,1)} %b0.1), channel_id=1, source_target_pairs={{0,2},{1,3},{2,0},{3,1},{4,6},{5,7},{6,4},{7,5},{8,10},{9,11},{10,... | collective-permute-start | bytes 786440 | tf_op jit(solution)/shard_map/ppermute | solution.py:494
  5.2 3.1 %collective-permute-start.5 = (bf16[9,128,128]{2,1,0:T(8,128)(2,1)S(1)}, bf16[9,128,128]{2,1,0:T(8,128)(2,1)S(1)}, u32[]{:S(2)}, u32[]{:S(2)}) collective-permute-start(bf16[9,128,128]{2,1,0:T(8,128)(2,1)S(1)} %get-tuple-element.20.far_end), channel_id=1, source_target_pairs={{4,8},{8,4},{12,16},{16,12},{20,24},{24,20},{5,9},{9,5},{13,17},{1... | collective-permute-start | bytes 884744 | tf_op jit(solution)/shard_map/ppermute | solution.py:499
  8.4 1.6 %collective-permute-start.3 = (bf16[8,128,128]{2,1,0:T(8,128)(2,1)}, bf16[8,128,128]{2,1,0:T(8,128)(2,1)S(1)}, u32[]{:S(2)}, u32[]{:S(2)}) collective-permute-start(bf16[8,128,128]{2,1,0:T(8,128)(2,1)} %b0.1), channel_id=1, source_target_pairs={{0,1},{1,0},{2,3},{3,2},{4,5},{5,4},{6,7},{7,6},{8,9},{9,8},{10,11... | collective-permute-start | bytes 786440 | tf_op jit(solution)/shard_map/ppermute | solution.py:501
  10.0 3.1 %collective-permute-start.4 = (bf16[8,128,128]{2,1,0:T(8,128)(2,1)S(1)}, bf16[8,128,128]{2,1,0:T(8,128)(2,1)S(1)}, u32[]{:S(2)}, u32[]{:S(2)}) collective-permute-start(bf16[8,128,128]{2,1,0:T(8,128)(2,1)S(1)} %get-tuple-element.19.far), channel_id=1, source_target_pairs={{4,8},{8,4},{12,16},{16,12},{20,24},{24,20},{5,9},{9,5},{13,17},{1... | collective-permute-start | bytes 786440 | tf_op jit(solution)/shard_map/ppermute | solution.py:498
  13.1 0.0 copy-start.4
  13.1 0.7 %copy-done.4 = s32[1,3,16]{2,0,1:T(1,128)S(1)} copy-done((s32[1,3,16]{2,0,1:T(1,128)S(1)}, s32[1,3,16]{2,0,1:T(1,128)}, u32[]{:S(2)}) %copy-start.4) | copy-done | bytes 216
  13.8 3.2 %windows.1 = (f32[4,17,40,128]{3,2,1,0:T(8,128)}, f32[4,17,40,128]{3,2,1,0:T(8,128)}) custom-call(s32[2]{0:T(128)S(1)} %pad_add_fusion.place, s32[3,1,16]{2,1,0:T(1,128)S(1)} %bitcast.8, bf16[17,128,128]{2,1,0:T(8,128)(2,1)S(1)} %get-tuple-element.18.near, bf16[8,128,128]{2,1,0:T(8,128)(2,1)S(1)} %get-tuple-element.19.far, ...), custom_call_target="tpu_custom_call" | custom-call | tf_op jit(solution)/shard_map/windows/pallas_call | solution.py:272
  17.0 1.2 %collective-permute-done.b2 = bf16[8,128,128]{2,1,0:T(8,128)(2,1)S(1)} collective-permute-done((bf16[8,128,128]{2,1,0:T(8,128)(2,1)}, bf16[8,128,128]{2,1,0:T(8,128)(2,1)S(1)}, u32[]{:S(2)}, u32[]{:S(2)}) %collective-permute-start) | collective-permute-done | bytes 262176 | tf_op jit(solution)/shard_map/ppermute | solution.py:494
  18.1 0.7 %collective-permute-start.2 = (bf16[8,128,128]{2,1,0:T(8,128)(2,1)S(1)}, bf16[8,128,128]{2,1,0:T(8,128)(2,1)S(1)}, u32[]{:S(2)}, u32[]{:S(2)}) collective-permute-start(bf16[8,128,128]{2,1,0:T(8,128)(2,1)S(1)} %collective-permute-done.b2), channel_id=1, source_target_pairs={{0,1},{1,0},{2,3},{3,2},{4,5},{5,4},{6,7},{7,6},{8,9},{9,8},{10,11... | collective-permute-start | bytes 786440 | tf_op jit(solution)/shard_map/ppermute | solution.py:505
  18.9 3.5 %collective-permute-done.4.far_halo = bf16[8,128,128]{2,1,0:T(8,128)(2,1)S(1)} collective-permute-done((bf16[8,128,128]{2,1,0:T(8,128)(2,1)S(1)}, bf16[8,128,128]{2,1,0:T(8,128)(2,1)S(1)}, u32[]{:S(2)}, u32[]{:S(2)}) %collective-permute-start.4) | collective-permute-done | bytes 262176 | tf_op jit(solution)/shard_map/ppermute | solution.py:498
  22.3 4.4 %warp.1.warped = f32[32,128,128]{2,1,0:T(8,128)S(1)} custom-call(s32[2]{0:T(128)S(1)} %pad_add_fusion.place, s32[3,1,16]{2,1,0:T(1,128)S(1)} %bitcast.9, bf16[17,128,128]{2,1,0:T(8,128)(2,1)S(1)} %get-tuple-element.18.near, bf16[8,128,128]{2,1,0:T(8,128)(2,1)S(1)} %get-tuple-element.19.far, bf16[9,128,128]{2,1,0:T(8,128)(2,1)S(1)} %get-tuple-element.20.far_end, ...), custom_call_target="tpu_custom_call" | custom-call | tf_op jit(solution)/shard_map/warp/pallas_call | solution.py:272
  26.8 0.0 copy-start.3
  26.8 0.6 %collective-permute-done.2.b3 = bf16[8,128,128]{2,1,0:T(8,128)(2,1)S(1)} collective-permute-done((bf16[8,128,128]{2,1,0:T(8,128)(2,1)S(1)}, bf16[8,128,128]{2,1,0:T(8,128)(2,1)S(1)}, u32[]{:S(2)}, u32[]{:S(2)}) %collective-permute-start.2) | collective-permute-done | bytes 262176 | tf_op jit(solution)/shard_map/ppermute | solution.py:505
  27.4 0.1 broadcast_select_fusion
  27.5 0.1 collective-permute-start.6
  27.6 3.1 %collective-permute-start.7 = (bf16[3,128,128]{2,1,0:T(8,128)(2,1)S(1)}, bf16[3,128,128]{2,1,0:T(8,128)(2,1)S(1)}, u32[]{:S(2)}, u32[]{:S(2)}) collective-permute-start(bf16[3,128,128]{2,1,0:T(8,128)(2,1)S(1)} %get-tuple-element.29), channel_id=1, source_target_pairs={{4,8},{8,4},{12,16},{16,12},{20,24},{24,20},{5,9},{9,5},{13,17},{1... | collective-permute-start | bytes 294920 | tf_op jit(solution)/shard_map/ppermute | solution.py:519
  30.7 3.9 %filters.1 = (f32[32,128,128]{2,1,0:T(8,128)S(1)}, bf16[32,128,128]{2,1,0:T(8,128)(2,1)}, f32[3,32,128,128]{3,2,1,0:T(8,128)S(1)}) custom-call(s32[2]{0:T(128)S(1)} %pad_add_fusion.place, f32[32,128,128]{2,1,0:T(8,128)S(1)} %warp.1.warped, bf16[128,256]{1,0:T(8,128)(2,1)S(1)} %copy-done.2, bf16[256,128]{1,0:T(8,128)(2,1)S(1)} %copy-done.1, ...), custom_call_target="tpu_custom_call" | custom-call | tf_op jit(solution)/shard_map/filters/pallas_call | solution.py:272
  34.6 4.3 %rhs.1 = (f32[3,1,25]{2,1,0:T(1,128)S(1)}, f32[3,1,25]{2,1,0:T(1,128)S(1)}) custom-call(s32[2]{0:T(128)S(1)} %pad_add_fusion.place, bf16[3,128,128]{2,1,0:T(8,128)(2,1)S(1)} %collective-permute-done.6.edge_a, bf16[3,128,128]{2,1,0:T(8,128)(2,1)S(1)} %collective-permute-done.7.edge_b, f32[32,128,128]{2,1,0:T(8,128)S(1)} %get-tuple-element.30.misfit, ...), custom_call_target="tpu_custom_call" | custom-call | tf_op jit(solution)/shard_map/rhs/pallas_call | solution.py:272
  38.9 1.9 %collective-permute-start.8 = (f32[3,1,25]{2,1,0:T(1,128)S(1)}, f32[3,1,25]{2,1,0:T(1,128)S(1)}, u32[]{:S(2)}, u32[]{:S(2)}) collective-permute-start(f32[3,1,25]{2,1,0:T(1,128)S(1)} %get-tuple-element.33), channel_id=1, source_target_pairs={{0,4},{4,8},{8,12},{12,16},{16,20},{20,24},{24,28},{1,5},{5,9},{9,... | collective-permute-start | bytes 908 | tf_op jit(solution)/shard_map/ppermute | solution.py:522
  40.8 3.9 %collective-permute-done.8 = f32[3,1,25]{2,1,0:T(1,128)S(1)} collective-permute-done((f32[3,1,25]{2,1,0:T(1,128)S(1)}, f32[3,1,25]{2,1,0:T(1,128)S(1)}, u32[]{:S(2)}, u32[]{:S(2)}) %collective-permute-start.8) | collective-permute-done | bytes 332 | tf_op jit(solution)/shard_map/ppermute | solution.py:522
  44.7 0.6 %add_bitcast_fusion = f32[1,3,1,25]{3,2,1,0:T(1,128)} fusion(f32[3,1,25]{2,1,0:T(1,128)S(1)} %get-tuple-element.32, f32[3,1,25]{2,1,0:T(1,128)S(1)} %collective-permute-done.8), kind=kLoop, calls=%fused_computation.8 | loop fusion | flops 75 | bytes 900
  (15 shorter events, 0.0 us)
Async XLA Ops:
  0.6 21.7 %copy-start.5 = (s32[1,3,16]{2,0,1:T(1,128)S(1)}, s32[1,3,16]{2,0,1:T(1,128)}, u32[]{:S(2)}) copy-start(s32[1,3,16]{2,0,1:T(1,128)} %param.12) | copy-start | bytes 580
  2.5 10.6 %collective-permute-start.1 = (bf16[17,128,128]{2,1,0:T(8,128)(2,1)S(1)}, bf16[17,128,128]{2,1,0:T(8,128)(2,1)S(1)}, u32[]{:S(2)}, u32[]{:S(2)}) collective-permute-start(bf16[17,128,128]{2,1,0:T(8,128)(2,1)S(1)} %get-tuple-element.18.near), channel_id=1, source_target_pairs={{0,4},{4,0},{8,12},{12,8},{16,20},{20,16},{24,28},{28,24},{1,5},{5... | collective-permute-start | bytes 1671176 | tf_op jit(solution)/shard_map/ppermute | solution.py:497
  2.6 15.6 %collective-permute-start = (bf16[8,128,128]{2,1,0:T(8,128)(2,1)}, bf16[8,128,128]{2,1,0:T(8,128)(2,1)S(1)}, u32[]{:S(2)}, u32[]{:S(2)}) collective-permute-start(bf16[8,128,128]{2,1,0:T(8,128)(2,1)} %b0.1), channel_id=1, source_target_pairs={{0,2},{1,3},{2,0},{3,1},{4,6},{5,7},{6,4},{7,5},{8,10},{9,11},{10,... | collective-permute-start | bytes 786440 | tf_op jit(solution)/shard_map/ppermute | solution.py:494
  5.2 17.1 %collective-permute-start.5 = (bf16[9,128,128]{2,1,0:T(8,128)(2,1)S(1)}, bf16[9,128,128]{2,1,0:T(8,128)(2,1)S(1)}, u32[]{:S(2)}, u32[]{:S(2)}) collective-permute-start(bf16[9,128,128]{2,1,0:T(8,128)(2,1)S(1)} %get-tuple-element.20.far_end), channel_id=1, source_target_pairs={{4,8},{8,4},{12,16},{16,12},{20,24},{24,20},{5,9},{9,5},{13,17},{1... | collective-permute-start | bytes 884744 | tf_op jit(solution)/shard_map/ppermute | solution.py:499
  8.4 18.4 %collective-permute-start.3 = (bf16[8,128,128]{2,1,0:T(8,128)(2,1)}, bf16[8,128,128]{2,1,0:T(8,128)(2,1)S(1)}, u32[]{:S(2)}, u32[]{:S(2)}) collective-permute-start(bf16[8,128,128]{2,1,0:T(8,128)(2,1)} %b0.1), channel_id=1, source_target_pairs={{0,1},{1,0},{2,3},{3,2},{4,5},{5,4},{6,7},{7,6},{8,9},{9,8},{10,11... | collective-permute-start | bytes 786440 | tf_op jit(solution)/shard_map/ppermute | solution.py:501
  10.0 12.3 %collective-permute-start.4 = (bf16[8,128,128]{2,1,0:T(8,128)(2,1)S(1)}, bf16[8,128,128]{2,1,0:T(8,128)(2,1)S(1)}, u32[]{:S(2)}, u32[]{:S(2)}) collective-permute-start(bf16[8,128,128]{2,1,0:T(8,128)(2,1)S(1)} %get-tuple-element.19.far), channel_id=1, source_target_pairs={{4,8},{8,4},{12,16},{16,12},{20,24},{24,20},{5,9},{9,5},{13,17},{1... | collective-permute-start | bytes 786440 | tf_op jit(solution)/shard_map/ppermute | solution.py:498
  13.1 0.7 %copy-start.4 = (s32[1,3,16]{2,0,1:T(1,128)S(1)}, s32[1,3,16]{2,0,1:T(1,128)}, u32[]{:S(2)}) copy-start(s32[1,3,16]{2,0,1:T(1,128)} %param.12) | copy-start | bytes 580
  18.1 9.2 %collective-permute-start.2 = (bf16[8,128,128]{2,1,0:T(8,128)(2,1)S(1)}, bf16[8,128,128]{2,1,0:T(8,128)(2,1)S(1)}, u32[]{:S(2)}, u32[]{:S(2)}) collective-permute-start(bf16[8,128,128]{2,1,0:T(8,128)(2,1)S(1)} %collective-permute-done.b2), channel_id=1, source_target_pairs={{0,1},{1,0},{2,3},{3,2},{4,5},{5,4},{6,7},{7,6},{8,9},{9,8},{10,11... | collective-permute-start | bytes 786440 | tf_op jit(solution)/shard_map/ppermute | solution.py:505
  18.9 8.5 %copy-start = (bf16[8,128,128]{2,1,0:T(8,128)(2,1)S(1)}, bf16[8,128,128]{2,1,0:T(8,128)(2,1)}, u32[]{:S(2)}) copy-start(bf16[8,128,128]{2,1,0:T(8,128)(2,1)} %b0.1) | copy-start | bytes 786436
  18.9 11.8 %copy-start.1 = (bf16[256,128]{1,0:T(8,128)(2,1)S(1)}, bf16[256,128]{1,0:T(8,128)(2,1)}, u32[]{:S(2)}) copy-start(bf16[256,128]{1,0:T(8,128)(2,1)} %constant.33.clone.y_bands) | copy-start | bytes 196612
  18.9 11.8 %copy-start.2 = (bf16[128,256]{1,0:T(8,128)(2,1)S(1)}, bf16[128,256]{1,0:T(8,128)(2,1)}, u32[]{:S(2)}) copy-start(bf16[128,256]{1,0:T(8,128)(2,1)} %constant.32.clone.x_bands) | copy-start | bytes 196612
  26.8 7.8 %copy-start.3 = (bf16[5,128,128]{2,1,0:T(8,128)(2,1)S(1)}, bf16[5,128,128]{2,1,0:T(8,128)(2,1)}, u32[]{:S(2)}) copy-start(bf16[5,128,128]{2,1,0:T(8,128)(2,1)} %constant.34.clone.hats) | copy-start | bytes 491524
  27.5 7.1 %collective-permute-start.6 = (bf16[3,128,128]{2,1,0:T(8,128)(2,1)S(1)}, bf16[3,128,128]{2,1,0:T(8,128)(2,1)S(1)}, u32[]{:S(2)}, u32[]{:S(2)}) collective-permute-start(bf16[3,128,128]{2,1,0:T(8,128)(2,1)S(1)} %broadcast_select_fusion.1), channel_id=1, source_target_pairs={{0,4},{4,0},{8,12},{12,8},{16,20},{20,16},{24,28},{28,24},{1,5},{5... | collective-permute-start | bytes 294920 | tf_op jit(solution)/shard_map/ppermute | solution.py:519
  27.6 7.0 %collective-permute-start.7 = (bf16[3,128,128]{2,1,0:T(8,128)(2,1)S(1)}, bf16[3,128,128]{2,1,0:T(8,128)(2,1)S(1)}, u32[]{:S(2)}, u32[]{:S(2)}) collective-permute-start(bf16[3,128,128]{2,1,0:T(8,128)(2,1)S(1)} %get-tuple-element.29), channel_id=1, source_target_pairs={{4,8},{8,4},{12,16},{16,12},{20,24},{24,20},{5,9},{9,5},{13,17},{1... | collective-permute-start | bytes 294920 | tf_op jit(solution)/shard_map/ppermute | solution.py:519
  38.9 5.8 %collective-permute-start.8 = (f32[3,1,25]{2,1,0:T(1,128)S(1)}, f32[3,1,25]{2,1,0:T(1,128)S(1)}, u32[]{:S(2)}, u32[]{:S(2)}) collective-permute-start(f32[3,1,25]{2,1,0:T(1,128)S(1)} %get-tuple-element.33), channel_id=1, source_target_pairs={{0,4},{4,8},{8,12},{12,16},{16,20},{20,24},{24,28},{1,5},{5,9},{9,... | collective-permute-start | bytes 908 | tf_op jit(solution)/shard_map/ppermute | solution.py:522

commit v3 on v2

v3 whole, which is shorter than its diff:
```python
import functools

import jax
import jax.numpy as jnp
import numpy as np
from jax import lax
from jax.experimental import pallas as pl
from jax.experimental.pallas import tpu as pltpu
from jax.sharding import PartitionSpec as P

E = 32
HALO = 16
RADIUS = 3
N = 128
ROW = N // E
WIN = 48
HALF = E // 2
FAR = HALO // 2
ROWS = HALO + N + E


def taps():
    t = np.arange(-RADIUS, RADIUS + 1).astype(np.float32)
    g = np.exp(-t * t / np.float32(2.0))
    smooth = g / np.sum(g)
    slope = t * g / np.sum(t * t * g)
    return [np.asarray(v, jnp.bfloat16).astype(np.float32) for v in (smooth, slope)]


def band(coeff):
    out = np.zeros((N, N), np.float32)
    for tap in range(2 * RADIUS + 1):
        out += coeff[tap] * np.eye(N, k=RADIUS - tap, dtype=np.float32)
    return out


SMOOTH, SLOPE = taps()
BAND_S, BAND_D = band(SMOOTH), band(SLOPE)
X_BANDS = np.concatenate(
    [
        np.concatenate([BAND_S, BAND_D], axis=1),
        np.concatenate([BAND_S, 0 * BAND_S], axis=1),
        np.concatenate([0 * BAND_S, BAND_S], axis=1),
    ]
)
Y_BANDS = np.concatenate([BAND_S.T, BAND_D.T], axis=0)


def rhs_hats():
    at = (np.arange(N, dtype=np.float32) + 0.5) / E
    hats = np.maximum(0.0, 1.0 - np.abs(at[:, None] - np.arange(ROW + 1, dtype=np.float32)))
    out = np.zeros((ROW + 1, N, N), np.float32)
    for iy in range(ROW + 1):
        out[iy, :, iy * (ROW + 1) : (iy + 1) * (ROW + 1)] = hats
    return out


RHS_HATS = rhs_hats()


def lane_position(shape, dim):
    v = lax.broadcasted_iota(jnp.int32, shape, dim)
    return ((v % E).astype(jnp.float32) + 0.5) * (1.0 / E)


def split_kernel(place, nodes_in, slab, near, far, far_end, nodes, wide, sems):
    odd = place[1]
    parts = ((1 - odd, 0, HALO, near), (odd, 0, FAR, far), (odd, FAR, HALO - FAR, far_end))
    copies = [
        pltpu.make_async_copy(
            slab.at[0, pl.ds(HALO * first + skip, count)], out.at[pl.ds(0, count)], sems.at[i]
        )
        for i, (first, skip, count, out) in enumerate(parts)
    ]
    fetch = pltpu.make_async_copy(nodes_in, nodes, sems.at[len(parts)])
    fetch.start()
    for c in copies:
        c.start()
    fetch.wait()
    wide[...] = jnp.zeros_like(wide)
    for c in range(3):
        wide[c : c + 1, 0 : (ROW + 1) ** 2] = nodes[0, c]
    rest = wide[...]
    rows = []
    for _ in range(3):
        rows.append(rest.astype(jnp.bfloat16).astype(jnp.float32))
        rest = rest - rows[-1]
    rows = jnp.concatenate(rows + [rest], axis=0).astype(jnp.bfloat16)
    for out, last in ((near, HALO), (far, FAR)):
        out[last, 0 : 4 * 8] = rows
        out[last, 4 * 8 : N] = jnp.zeros((N - 4 * 8, N), jnp.bfloat16)
    for c in copies:
        c.wait()


def shifted(below, offs, fetch, middle, other, halo, vol, lhs, s_val, s_dif, done=None):
    zero_top = jnp.zeros((HALO, N), jnp.float32)
    zero_end = jnp.zeros((E, N), jnp.float32)

    def fill(srcs, first):
        counts = (HALO,) if len(srcs) == 1 else (FAR, HALO - FAR)
        for src, count in zip(srcs, counts):

            def step(i, c, src=src, at=first):
                vol[at + i, 0:HALO] = zero_top
                vol[at + i, HALO : HALO + N] = src[i].astype(jnp.float32)
                vol[at + i, HALO + N : ROWS] = zero_end
                return c

            lax.fori_loop(0, count, step, 0, unroll=count // 2)
            first = first + count

    fill(halo, jnp.where(below, 0, E))
    fill(middle, HALO)
    fill(other, jnp.where(below, E, 0))
    fetch.wait()

    lane = lax.broadcasted_iota(jnp.int32, (WIN, N), 1)
    src_lane = lax.broadcasted_iota(jnp.int32, (N, N), 0)
    out_lane = lax.broadcasted_iota(jnp.int32, (N, N), 1)
    distance = src_lane - out_lane
    block = out_lane // E

    def element_row(ey):
        first_z, first_y, shift = [], [], []
        for ex in range(ROW):
            e = ey * ROW + ex
            first_z.append(offs[0, 0, e] + HALO)
            first_y.append(ey * E + offs[1, 0, e] + HALO)
            shift.append(offs[2, 0, e])
        mats = []
        for ex in range(2):
            moved = jnp.where(block == ex, distance - shift[ex], N)
            moved = jnp.where(block == ex + 2, distance - shift[ex + 2], moved)
            here = jnp.where(moved == 0, 1.0, 0.0)
            mats.append(jnp.concatenate([here, jnp.where(moved == 1, 1.0, 0.0) - here], axis=1))
        select = jnp.concatenate(mats, axis=0).astype(jnp.bfloat16)

        for z in range(HALF + 1):
            part = [vol[first_z[ex] + z, pl.ds(first_y[ex], WIN), :] for ex in range(ROW)]
            lhs[z, :, :N] = jnp.where(lane < E + HALO, part[0], part[2]).astype(jnp.bfloat16)
            lhs[z, :, N:] = jnp.where(lane < 2 * E + HALO, part[1], part[3]).astype(jnp.bfloat16)

        out = jnp.dot(
            lhs[...].reshape((HALF + 1) * WIN, 2 * N), select, preferred_element_type=jnp.float32
        )
        out = out.reshape(HALF + 1, WIN, 2 * N)
        s_val[ey] = out[:, : E + 8, :N]
        s_dif[ey] = out[:, : E + 8, N:]
        if done is not None:
            done(ey)

    for ey in range(ROW):
        element_row(ey)


def node_rows(plane, hats):
    row = lax.broadcasted_iota(jnp.int32, (16, N), 0)
    mine = lax.broadcasted_iota(jnp.int32, (16, N), 1) // (ROW + 1) == row % (ROW + 1)
    component = row // (ROW + 1)
    out = jnp.zeros((16, N), jnp.float32)
    values = plane[0 : 4 * 8].astype(jnp.float32)
    for piece in range(3):
        v = values[piece * 8 : piece * 8 + 8]
        line = jnp.where(component == 0, v[0:1], jnp.where(component == 1, v[1:2], v[2:3]))
        line = jnp.where(mine, line, 0.0).astype(jnp.bfloat16)
        out = out + jnp.dot(line, hats, preferred_element_type=jnp.float32)
    return out


def displacements(odd, near, near_halo, far_halo, w_base, w_step):
    node = lax.broadcasted_iota(jnp.int32, (N, N), 0)
    at = (lax.broadcasted_iota(jnp.int32, (N, N), 1).astype(jnp.float32) + 0.5) * (1.0 / E)
    hat = jnp.maximum(0.0, 1.0 - jnp.abs(at - (node % (ROW + 1)).astype(jnp.float32)))
    hats = jnp.where(node < (ROW + 1) ** 2, hat, 0.0).astype(jnp.bfloat16)
    lower = node_rows(near[HALO], hats)
    upper = node_rows(jnp.where(odd, far_halo[FAR], near_halo[HALO]), hats)
    py = lane_position((E, N), 0)
    for c in range(3):
        for ey in range(ROW):
            q = c * (ROW + 1) + ey
            lo = lower[q : q + 1] + py * (lower[q + 1 : q + 2] - lower[q : q + 1])
            up = upper[q : q + 1] + py * (upper[q + 1 : q + 2] - upper[q : q + 1])
            w_step[c, ey * E : (ey + 1) * E] = up - lo
            w_base[c, ey * E : (ey + 1) * E] = lo


def interpolate(val, dif, w_base, w_step, first_plane, warped, ey):
    start = first_plane.astype(jnp.float32) * (1.0 / E)

    for base in range(0, E, 8):
        at = ey * E + base
        wz1, wy1, wx1 = [w_step[k, pl.ds(at, 8)] for k in range(3)]
        wz0, wy0, wx0 = [
            w_base[k, pl.ds(at, 8)] + start * w for k, w in enumerate((wz1, wy1, wx1))
        ]

        def corners(z, base=base):
            return (
                val[ey, z, pl.ds(base, 8)],
                dif[ey, z, pl.ds(base, 8)],
                val[ey, z, pl.ds(base + 1, 8)],
                dif[ey, z, pl.ds(base + 1, 8)],
            )

        lower = corners(0)
        for z in range(HALF):
            upper = corners(z + 1)
            p = (z + 0.5) / E
            wz = wz0 + p * wz1
            wy = wy0 + p * wy1
            wx = wx0 + p * wx1
            lines = []
            for v0, d0, v1, d1 in (lower, upper):
                a0 = v0 + wx * d0
                a1 = v1 + wx * d1
                lines.append(a0 + wy * (a1 - a0))
            warped[z, pl.ds(at, 8)] = lines[0] + wz * (lines[1] - lines[0])
            lower = upper


def window_kernel(
    place, near, far, far_end, near_halo, offs_in,
    val_out, dif_out, vol, lhs, s_val, s_dif, offs, sem, sems,
):
    fetch = pltpu.make_async_copy(offs_in, offs, sem)
    fetch.start()

    def copies(ey):
        return [
            pltpu.make_async_copy(src.at[ey], out.at[ey], sems.at[i, ey])
            for i, (src, out) in enumerate(((s_val, val_out), (s_dif, dif_out)))
        ]

    def done(ey):
        for c in copies(ey):
            c.start()

    shifted(
        place[1] == 1, offs, fetch, (near,), (far, far_end), (near_halo,), vol, lhs, s_val, s_dif, done
    )
    for ey in range(ROW):
        for c in copies(ey):
            c.wait()


def first_kernel(
    place, near, near_halo, far_halo, val_in, dif_in, warped, w_base, w_step, val, dif, sems
):
    copies = [
        [
            pltpu.make_async_copy(src.at[ey], out.at[ey], sems.at[i, ey])
            for i, (src, out) in enumerate(((val_in, val), (dif_in, dif)))
        ]
        for ey in range(ROW)
    ]
    for pair in copies:
        for c in pair:
            c.start()
    odd = place[1] == 1
    displacements(odd, near, near_halo, far_halo, w_base, w_step)
    for ey, pair in enumerate(copies):
        for c in pair:
            c.wait()
        interpolate(val, dif, w_base, w_step, jnp.where(odd, 0, HALF), warped, ey)


def second_kernel(
    place, near, far, far_end, far_halo, far_halo_end, w_base, w_step,
    warp_a, b0, b1, x_bands, y_bands, offs_in,
    warped, residual, y, misfit, vol, lhs, s_val, s_dif, offs, sem, rounded, out_sem,
):
    odd = place[1] == 1
    fetch = pltpu.make_async_copy(offs_in, offs, sem)
    fetch.start()
    halo = (far_halo, far_halo_end)
    shifted(
        jnp.logical_not(odd), offs, fetch, (far, far_end), (near,), halo, vol, lhs, s_val, s_dif
    )
    for ey in range(ROW):
        interpolate(s_val, s_dif, w_base, w_step, jnp.where(odd, HALF, 0), warped, ey)
    filter_half(
        (0, 1), place, warp_a, warped, (b0, b1), x_bands, y_bands,
        residual, y, misfit, rounded, out_sem,
    ).wait()


VMEM = pl.BlockSpec(memory_space=pltpu.VMEM)
SMEM = pl.BlockSpec(memory_space=pltpu.SMEM)
HBM = pl.BlockSpec(memory_space=pltpu.HBM)
FIELD = jax.ShapeDtypeStruct((3, N, N), jnp.float32)
HALF_VOLUME = jax.ShapeDtypeStruct((HALF, N, N), jnp.float32)
SAMPLES = (ROW, HALF + 1, E + 8, N)
RESIDUAL = jax.ShapeDtypeStruct((E, N, N), jnp.bfloat16)
FILTERED = jax.ShapeDtypeStruct((3, HALF, N, N), jnp.float32)
SMALL = jax.ShapeDtypeStruct((3, 1, (ROW + 1) ** 2), jnp.float32)


def call(kernel, name, outs, smem, vmem, scratch, mib, hbm=(), hbm_outs=(), alias=None):
    specs = [SMEM] * len(smem) + [VMEM] * len(vmem)
    return pl.pallas_call(
        kernel,
        out_shape=outs,
        in_specs=specs + [HBM] * len(hbm),
        out_specs=tuple(HBM if i in hbm_outs else VMEM for i in range(len(outs))),
        input_output_aliases=alias or {},
        scratch_shapes=scratch,
        compiler_params=pltpu.CompilerParams(vmem_limit_bytes=mib * 1024 * 1024),
        name=name,
    )(*smem, *vmem, *hbm)


def split(place, nodes, slab):
    return call(
        split_kernel,
        "split",
        tuple(jax.ShapeDtypeStruct((n, N, N), jnp.bfloat16) for n in (HALO + 1, FAR + 1, HALO - FAR)),
        [place],
        [],
        [
            pltpu.VMEM((1, 3, 1, (ROW + 1) ** 2), jnp.float32),
            pltpu.VMEM((8, N), jnp.float32),
            pltpu.SemaphoreType.DMA((4,)),
        ],
        4,
        hbm=[nodes, slab],
    )


SAMPLE_SCRATCH = [pltpu.VMEM(SAMPLES, jnp.float32)] * 2
WINDOW_SCRATCH = [
    pltpu.VMEM((E + HALO, ROWS, N), jnp.float32),
    pltpu.VMEM((HALF + 1, WIN, 2 * N), jnp.bfloat16),
    *SAMPLE_SCRATCH,
    pltpu.SMEM((3, 1, ROW * ROW), jnp.int32),
    pltpu.SemaphoreType.DMA,
]
EACH_ROW = pltpu.SemaphoreType.DMA((2, ROW))


def windows(place, offs, planes):
    out = pltpu.HBM(SAMPLES, jnp.float32)
    scratch = WINDOW_SCRATCH + [EACH_ROW]
    return call(
        window_kernel, "windows", (out, out), [place], planes, scratch, 20, hbm=[offs], hbm_outs=(0, 1)
    )


def first_half(place, planes, samples):
    samples = [pltpu.with_memory_space_constraint(x, pltpu.HBM) for x in samples]
    scratch = SAMPLE_SCRATCH + [EACH_ROW]
    outs = (HALF_VOLUME, FIELD, FIELD)
    return call(first_kernel, "first_half", outs, [place], planes, scratch, 16, hbm=samples)


ROUNDED = [pltpu.VMEM((HALF, N, N), jnp.bfloat16), pltpu.SemaphoreType.DMA]


def bands():
    return jnp.asarray(X_BANDS, jnp.bfloat16), jnp.asarray(Y_BANDS, jnp.bfloat16)


def second_half(place, offs, planes, warp_a, blocks):
    return call(
        second_kernel,
        "second_half",
        (HALF_VOLUME, RESIDUAL, FILTERED, HALF_VOLUME),
        [place],
        [*planes, warp_a, *blocks, *bands()],
        WINDOW_SCRATCH + ROUNDED,
        32,
        hbm=[offs],
        hbm_outs=(1,),
    )


def filter_into(y, planes, at, x_bands, y_bands):
    count = len(planes)
    smoothed, slopes = [], []
    for i in range(0, count, 2):
        pair = jnp.concatenate(planes[i : i + 2], axis=1)
        along_y = jnp.dot(y_bands[...], pair, preferred_element_type=jnp.float32)
        along_y = along_y.astype(jnp.bfloat16)
        smoothed += [along_y[:N, :N], along_y[:N, N:]]
        slopes.append(along_y[N:])
    rows = pl.ds(at, count)
    out = jnp.dot(jnp.concatenate(smoothed), x_bands[0:N], preferred_element_type=jnp.float32)
    y[0, rows] = out[:, :N].reshape(-1, N, N)
    y[2, rows] = out[:, N:].reshape(-1, N, N)
    out = jnp.dot(jnp.concatenate(slopes), x_bands[N:], preferred_element_type=jnp.float32)
    for i in range(count):
        y[1, at + i] = out[i // 2 * N : i // 2 * N + N, i % 2 * N : i % 2 * N + N]


def filter_half(
    slots, place, warp_a, warp_b, blocks, x_bands, y_bands, residual, y, misfit, rounded, sem
):
    me, odd = place[0], place[1]
    depth = blocks[0].shape[0]
    half = (me ^ slots[0]) // 2

    def subtract(warped):
        for j, b in zip(slots, blocks):
            at = ((me ^ j) % 2) * depth
            for i in range(depth):
                m = warped[at + i] - b[i].astype(jnp.float32)
                misfit[at + i] = m
                rounded[at + i] = m.astype(jnp.bfloat16)

    pl.when(half + odd == 1)(lambda: subtract(warp_a))
    pl.when(half + odd != 1)(lambda: subtract(warp_b))
    out = pltpu.make_async_copy(rounded, residual.at[pl.ds(half * HALF, HALF)], sem)
    out.start()
    for j, b in zip(slots, blocks):
        at = ((me ^ j) % 2) * depth
        filter_into(y, [b[i] for i in range(depth)], at, x_bands, y_bands)
    return out


def add_up(sums, odd, y, misfit, edges, ranges):
    smooth = [float(SMOOTH[RADIUS + t] / SMOOTH[RADIUS]) for t in range(RADIUS + 1)]
    slope = [float(SLOPE[RADIUS + t] / SLOPE[RADIUS + 1]) for t in range(RADIUS + 1)]
    below = RADIUS * (1 - odd)
    above = RADIUS * odd

    def plane(k, z, rows):
        if z < 0:
            return edges[k, below + RADIUS + z, rows]
        if z >= E:
            return edges[k, above + z - E, rows]
        return y[z // HALF][k, z % HALF, rows]

    def planes_of(rows, begin, end):
        window = [[plane(k, begin + t, rows) for t in range(-RADIUS, RADIUS)] for k in range(3)]
        zero = jnp.zeros((8, N), jnp.float32)
        plain = [zero] * 3
        running = [zero] * 3
        for z in range(begin, end):
            for k in range(3):
                window[k] = window[k] + [plane(k, z + RADIUS, rows)]
            m = misfit[z // HALF][z % HALF, rows]
            w = window[0]
            grads = [(w[4] - w[2]) + slope[2] * (w[5] - w[1]) + slope[3] * (w[6] - w[0])]
            for k in (1, 2):
                w = window[k]
                grads.append(
                    w[3]
                    + smooth[1] * (w[4] + w[2])
                    + smooth[2] * (w[5] + w[1])
                    + smooth[3] * (w[6] + w[0])
                )
            for k in range(3):
                plain[k] = plain[k] + grads[k] * m
                running[k] = running[k] + plain[k]
                window[k] = window[k][1:]
        return plain, [plain[k] * ((end + 0.5) / E) - running[k] * (1.0 / E) for k in range(3)]

    def rows_of(r, carry):
        rows = pl.ds(pl.multiple_of(r * 8, 8), 8)
        ey = r // (E // 8)
        parts = [planes_of(rows, begin, end) for begin, end in ranges]
        row = lax.broadcasted_iota(jnp.int32, (8, N), 0) + (r % (E // 8)) * 8
        py = (row.astype(jnp.float32) + 0.5) * (1.0 / E)
        for k in range(3):
            plain = sum(p[0][k] for p in parts[1:]) + parts[0][0][k]
            upper = sum(p[1][k] for p in parts[1:]) + parts[0][1][k]
            for iz, part in enumerate((plain - upper, upper)):
                right = part * py
                sums[ey, iz * 3 + k] += part - right
                sums[ey + 1, iz * 3 + k] += right
        return carry

    lax.fori_loop(0, N // 8, rows_of, 0)


def inner_kernel(
    place, warp_a, warp_b, b2, b3, y_a, misfit_a, x_bands, y_bands, residual_in,
    residual, y, misfit, sums, rounded, sem,
):
    me, odd = place[0], place[1]
    out = filter_half(
        (2, 3), place, warp_a, warp_b, (b2, b3), x_bands, y_bands,
        residual, y, misfit, rounded, sem,
    )
    sums[...] = jnp.zeros_like(sums)
    inner = (None, [(RADIUS, E - RADIUS)])
    pl.when(me < 2)(lambda: add_up(sums, odd, (y_a, y), (misfit_a, misfit), *inner))
    pl.when(me >= 2)(lambda: add_up(sums, odd, (y, y_a), (misfit, misfit_a), *inner))
    out.wait()


def outer_kernel(
    place, edge_a, edge_b, y_a, misfit_a, y_b, misfit_b, earlier, x_bands, y_bands, hats,
    bottom, top, edges, sums,
):
    me, odd = place[0], place[1]
    planes = [edge[i] for edge in (edge_a, edge_b) for i in range(RADIUS)]
    filter_into(edges, planes, 0, x_bands, y_bands)
    sums[...] = earlier[...]

    outer = (edges, [(0, RADIUS), (E - RADIUS, E)])
    pl.when(me < 2)(lambda: add_up(sums, odd, (y_a, y_b), (misfit_a, misfit_b), *outer))
    pl.when(me >= 2)(lambda: add_up(sums, odd, (y_b, y_a), (misfit_b, misfit_a), *outer))
    out = jnp.zeros((48, N), jnp.float32)
    for iy in range(ROW + 1):
        rest = sums[iy].reshape(48, N)
        for piece in range(3):
            part = rest.astype(jnp.bfloat16)
            rest = rest - part.astype(jnp.float32)
            out = out + jnp.dot(part, hats[iy], preferred_element_type=jnp.float32)
    out = jnp.sum(out.reshape(6, 8, N), axis=1)
    for k in range(3):
        gain = float(SLOPE[RADIUS + 1] if k == 0 else SMOOTH[RADIUS]) / E
        bottom[k] = out[k : k + 1, : (ROW + 1) ** 2] * gain
        top[k] = out[3 + k : 4 + k, : (ROW + 1) ** 2] * gain


SUMS = jax.ShapeDtypeStruct((ROW + 1, 6, 8, N), jnp.float32)


def inner(place, halves, blocks, lower, residual):
    return call(
        inner_kernel,
        "inner",
        (RESIDUAL, FILTERED, HALF_VOLUME, SUMS),
        [place],
        [*halves, *blocks, *lower, *bands()],
        ROUNDED,
        32,
        hbm=[residual],
        hbm_outs=(0,),
        alias={9: 0},
    )


def assemble(place, edges, halves, earlier):
    return call(
        outer_kernel,
        "outer",
        (SMALL, SMALL),
        [place],
        [
            *edges, *halves, earlier,
            *bands(),
            jnp.asarray(RHS_HATS, jnp.bfloat16),
        ],
        [
            pltpu.VMEM((3, 2 * RADIUS, N, N), jnp.float32),
            pltpu.VMEM(SUMS.shape, jnp.float32),
        ],
        24,
    )


def body(tomogram, deformed, subvoxel, offsets):
    bricks = lax.axis_size("brick")
    me = lax.axis_index("scan")
    odd = lax.axis_index("brick") % 2
    place = jnp.stack([me, odd]).astype(jnp.int32)
    up = [(i, i + 1) for i in range(bricks - 1)]
    inside = [r for i in range(0, bricks - 1, 2) for r in ((i, i + 1), (i + 1, i))]
    outside = [r for i in range(1, bricks - 1, 2) for r in ((i, i + 1), (i + 1, i))]
    pairs = [(0, 1), (1, 0), (2, 3), (3, 2)]

    slab = pltpu.with_memory_space_constraint(deformed, pltpu.HBM)
    across = lax.ppermute(tomogram, "scan", [(0, 2), (1, 3), (2, 0), (3, 1)])
    near, far, far_end = split(place, pltpu.with_memory_space_constraint(subvoxel, pltpu.HBM), slab)
    offs = pltpu.with_memory_space_constraint(offsets.reshape(3, 1, -1), pltpu.HBM)
    halo_a = lax.ppermute(near, "brick", inside)
    halo_b = lax.ppermute(far, "brick", outside)
    halo_c = lax.ppermute(far_end, "brick", outside)
    late = tomogram
    beside = lax.ppermute(late, "scan", pairs)
    slab_parts = (near, far, far_end)
    samples = windows(place, offs, (*slab_parts, halo_a))
    across, samples = lax.optimization_barrier((across, samples))
    relayed = lax.ppermute(across, "scan", pairs)
    blocks = (tomogram, beside, across, relayed)
    warp_a, *field = first_half(place, (near, halo_a, halo_b), samples)
    warp_b, residual, *lower = second_half(
        place, offs, (*slab_parts, halo_b, halo_c, *field), warp_a, blocks[:2]
    )
    halves = (warp_a, warp_b)

    def pick(index, part):
        out = part(blocks[0])
        for j in range(1, 4):
            out = jnp.where((me ^ j) == index, part(blocks[j]), out)
        return out

    tail, head = pick(3, lambda b: b[-RADIUS:]), pick(0, lambda b: b[:RADIUS])
    send_a, send_b, lower[0] = lax.optimization_barrier(
        (jnp.where(odd == 1, head, tail), jnp.where(odd == 1, tail, head), lower[0])
    )
    edges = (lax.ppermute(send_a, "brick", inside), lax.ppermute(send_b, "brick", outside))
    residual, y, misfit, sums = inner(place, halves, blocks[2:], lower, residual)
    bottom, top = assemble(place, edges, (*lower, y, misfit), sums)
    node_rhs = bottom + lax.ppermute(top, "brick", up)
    return residual[None], node_rhs[None]


def solution(mesh):
    return jax.shard_map(
        body,
        mesh=mesh,
        in_specs=(
            P(("brick", "scan"), None, None),
            P("scan", "brick", None, None),
            P("scan", None, "brick", None),
            P("scan", None, "brick"),
        ),
        out_specs=(P("scan", "brick", None, None), P("scan", None, "brick", None)),
        check_vma=False,
    )
```

time: 45.5 us -> 43.4 us (0.954)
  waiting for transfers between devices: 9.12 us -> 6.89 us
  Pallas kernels: 17.6 us -> 18.4 us
  local copies, waits for them, and re-layouts: 0.7 us -> 0.03 us
    ppermute x1, waiting for transfers between devices: 3.47 us -> 0.01 us  [body(): halo_b = lax.ppermute(far, 'brick', outside)]
    ppermute x1, waiting for transfers between devices: 0.01 us -> 0.82 us  [body(): beside = lax.ppermute(late, 'scan', pairs)]
    pallas_call x5 -> x6, Pallas kernels: 17.6 us -> 18.4 us  [call(): pl.pallas_call(kernel, out_shape=outs, in_specs=specs + [HBM] * len(hbm),...]
    unnamed x12 -> x8, local copies, waits for them, and re-layouts: 0.7 us -> 0.03 us
  transfers between devices with their start and end apart: 9 -> 9, of which waited for: 4 -> 5; matrix products, arithmetic and copies ran while one was open for 0% -> 0% of each run, Pallas kernels for 25% -> 33%
where the time goes in v3:
time: 43.4 us; the launch traced here: 43.1 us
  Pallas kernels  18.4 us (42%)
  starting transfers between devices  16.3 us (38%)
  waiting for transfers between devices  6.89 us (16%)
  between operations  0.82 us (2%)
  other arithmetic  0.7 us (2%)
    pallas_call x6, Pallas kernels, call(): pl.pallas_call(kernel, out_shape=outs, in_specs=specs + [HBM] * len(hbm),...  18.4 us
    ppermute x1, waiting for transfers between devices, body(): node_rhs = bottom + lax.ppermute(top, 'brick', up)  3.87 us
    ppermute x1, starting transfers between devices, body(): halo_b = lax.ppermute(far, 'brick', outside)  3.1 us
    ppermute x1, starting transfers between devices, body(): lax.ppermute(send_b, 'brick', outside)  3.07 us
    ppermute x1, starting transfers between devices, body(): halo_c = lax.ppermute(far_end, 'brick', outside)  3.06 us
    ppermute x1, starting transfers between devices, body(): across = lax.ppermute(tomogram, 'scan', [(0, 2), (1, 3), (2, 0), (3, 1)])  2.65 us
    ppermute x1, starting transfers between devices, body(): node_rhs = bottom + lax.ppermute(top, 'brick', up)  1.92 us
    ppermute x1, starting transfers between devices, body(): beside = lax.ppermute(late, 'scan', pairs)  1.64 us
  transfers between devices with their start and end apart: 9, of which 5 were waited for; matrix products, arithmetic and copies ran while one was open for 0% of the time, Pallas kernels for 33%

profile of v3, /device:TPU:4, one launch (start us, length us, event | category | flops | bytes accessed | tf_op | source)
XLA Modules:
  0.0 43.1 jit_solution(10630161533549056014)
XLA Ops:
  0.6 0.1 pad_add_fusion.place
  0.7 1.8 %split.1 = (bf16[17,128,128]{2,1,0:T(8,128)(2,1)S(1)}, bf16[9,128,128]{2,1,0:T(8,128)(2,1)S(1)}, bf16[8,128,128]{2,1,0:T(8,128)(2,1)S(1)}) custom-call(s32[2]{0:T(128)S(1)} %pad_add_fusion.place, f32[1,3,1,25]{3,2,1,0:T(1,128)} %nodes_in.1, bf16[1,32,128,128]{3,2,1,0:T(8,128)(2,1)} %slab.1), custom_call_target="tpu_custom_call" | custom-call | tf_op jit(solution)/shard_map/split/pallas_call | solution.py:301
  2.5 0.0 copy-start
  2.5 0.1 collective-permute-start
  2.6 2.7 %collective-permute-start.2 = (bf16[8,128,128]{2,1,0:T(8,128)(2,1)}, bf16[8,128,128]{2,1,0:T(8,128)(2,1)S(1)}, u32[]{:S(2)}, u32[]{:S(2)}) collective-permute-start(bf16[8,128,128]{2,1,0:T(8,128)(2,1)} %b0.1), channel_id=1, source_target_pairs={{0,2},{1,3},{2,0},{3,1},{4,6},{5,7},{6,4},{7,5},{8,10},{9,11},{10,... | collective-permute-start | bytes 786440 | tf_op jit(solution)/shard_map/ppermute | solution.py:566
  5.3 3.1 %collective-permute-start.1 = (bf16[9,128,128]{2,1,0:T(8,128)(2,1)S(1)}, bf16[9,128,128]{2,1,0:T(8,128)(2,1)S(1)}, u32[]{:S(2)}, u32[]{:S(2)}) collective-permute-start(bf16[9,128,128]{2,1,0:T(8,128)(2,1)S(1)} %get-tuple-element.27.far), channel_id=1, source_target_pairs={{4,8},{8,4},{12,16},{16,12},{20,24},{24,20},{5,9},{9,5},{13,17},{1... | collective-permute-start | bytes 884744 | tf_op jit(solution)/shard_map/ppermute | solution.py:570
  8.4 1.6 %collective-permute-start.4 = (bf16[8,128,128]{2,1,0:T(8,128)(2,1)}, bf16[8,128,128]{2,1,0:T(8,128)(2,1)S(1)}, u32[]{:S(2)}, u32[]{:S(2)}) collective-permute-start(bf16[8,128,128]{2,1,0:T(8,128)(2,1)} %b0.1), channel_id=1, source_target_pairs={{0,1},{1,0},{2,3},{3,2},{4,5},{5,4},{6,7},{7,6},{8,9},{9,8},{10,11... | collective-permute-start | bytes 786440 | tf_op jit(solution)/shard_map/ppermute | solution.py:573
  10.0 3.1 %collective-permute-start.3 = (bf16[8,128,128]{2,1,0:T(8,128)(2,1)S(1)}, bf16[8,128,128]{2,1,0:T(8,128)(2,1)S(1)}, u32[]{:S(2)}, u32[]{:S(2)}) collective-permute-start(bf16[8,128,128]{2,1,0:T(8,128)(2,1)S(1)} %get-tuple-element.28.far_end), channel_id=1, source_target_pairs={{4,8},{8,4},{12,16},{16,12},{20,24},{24,20},{5,9},{9,5},{13,17},{1... | collective-permute-start | bytes 786440 | tf_op jit(solution)/shard_map/ppermute | solution.py:571
  13.1 3.6 %windows.1 = (f32[4,17,40,128]{3,2,1,0:T(8,128)}, f32[4,17,40,128]{3,2,1,0:T(8,128)}) custom-call(s32[2]{0:T(128)S(1)} %pad_add_fusion.place, bf16[17,128,128]{2,1,0:T(8,128)(2,1)S(1)} %get-tuple-element.26.near, bf16[9,128,128]{2,1,0:T(8,128)(2,1)S(1)} %get-tuple-element.27.far, bf16[8,128,128]{2,1,0:T(8,128)(2,1)S(1)} %get-tuple-element.28.far_end, ...), custom_call_target="tpu_custom_call" | custom-call | tf_op jit(solution)/shard_map/windows/pallas_call | solution.py:301
  16.7 1.5 %collective-permute-done.2.b2 = bf16[8,128,128]{2,1,0:T(8,128)(2,1)S(1)} collective-permute-done((bf16[8,128,128]{2,1,0:T(8,128)(2,1)}, bf16[8,128,128]{2,1,0:T(8,128)(2,1)S(1)}, u32[]{:S(2)}, u32[]{:S(2)}) %collective-permute-start.2) | collective-permute-done | bytes 262176 | tf_op jit(solution)/shard_map/ppermute | solution.py:566
  18.2 0.7 %collective-permute-start.5 = (bf16[8,128,128]{2,1,0:T(8,128)(2,1)S(1)}, bf16[8,128,128]{2,1,0:T(8,128)(2,1)S(1)}, u32[]{:S(2)}, u32[]{:S(2)}) collective-permute-start(bf16[8,128,128]{2,1,0:T(8,128)(2,1)S(1)} %collective-permute-done.2.b2), channel_id=1, source_target_pairs={{0,1},{1,0},{2,3},{3,2},{4,5},{5,4},{6,7},{7,6},{8,9},{9,8},{10,11... | collective-permute-start | bytes 786440 | tf_op jit(solution)/shard_map/ppermute | solution.py:577
  18.9 2.5 %first_half.1 = (f32[16,128,128]{2,1,0:T(8,128)S(1)}, f32[3,128,128]{2,1,0:T(8,128)S(1)}, f32[3,128,128]{2,1,0:T(8,128)S(1)}) custom-call(s32[2]{0:T(128)S(1)} %pad_add_fusion.place, bf16[17,128,128]{2,1,0:T(8,128)(2,1)S(1)} %get-tuple-element.26.near, bf16[17,128,128]{2,1,0:T(8,128)(2,1)S(1)} %collective-permute-done.near_halo, ...), custom_call_target="tpu_custom_call" | custom-call | tf_op jit(solution)/shard_map/first_half/pallas_call | solution.py:301
  21.5 0.8 %collective-permute-done.4.b1 = bf16[8,128,128]{2,1,0:T(8,128)(2,1)S(1)} collective-permute-done((bf16[8,128,128]{2,1,0:T(8,128)(2,1)}, bf16[8,128,128]{2,1,0:T(8,128)(2,1)S(1)}, u32[]{:S(2)}, u32[]{:S(2)}) %collective-permute-start.4) | collective-permute-done | bytes 262176 | tf_op jit(solution)/shard_map/ppermute | solution.py:573
  22.3 0.1 collective-permute-done.3.far_halo_end
  22.4 4.4 %second_half.1 = (f32[16,128,128]{2,1,0:T(8,128)S(1)}, bf16[32,128,128]{2,1,0:T(8,128)(2,1)}, f32[3,16,128,128]{3,2,1,0:T(8,128)S(1)}, f32[16,128,128]{2,1,0:T(8,128)S(1)}) custom-call(s32[2]{0:T(128)S(1)} %pad_add_fusion.place, bf16[17,128,128]{2,1,0:T(8,128)(2,1)S(1)} %get-tuple-element.26.near, bf16[9,128,128]{2,1,0:T(8,128)(2,1)S(1)} %get-tuple-element.27.far, ...), custom_call_target="tpu_custom_call" | custom-call | tf_op jit(solution)/shard_map/second_half/pallas_call | solution.py:301
  26.8 0.6 %collective-permute-done.5.b3 = bf16[8,128,128]{2,1,0:T(8,128)(2,1)S(1)} collective-permute-done((bf16[8,128,128]{2,1,0:T(8,128)(2,1)S(1)}, bf16[8,128,128]{2,1,0:T(8,128)(2,1)S(1)}, u32[]{:S(2)}, u32[]{:S(2)}) %collective-permute-start.5) | collective-permute-done | bytes 262176 | tf_op jit(solution)/shard_map/ppermute | solution.py:577
  27.5 0.1 collective-permute-start.6
  27.6 3.1 %collective-permute-start.7 = (bf16[3,128,128]{2,1,0:T(8,128)(2,1)S(1)}, bf16[3,128,128]{2,1,0:T(8,128)(2,1)S(1)}, u32[]{:S(2)}, u32[]{:S(2)}) collective-permute-start(bf16[3,128,128]{2,1,0:T(8,128)(2,1)S(1)} %get-tuple-element.44), channel_id=1, source_target_pairs={{4,8},{8,4},{12,16},{16,12},{20,24},{24,20},{5,9},{9,5},{13,17},{1... | collective-permute-start | bytes 294920 | tf_op jit(solution)/shard_map/ppermute | solution.py:595
  30.7 3.7 %inner.1 = (bf16[32,128,128]{2,1,0:T(8,128)(2,1)}, f32[3,16,128,128]{3,2,1,0:T(8,128)S(1)}, f32[16,128,128]{2,1,0:T(8,128)S(1)}, f32[5,6,8,128]{3,2,1,0:T(8,128)S(1)}) custom-call(s32[2]{0:T(128)S(1)} %pad_add_fusion.place, f32[16,128,128]{2,1,0:T(8,128)S(1)} %get-tuple-element.33.warp_a, ...), custom_call_target="tpu_custom_call", output_to_operand_aliasing={{0}: (9, {})} | custom-call | tf_op jit(solution)/shard_map/inner/pallas_call | solution.py:301
  34.4 0.0 collective-permute-done.7.edge_b
  34.4 2.3 %outer.1 = (f32[3,1,25]{2,1,0:T(1,128)S(1)}, f32[3,1,25]{2,1,0:T(1,128)S(1)}) custom-call(s32[2]{0:T(128)S(1)} %pad_add_fusion.place, bf16[3,128,128]{2,1,0:T(8,128)(2,1)S(1)} %collective-permute-done.6.edge_a, bf16[3,128,128]{2,1,0:T(8,128)(2,1)S(1)} %collective-permute-done.7.edge_b, f32[3,16,128,128]{3,2,1,0:T(8,128)S(1)} %get-tuple-element.39.y_a, ...), custom_call_target="tpu_custom_call" | custom-call | tf_op jit(solution)/shard_map/outer/pallas_call | solution.py:301
  36.8 1.9 %collective-permute-start.8 = (f32[3,1,25]{2,1,0:T(1,128)S(1)}, f32[3,1,25]{2,1,0:T(1,128)S(1)}, u32[]{:S(2)}, u32[]{:S(2)}) collective-permute-start(f32[3,1,25]{2,1,0:T(1,128)S(1)} %get-tuple-element.49), channel_id=1, source_target_pairs={{0,4},{4,8},{8,12},{12,16},{16,20},{20,24},{24,28},{1,5},{5,9},{9,... | collective-permute-start | bytes 908 | tf_op jit(solution)/shard_map/ppermute | solution.py:598
  38.7 3.9 %collective-permute-done.8 = f32[3,1,25]{2,1,0:T(1,128)S(1)} collective-permute-done((f32[3,1,25]{2,1,0:T(1,128)S(1)}, f32[3,1,25]{2,1,0:T(1,128)S(1)}, u32[]{:S(2)}, u32[]{:S(2)}) %collective-permute-start.8) | collective-permute-done | bytes 332 | tf_op jit(solution)/shard_map/ppermute | solution.py:598
  42.6 0.6 %add_bitcast_fusion = f32[1,3,1,25]{3,2,1,0:T(1,128)} fusion(f32[3,1,25]{2,1,0:T(1,128)S(1)} %get-tuple-element.48, f32[3,1,25]{2,1,0:T(1,128)S(1)} %collective-permute-done.8), kind=kLoop, calls=%fused_computation.8 | loop fusion | flops 75 | bytes 900
  (12 shorter events, 0.1 us)
Async XLA Ops:
  2.5 19.9 %copy-start = (bf16[384,256]{1,0:T(8,128)(2,1)S(1)}, bf16[384,256]{1,0:T(8,128)(2,1)}, u32[]{:S(2)}) copy-start(bf16[384,256]{1,0:T(8,128)(2,1)} %constant.32.clone.x_bands) | copy-start | bytes 589828
  2.5 19.9 %copy-start.1 = (bf16[8,128,128]{2,1,0:T(8,128)(2,1)S(1)}, bf16[8,128,128]{2,1,0:T(8,128)(2,1)}, u32[]{:S(2)}) copy-start(bf16[8,128,128]{2,1,0:T(8,128)(2,1)} %b0.1) | copy-start | bytes 786436
  2.5 19.9 %copy-start.2 = (bf16[256,128]{1,0:T(8,128)(2,1)S(1)}, bf16[256,128]{1,0:T(8,128)(2,1)}, u32[]{:S(2)}) copy-start(bf16[256,128]{1,0:T(8,128)(2,1)} %constant.33.clone.y_bands) | copy-start | bytes 196612
  2.5 10.6 %collective-permute-start = (bf16[17,128,128]{2,1,0:T(8,128)(2,1)S(1)}, bf16[17,128,128]{2,1,0:T(8,128)(2,1)S(1)}, u32[]{:S(2)}, u32[]{:S(2)}) collective-permute-start(bf16[17,128,128]{2,1,0:T(8,128)(2,1)S(1)} %get-tuple-element.26.near), channel_id=1, source_target_pairs={{0,4},{4,0},{8,12},{12,8},{16,20},{20,16},{24,28},{28,24},{1,5},{5... | collective-permute-start | bytes 1671176 | tf_op jit(solution)/shard_map/ppermute | solution.py:569
  2.6 15.6 %collective-permute-start.2 = (bf16[8,128,128]{2,1,0:T(8,128)(2,1)}, bf16[8,128,128]{2,1,0:T(8,128)(2,1)S(1)}, u32[]{:S(2)}, u32[]{:S(2)}) collective-permute-start(bf16[8,128,128]{2,1,0:T(8,128)(2,1)} %b0.1), channel_id=1, source_target_pairs={{0,2},{1,3},{2,0},{3,1},{4,6},{5,7},{6,4},{7,5},{8,10},{9,11},{10,... | collective-permute-start | bytes 786440 | tf_op jit(solution)/shard_map/ppermute | solution.py:566
  5.3 13.6 %collective-permute-start.1 = (bf16[9,128,128]{2,1,0:T(8,128)(2,1)S(1)}, bf16[9,128,128]{2,1,0:T(8,128)(2,1)S(1)}, u32[]{:S(2)}, u32[]{:S(2)}) collective-permute-start(bf16[9,128,128]{2,1,0:T(8,128)(2,1)S(1)} %get-tuple-element.27.far), channel_id=1, source_target_pairs={{4,8},{8,4},{12,16},{16,12},{20,24},{24,20},{5,9},{9,5},{13,17},{1... | collective-permute-start | bytes 884744 | tf_op jit(solution)/shard_map/ppermute | solution.py:570
  8.4 13.9 %collective-permute-start.4 = (bf16[8,128,128]{2,1,0:T(8,128)(2,1)}, bf16[8,128,128]{2,1,0:T(8,128)(2,1)S(1)}, u32[]{:S(2)}, u32[]{:S(2)}) collective-permute-start(bf16[8,128,128]{2,1,0:T(8,128)(2,1)} %b0.1), channel_id=1, source_target_pairs={{0,1},{1,0},{2,3},{3,2},{4,5},{5,4},{6,7},{7,6},{8,9},{9,8},{10,11... | collective-permute-start | bytes 786440 | tf_op jit(solution)/shard_map/ppermute | solution.py:573
  10.0 12.3 %collective-permute-start.3 = (bf16[8,128,128]{2,1,0:T(8,128)(2,1)S(1)}, bf16[8,128,128]{2,1,0:T(8,128)(2,1)S(1)}, u32[]{:S(2)}, u32[]{:S(2)}) collective-permute-start(bf16[8,128,128]{2,1,0:T(8,128)(2,1)S(1)} %get-tuple-element.28.far_end), channel_id=1, source_target_pairs={{4,8},{8,4},{12,16},{16,12},{20,24},{24,20},{5,9},{9,5},{13,17},{1... | collective-permute-start | bytes 786440 | tf_op jit(solution)/shard_map/ppermute | solution.py:571
  18.2 9.2 %collective-permute-start.5 = (bf16[8,128,128]{2,1,0:T(8,128)(2,1)S(1)}, bf16[8,128,128]{2,1,0:T(8,128)(2,1)S(1)}, u32[]{:S(2)}, u32[]{:S(2)}) collective-permute-start(bf16[8,128,128]{2,1,0:T(8,128)(2,1)S(1)} %collective-permute-done.2.b2), channel_id=1, source_target_pairs={{0,1},{1,0},{2,3},{3,2},{4,5},{5,4},{6,7},{7,6},{8,9},{9,8},{10,11... | collective-permute-start | bytes 786440 | tf_op jit(solution)/shard_map/ppermute | solution.py:577
  27.5 6.9 %collective-permute-start.6 = (bf16[3,128,128]{2,1,0:T(8,128)(2,1)S(1)}, bf16[3,128,128]{2,1,0:T(8,128)(2,1)S(1)}, u32[]{:S(2)}, u32[]{:S(2)}) collective-permute-start(bf16[3,128,128]{2,1,0:T(8,128)(2,1)S(1)} %broadcast_select_fusion.1), channel_id=1, source_target_pairs={{0,4},{4,0},{8,12},{12,8},{16,20},{20,16},{24,28},{28,24},{1,5},{5... | collective-permute-start | bytes 294920 | tf_op jit(solution)/shard_map/ppermute | solution.py:595
  27.6 6.9 %collective-permute-start.7 = (bf16[3,128,128]{2,1,0:T(8,128)(2,1)S(1)}, bf16[3,128,128]{2,1,0:T(8,128)(2,1)S(1)}, u32[]{:S(2)}, u32[]{:S(2)}) collective-permute-start(bf16[3,128,128]{2,1,0:T(8,128)(2,1)S(1)} %get-tuple-element.44), channel_id=1, source_target_pairs={{4,8},{8,4},{12,16},{16,12},{20,24},{24,20},{5,9},{9,5},{13,17},{1... | collective-permute-start | bytes 294920 | tf_op jit(solution)/shard_map/ppermute | solution.py:595
  30.7 3.8 %copy-start.3 = (bf16[5,128,128]{2,1,0:T(8,128)(2,1)S(1)}, bf16[5,128,128]{2,1,0:T(8,128)(2,1)}, u32[]{:S(2)}) copy-start(bf16[5,128,128]{2,1,0:T(8,128)(2,1)} %constant.34.clone.hats) | copy-start | bytes 491524
  36.8 5.8 %collective-permute-start.8 = (f32[3,1,25]{2,1,0:T(1,128)S(1)}, f32[3,1,25]{2,1,0:T(1,128)S(1)}, u32[]{:S(2)}, u32[]{:S(2)}) collective-permute-start(f32[3,1,25]{2,1,0:T(1,128)S(1)} %get-tuple-element.49), channel_id=1, source_target_pairs={{0,4},{4,8},{8,12},{12,16},{16,20},{20,24},{24,28},{1,5},{5,9},{9,... | collective-permute-start | bytes 908 | tf_op jit(solution)/shard_map/ppermute | solution.py:598

commit v4 on v3

--- a/solution.py
+++ b/solution.py
@@ -58,13 +58,17 @@
 RHS_HATS = rhs_hats()
 
 
+def position():
+    return lax.axis_index("scan"), lax.axis_index("brick") % 2
+
+
 def lane_position(shape, dim):
     v = lax.broadcasted_iota(jnp.int32, shape, dim)
     return ((v % E).astype(jnp.float32) + 0.5) * (1.0 / E)
 
 
-def split_kernel(place, nodes_in, slab, near, far, far_end, nodes, wide, sems):
-    odd = place[1]
+def split_kernel(nodes_in, slab, near, far, far_end, nodes, wide, sems):
+    odd = position()[1]
     parts = ((1 - odd, 0, HALO, near), (odd, 0, FAR, far), (odd, FAR, HALO - FAR, far_end))
     copies = [
         pltpu.make_async_copy(
@@ -220,7 +224,7 @@
 
 
 def window_kernel(
-    place, near, far, far_end, near_halo, offs_in,
+    near, far, far_end, near_halo, offs_in,
     val_out, dif_out, vol, lhs, s_val, s_dif, offs, sem, sems,
 ):
     fetch = pltpu.make_async_copy(offs_in, offs, sem)
@@ -237,7 +241,7 @@
             c.start()
 
     shifted(
-        place[1] == 1, offs, fetch, (near,), (far, far_end), (near_halo,), vol, lhs, s_val, s_dif, done
+        position()[1] == 1, offs, fetch, (near,), (far, far_end), (near_halo,), vol, lhs, s_val, s_dif, done
     )
     for ey in range(ROW):
         for c in copies(ey):
@@ -245,7 +249,7 @@
 
 
 def first_kernel(
-    place, near, near_halo, far_halo, val_in, dif_in, warped, w_base, w_step, val, dif, sems
+    near, near_halo, far_halo, val_in, dif_in, warped, w_base, w_step, val, dif, sems
 ):
     copies = [
         [
@@ -257,7 +261,7 @@
     for pair in copies:
         for c in pair:
             c.start()
-    odd = place[1] == 1
+    odd = position()[1] == 1
     displacements(odd, near, near_halo, far_halo, w_base, w_step)
     for ey, pair in enumerate(copies):
         for c in pair:
@@ -266,11 +270,11 @@
 
 
 def second_kernel(
-    place, near, far, far_end, far_halo, far_halo_end, w_base, w_step,
+    near, far, far_end, far_halo, far_halo_end, w_base, w_step,
     warp_a, b0, b1, x_bands, y_bands, offs_in,
     warped, residual, y, misfit, vol, lhs, s_val, s_dif, offs, sem, rounded, out_sem,
 ):
-    odd = place[1] == 1
+    odd = position()[1] == 1
     fetch = pltpu.make_async_copy(offs_in, offs, sem)
     fetch.start()
     halo = (far_halo, far_halo_end)
@@ -280,13 +284,12 @@
     for ey in range(ROW):
         interpolate(s_val, s_dif, w_base, w_step, jnp.where(odd, HALF, 0), warped, ey)
     filter_half(
-        (0, 1), place, warp_a, warped, (b0, b1), x_bands, y_bands,
+        (0, 1), warp_a, warped, (b0, b1), x_bands, y_bands,
         residual, y, misfit, rounded, out_sem,
     ).wait()
 
 
 VMEM = pl.BlockSpec(memory_space=pltpu.VMEM)
-SMEM = pl.BlockSpec(memory_space=pltpu.SMEM)
 HBM = pl.BlockSpec(memory_space=pltpu.HBM)
 FIELD = jax.ShapeDtypeStruct((3, N, N), jnp.float32)
 HALF_VOLUME = jax.ShapeDtypeStruct((HALF, N, N), jnp.float32)
@@ -296,8 +299,8 @@
 SMALL = jax.ShapeDtypeStruct((3, 1, (ROW + 1) ** 2), jnp.float32)
 
 
-def call(kernel, name, outs, smem, vmem, scratch, mib, hbm=(), hbm_outs=(), alias=None):
-    specs = [SMEM] * len(smem) + [VMEM] * len(vmem)
+def call(kernel, name, outs, vmem, scratch, mib, hbm=(), hbm_outs=(), alias=None):
+    specs = [VMEM] * len(vmem)
     return pl.pallas_call(
         kernel,
         out_shape=outs,
@@ -307,15 +310,14 @@
         scratch_shapes=scratch,
         compiler_params=pltpu.CompilerParams(vmem_limit_bytes=mib * 1024 * 1024),
         name=name,
-    )(*smem, *vmem, *hbm)
-
-
-def split(place, nodes, slab):
+    )(*vmem, *hbm)
+
+
+def split(nodes, slab):
     return call(
         split_kernel,
         "split",
         tuple(jax.ShapeDtypeStruct((n, N, N), jnp.bfloat16) for n in (HALO + 1, FAR + 1, HALO - FAR)),
-        [place],
         [],
         [
             pltpu.VMEM((1, 3, 1, (ROW + 1) ** 2), jnp.float32),
@@ -338,19 +340,19 @@
 EACH_ROW = pltpu.SemaphoreType.DMA((2, ROW))
 
 
-def windows(place, offs, planes):
+def windows(offs, planes):
     out = pltpu.HBM(SAMPLES, jnp.float32)
     scratch = WINDOW_SCRATCH + [EACH_ROW]
     return call(
-        window_kernel, "windows", (out, out), [place], planes, scratch, 20, hbm=[offs], hbm_outs=(0, 1)
-    )
-
-
-def first_half(place, planes, samples):
+        window_kernel, "windows", (out, out), planes, scratch, 20, hbm=[offs], hbm_outs=(0, 1)
+    )
+
+
+def first_half(planes, samples):
     samples = [pltpu.with_memory_space_constraint(x, pltpu.HBM) for x in samples]
     scratch = SAMPLE_SCRATCH + [EACH_ROW]
     outs = (HALF_VOLUME, FIELD, FIELD)
-    return call(first_kernel, "first_half", outs, [place], planes, scratch, 16, hbm=samples)
+    return call(first_kernel, "first_half", outs, planes, scratch, 16, hbm=samples)
 
 
 ROUNDED = [pltpu.VMEM((HALF, N, N), jnp.bfloat16), pltpu.SemaphoreType.DMA]
@@ -360,12 +362,11 @@
     return jnp.asarray(X_BANDS, jnp.bfloat16), jnp.asarray(Y_BANDS, jnp.bfloat16)
 
 
-def second_half(place, offs, planes, warp_a, blocks):
+def second_half(offs, planes, warp_a, blocks):
     return call(
         second_kernel,
         "second_half",
         (HALF_VOLUME, RESIDUAL, FILTERED, HALF_VOLUME),
-        [place],
         [*planes, warp_a, *blocks, *bands()],
         WINDOW_SCRATCH + ROUNDED,
         32,
@@ -393,9 +394,9 @@
 
 
 def filter_half(
-    slots, place, warp_a, warp_b, blocks, x_bands, y_bands, residual, y, misfit, rounded, sem
+    slots, warp_a, warp_b, blocks, x_bands, y_bands, residual, y, misfit, rounded, sem
 ):
-    me, odd = place[0], place[1]
+    me, odd = position()
     depth = blocks[0].shape[0]
     half = (me ^ slots[0]) // 2
 
@@ -474,12 +475,12 @@
 
 
 def inner_kernel(
-    place, warp_a, warp_b, b2, b3, y_a, misfit_a, x_bands, y_bands, residual_in,
+    warp_a, warp_b, b2, b3, y_a, misfit_a, x_bands, y_bands, residual_in,
     residual, y, misfit, sums, rounded, sem,
 ):
-    me, odd = place[0], place[1]
+    me, odd = position()
     out = filter_half(
-        (2, 3), place, warp_a, warp_b, (b2, b3), x_bands, y_bands,
+        (2, 3), warp_a, warp_b, (b2, b3), x_bands, y_bands,
         residual, y, misfit, rounded, sem,
     )
     sums[...] = jnp.zeros_like(sums)
@@ -490,10 +491,10 @@
 
 
 def outer_kernel(
-    place, edge_a, edge_b, y_a, misfit_a, y_b, misfit_b, earlier, x_bands, y_bands, hats,
+    edge_a, edge_b, y_a, misfit_a, y_b, misfit_b, earlier, x_bands, y_bands, hats,
     bottom, top, edges, sums,
 ):
-    me, odd = place[0], place[1]
+    me, odd = position()
     planes = [edge[i] for edge in (edge_a, edge_b) for i in range(RADIUS)]
     filter_into(edges, planes, 0, x_bands, y_bands)
     sums[...] = earlier[...]
@@ -501,13 +502,18 @@
     outer = (edges, [(0, RADIUS), (E - RADIUS, E)])
     pl.when(me < 2)(lambda: add_up(sums, odd, (y_a, y_b), (misfit_a, misfit_b), *outer))
     pl.when(me >= 2)(lambda: add_up(sums, odd, (y_b, y_a), (misfit_b, misfit_a), *outer))
-    out = jnp.zeros((48, N), jnp.float32)
+    pieces = []
     for iy in range(ROW + 1):
         rest = sums[iy].reshape(48, N)
-        for piece in range(3):
-            part = rest.astype(jnp.bfloat16)
-            rest = rest - part.astype(jnp.float32)
-            out = out + jnp.dot(part, hats[iy], preferred_element_type=jnp.float32)
+        three = []
+        for _ in range(3):
+            three.append(rest.astype(jnp.bfloat16))
+            rest = rest - three[-1].astype(jnp.float32)
+        pieces.append(jnp.concatenate(three))
+    out = jnp.dot(
+        jnp.concatenate(pieces, axis=1), hats[...], preferred_element_type=jnp.float32
+    )
+    out = out[:48] + out[48:96] + out[96:]
     out = jnp.sum(out.reshape(6, 8, N), axis=1)
     for k in range(3):
         gain = float(SLOPE[RADIUS + 1] if k == 0 else SMOOTH[RADIUS]) / E
@@ -518,31 +524,29 @@
 SUMS = jax.ShapeDtypeStruct((ROW + 1, 6, 8, N), jnp.float32)
 
 
-def inner(place, halves, blocks, lower, residual):
+def inner(halves, blocks, lower, residual):
     return call(
         inner_kernel,
         "inner",
         (RESIDUAL, FILTERED, HALF_VOLUME, SUMS),
-        [place],
         [*halves, *blocks, *lower, *bands()],
         ROUNDED,
         32,
         hbm=[residual],
         hbm_outs=(0,),
-        alias={9: 0},
-    )
-
-
-def assemble(place, edges, halves, earlier):
+        alias={8: 0},
+    )
+
+
+def assemble(edges, halves, earlier):
     return call(
         outer_kernel,
         "outer",
         (SMALL, SMALL),
-        [place],
         [
             *edges, *halves, earlier,
             *bands(),
-            jnp.asarray(RHS_HATS, jnp.bfloat16),
+            jnp.asarray(RHS_HATS.reshape(-1, N), jnp.bfloat16),
         ],
         [
             pltpu.VMEM((3, 2 * RADIUS, N, N), jnp.float32),
@@ -556,7 +560,6 @@
     bricks = lax.axis_size("brick")
     me = lax.axis_index("scan")
     odd = lax.axis_index("brick") % 2
-    place = jnp.stack([me, odd]).astype(jnp.int32)
     up = [(i, i + 1) for i in range(bricks - 1)]
     inside = [r for i in range(0, bricks - 1, 2) for r in ((i, i + 1), (i + 1, i))]
     outside = [r for i in range(1, bricks - 1, 2) for r in ((i, i + 1), (i + 1, i))]
@@ -564,7 +567,7 @@
 
     slab = pltpu.with_memory_space_constraint(deformed, pltpu.HBM)
     across = lax.ppermute(tomogram, "scan", [(0, 2), (1, 3), (2, 0), (3, 1)])
-    near, far, far_end = split(place, pltpu.with_memory_space_constraint(subvoxel, pltpu.HBM), slab)
+    near, far, far_end = split(pltpu.with_memory_space_constraint(subvoxel, pltpu.HBM), slab)
     offs = pltpu.with_memory_space_constraint(offsets.reshape(3, 1, -1), pltpu.HBM)
     halo_a = lax.ppermute(near, "brick", inside)
     halo_b = lax.ppermute(far, "brick", outside)
@@ -572,13 +575,13 @@
     late = tomogram
     beside = lax.ppermute(late, "scan", pairs)
     slab_parts = (near, far, far_end)
-    samples = windows(place, offs, (*slab_parts, halo_a))
+    samples = windows(offs, (*slab_parts, halo_a))
     across, samples = lax.optimization_barrier((across, samples))
     relayed = lax.ppermute(across, "scan", pairs)
     blocks = (tomogram, beside, across, relayed)
-    warp_a, *field = first_half(place, (near, halo_a, halo_b), samples)
+    warp_a, *field = first_half((near, halo_a, halo_b), samples)
     warp_b, residual, *lower = second_half(
-        place, offs, (*slab_parts, halo_b, halo_c, *field), warp_a, blocks[:2]
+        offs, (*slab_parts, halo_b, halo_c, *field), warp_a, blocks[:2]
     )
     halves = (warp_a, warp_b)
 
@@ -593,8 +596,8 @@
         (jnp.where(odd == 1, head, tail), jnp.where(odd == 1, tail, head), lower[0])
     )
     edges = (lax.ppermute(send_a, "brick", inside), lax.ppermute(send_b, "brick", outside))
-    residual, y, misfit, sums = inner(place, halves, blocks[2:], lower, residual)
-    bottom, top = assemble(place, edges, (*lower, y, misfit), sums)
+    residual, y, misfit, sums = inner(halves, blocks[2:], lower, residual)
+    bottom, top = assemble(edges, (*lower, y, misfit), sums)
     node_rhs = bottom + lax.ppermute(top, "brick", up)
     return residual[None], node_rhs[None]
 

time: 43.4 us -> 42 us (0.968)
  Pallas kernels: 18.4 us -> 14.9 us
  waiting for transfers between devices: 6.89 us -> 9.06 us
    pallas_call x6, Pallas kernels: 18.4 us -> 14.9 us  [call(): pl.pallas_call(kernel, out_shape=outs, in_specs=specs + [HBM] * len(hbm),...]
    ppermute x1, waiting for transfers between devices: 0.62 us -> 1.22 us  [body(): relayed = lax.ppermute(across, 'scan', pairs)]
    ppermute x1, waiting for transfers between devices: 0.82 us -> 1.37 us  [body(): beside = lax.ppermute(late, 'scan', pairs)]
    ppermute x1, waiting for transfers between devices: 1.46 us -> 2.01 us  [body(): across = lax.ppermute(tomogram, 'scan', [(0, 2), (1, 3), (2, 0), (3, 1)])]
    ppermute x1, waiting for transfers between devices: 0.01 us -> 0.49 us  [body(): lax.ppermute(send_b, 'brick', outside)]
  transfers between devices with their start and end apart: 9 -> 9, of which waited for: 5 -> 6; matrix products, arithmetic and copies ran while one was open for 0% -> 0% of each run, Pallas kernels for 33% -> 29%
where the time goes in v4:
time: 42 us; the launch traced here: 41.7 us
  starting transfers between devices  16.3 us (39%)
  Pallas kernels  14.9 us (35%)
  waiting for transfers between devices  9.06 us (22%)
  between operations  0.79 us (2%)
  other arithmetic  0.62 us (1%)
    pallas_call x6, Pallas kernels, call(): pl.pallas_call(kernel, out_shape=outs, in_specs=specs + [HBM] * len(hbm),...  14.9 us
    ppermute x1, waiting for transfers between devices, body(): node_rhs = bottom + lax.ppermute(top, 'brick', up)  3.87 us
    ppermute x1, starting transfers between devices, body(): halo_b = lax.ppermute(far, 'brick', outside)  3.1 us
    ppermute x1, starting transfers between devices, body(): lax.ppermute(send_b, 'brick', outside)  3.07 us
    ppermute x1, starting transfers between devices, body(): halo_c = lax.ppermute(far_end, 'brick', outside)  3.06 us
    ppermute x1, starting transfers between devices, body(): across = lax.ppermute(tomogram, 'scan', [(0, 2), (1, 3), (2, 0), (3, 1)])  2.65 us
    ppermute x1, waiting for transfers between devices, body(): across = lax.ppermute(tomogram, 'scan', [(0, 2), (1, 3), (2, 0), (3, 1)])  2.01 us
    ppermute x1, starting transfers between devices, body(): node_rhs = bottom + lax.ppermute(top, 'brick', up)  1.92 us
  transfers between devices with their start and end apart: 9, of which 6 were waited for; matrix products, arithmetic and copies ran while one was open for 0% of the time, Pallas kernels for 29%

profile of v4, /device:TPU:4, one launch (start us, length us, event | category | flops | bytes accessed | tf_op | source)
XLA Modules:
  0.0 41.7 jit_solution(2964403013263910121)
XLA Ops:
  0.6 1.3 %split.1 = (bf16[17,128,128]{2,1,0:T(8,128)(2,1)S(1)}, bf16[9,128,128]{2,1,0:T(8,128)(2,1)S(1)}, bf16[8,128,128]{2,1,0:T(8,128)(2,1)S(1)}) custom-call(f32[1,3,1,25]{3,2,1,0:T(1,128)} %nodes_in.1, bf16[1,32,128,128]{3,2,1,0:T(8,128)(2,1)} %slab.1), custom_call_target="tpu_custom_call" | custom-call | tf_op jit(solution)/shard_map/split/pallas_call | solution.py:304
  1.9 0.0 copy-start
  1.9 0.0 copy-start.2
  1.9 0.1 collective-permute-start
  2.0 2.7 %collective-permute-start.2 = (bf16[8,128,128]{2,1,0:T(8,128)(2,1)}, bf16[8,128,128]{2,1,0:T(8,128)(2,1)S(1)}, u32[]{:S(2)}, u32[]{:S(2)}) collective-permute-start(bf16[8,128,128]{2,1,0:T(8,128)(2,1)} %b0.1), channel_id=1, source_target_pairs={{0,2},{1,3},{2,0},{3,1},{4,6},{5,7},{6,4},{7,5},{8,10},{9,11},{10,... | collective-permute-start | bytes 786440 | tf_op jit(solution)/shard_map/ppermute | solution.py:569
  4.7 3.1 %collective-permute-start.1 = (bf16[9,128,128]{2,1,0:T(8,128)(2,1)S(1)}, bf16[9,128,128]{2,1,0:T(8,128)(2,1)S(1)}, u32[]{:S(2)}, u32[]{:S(2)}) collective-permute-start(bf16[9,128,128]{2,1,0:T(8,128)(2,1)S(1)} %get-tuple-element.27.far), channel_id=1, source_target_pairs={{4,8},{8,4},{12,16},{16,12},{20,24},{24,20},{5,9},{9,5},{13,17},{1... | collective-permute-start | bytes 884744 | tf_op jit(solution)/shard_map/ppermute | solution.py:573
  7.8 1.6 %collective-permute-start.4 = (bf16[8,128,128]{2,1,0:T(8,128)(2,1)}, bf16[8,128,128]{2,1,0:T(8,128)(2,1)S(1)}, u32[]{:S(2)}, u32[]{:S(2)}) collective-permute-start(bf16[8,128,128]{2,1,0:T(8,128)(2,1)} %b0.1), channel_id=1, source_target_pairs={{0,1},{1,0},{2,3},{3,2},{4,5},{5,4},{6,7},{7,6},{8,9},{9,8},{10,11... | collective-permute-start | bytes 786440 | tf_op jit(solution)/shard_map/ppermute | solution.py:576
  9.4 3.1 %collective-permute-start.3 = (bf16[8,128,128]{2,1,0:T(8,128)(2,1)S(1)}, bf16[8,128,128]{2,1,0:T(8,128)(2,1)S(1)}, u32[]{:S(2)}, u32[]{:S(2)}) collective-permute-start(bf16[8,128,128]{2,1,0:T(8,128)(2,1)S(1)} %get-tuple-element.28.far_end), channel_id=1, source_target_pairs={{4,8},{8,4},{12,16},{16,12},{20,24},{24,20},{5,9},{9,5},{13,17},{1... | collective-permute-start | bytes 786440 | tf_op jit(solution)/shard_map/ppermute | solution.py:574
  12.5 3.1 %windows.1 = (f32[4,17,40,128]{3,2,1,0:T(8,128)}, f32[4,17,40,128]{3,2,1,0:T(8,128)}) custom-call(bf16[17,128,128]{2,1,0:T(8,128)(2,1)S(1)} %get-tuple-element.26.near, bf16[9,128,128]{2,1,0:T(8,128)(2,1)S(1)} %get-tuple-element.27.far, bf16[8,128,128]{2,1,0:T(8,128)(2,1)S(1)} %get-tuple-element.28.far_end, ...), custom_call_target="tpu_custom_call" | custom-call | tf_op jit(solution)/shard_map/windows/pallas_call | solution.py:304
  15.6 2.0 %collective-permute-done.2.b2 = bf16[8,128,128]{2,1,0:T(8,128)(2,1)S(1)} collective-permute-done((bf16[8,128,128]{2,1,0:T(8,128)(2,1)}, bf16[8,128,128]{2,1,0:T(8,128)(2,1)S(1)}, u32[]{:S(2)}, u32[]{:S(2)}) %collective-permute-start.2) | collective-permute-done | bytes 262176 | tf_op jit(solution)/shard_map/ppermute | solution.py:569
  17.6 0.7 %collective-permute-start.5 = (bf16[8,128,128]{2,1,0:T(8,128)(2,1)S(1)}, bf16[8,128,128]{2,1,0:T(8,128)(2,1)S(1)}, u32[]{:S(2)}, u32[]{:S(2)}) collective-permute-start(bf16[8,128,128]{2,1,0:T(8,128)(2,1)S(1)} %collective-permute-done.2.b2), channel_id=1, source_target_pairs={{0,1},{1,0},{2,3},{3,2},{4,5},{5,4},{6,7},{7,6},{8,9},{9,8},{10,11... | collective-permute-start | bytes 786440 | tf_op jit(solution)/shard_map/ppermute | solution.py:580
  18.3 2.0 %first_half.1 = (f32[16,128,128]{2,1,0:T(8,128)S(1)}, f32[3,128,128]{2,1,0:T(8,128)S(1)}, f32[3,128,128]{2,1,0:T(8,128)S(1)}) custom-call(bf16[17,128,128]{2,1,0:T(8,128)(2,1)S(1)} %get-tuple-element.26.near, bf16[17,128,128]{2,1,0:T(8,128)(2,1)S(1)} %collective-permute-done.near_halo, bf16[9,128,128]{2,1,0:T(8,128)(2,1)S(1)} %collective-permute-done.1.far_halo, ...), custom_call_target="tpu_custom_call" | custom-call | tf_op jit(solution)/shard_map/first_half/pallas_call | solution.py:304
  20.3 1.4 %collective-permute-done.4.b1 = bf16[8,128,128]{2,1,0:T(8,128)(2,1)S(1)} collective-permute-done((bf16[8,128,128]{2,1,0:T(8,128)(2,1)}, bf16[8,128,128]{2,1,0:T(8,128)(2,1)S(1)}, u32[]{:S(2)}, u32[]{:S(2)}) %collective-permute-start.4) | collective-permute-done | bytes 262176 | tf_op jit(solution)/shard_map/ppermute | solution.py:576
  21.7 0.1 collective-permute-done.3.far_halo_end
  21.8 3.8 %second_half.1 = (f32[16,128,128]{2,1,0:T(8,128)S(1)}, bf16[32,128,128]{2,1,0:T(8,128)(2,1)}, f32[3,16,128,128]{3,2,1,0:T(8,128)S(1)}, f32[16,128,128]{2,1,0:T(8,128)S(1)}) custom-call(bf16[17,128,128]{2,1,0:T(8,128)(2,1)S(1)} %get-tuple-element.26.near, bf16[9,128,128]{2,1,0:T(8,128)(2,1)S(1)} %get-tuple-element.27.far, ...), custom_call_target="tpu_custom_call" | custom-call | tf_op jit(solution)/shard_map/second_half/pallas_call | solution.py:304
  25.6 1.2 %collective-permute-done.5.b3 = bf16[8,128,128]{2,1,0:T(8,128)(2,1)S(1)} collective-permute-done((bf16[8,128,128]{2,1,0:T(8,128)(2,1)S(1)}, bf16[8,128,128]{2,1,0:T(8,128)(2,1)S(1)}, u32[]{:S(2)}, u32[]{:S(2)}) %collective-permute-start.5) | collective-permute-done | bytes 262176 | tf_op jit(solution)/shard_map/ppermute | solution.py:580
  26.9 0.1 collective-permute-start.6
  27.0 3.1 %collective-permute-start.7 = (bf16[3,128,128]{2,1,0:T(8,128)(2,1)S(1)}, bf16[3,128,128]{2,1,0:T(8,128)(2,1)S(1)}, u32[]{:S(2)}, u32[]{:S(2)}) collective-permute-start(bf16[3,128,128]{2,1,0:T(8,128)(2,1)S(1)} %get-tuple-element.44), channel_id=1, source_target_pairs={{4,8},{8,4},{12,16},{16,12},{20,24},{24,20},{5,9},{9,5},{13,17},{1... | collective-permute-start | bytes 294920 | tf_op jit(solution)/shard_map/ppermute | solution.py:598
  30.0 3.2 %inner.1 = (bf16[32,128,128]{2,1,0:T(8,128)(2,1)}, f32[3,16,128,128]{3,2,1,0:T(8,128)S(1)}, f32[16,128,128]{2,1,0:T(8,128)S(1)}, f32[5,6,8,128]{3,2,1,0:T(8,128)S(1)}) custom-call(f32[16,128,128]{2,1,0:T(8,128)S(1)} %get-tuple-element.33.warp_a, f32[16,128,128]{2,1,0:T(8,128)S(1)} %get-tuple-element.36.warp_b, ...), custom_call_target="tpu_custom_call", output_to_operand_aliasing={{0}: (8, {})} | custom-call | tf_op jit(solution)/shard_map/inner/pallas_call | solution.py:304
  33.3 0.5 %collective-permute-done.7.edge_b = bf16[3,128,128]{2,1,0:T(8,128)(2,1)S(1)} collective-permute-done((bf16[3,128,128]{2,1,0:T(8,128)(2,1)S(1)}, bf16[3,128,128]{2,1,0:T(8,128)(2,1)S(1)}, u32[]{:S(2)}, u32[]{:S(2)}) %collective-permute-start.7) | collective-permute-done | bytes 98336 | tf_op jit(solution)/shard_map/ppermute | solution.py:598
  33.8 1.5 %outer.1 = (f32[3,1,25]{2,1,0:T(1,128)S(1)}, f32[3,1,25]{2,1,0:T(1,128)S(1)}) custom-call(bf16[3,128,128]{2,1,0:T(8,128)(2,1)S(1)} %collective-permute-done.6.edge_a, bf16[3,128,128]{2,1,0:T(8,128)(2,1)S(1)} %collective-permute-done.7.edge_b, f32[3,16,128,128]{3,2,1,0:T(8,128)S(1)} %get-tuple-element.39.y_a, f32[16,128,128]{2,1,0:T(8,128)S(1)} %get-tuple-element.40.misfit_a, ...), custom_call_target="tpu_custom_call" | custom-call | tf_op jit(solution)/shard_map/outer/pallas_call | solution.py:304
  35.3 1.9 %collective-permute-start.8 = (f32[3,1,25]{2,1,0:T(1,128)S(1)}, f32[3,1,25]{2,1,0:T(1,128)S(1)}, u32[]{:S(2)}, u32[]{:S(2)}) collective-permute-start(f32[3,1,25]{2,1,0:T(1,128)S(1)} %get-tuple-element.49), channel_id=1, source_target_pairs={{0,4},{4,8},{8,12},{12,16},{16,20},{20,24},{24,28},{1,5},{5,9},{9,... | collective-permute-start | bytes 908 | tf_op jit(solution)/shard_map/ppermute | solution.py:601
  37.3 3.9 %collective-permute-done.8 = f32[3,1,25]{2,1,0:T(1,128)S(1)} collective-permute-done((f32[3,1,25]{2,1,0:T(1,128)S(1)}, f32[3,1,25]{2,1,0:T(1,128)S(1)}, u32[]{:S(2)}, u32[]{:S(2)}) %collective-permute-start.8) | collective-permute-done | bytes 332 | tf_op jit(solution)/shard_map/ppermute | solution.py:601
  41.1 0.6 %add_bitcast_fusion = f32[1,3,1,25]{3,2,1,0:T(1,128)} fusion(f32[3,1,25]{2,1,0:T(1,128)S(1)} %get-tuple-element.48, f32[3,1,25]{2,1,0:T(1,128)S(1)} %collective-permute-done.8), kind=kLoop, calls=%fused_computation.8 | loop fusion | flops 75 | bytes 900
  (11 shorter events, 0.1 us)
Async XLA Ops:
  1.9 19.9 %copy-start = (bf16[384,256]{1,0:T(8,128)(2,1)S(1)}, bf16[384,256]{1,0:T(8,128)(2,1)}, u32[]{:S(2)}) copy-start(bf16[384,256]{1,0:T(8,128)(2,1)} %constant.32.clone.x_bands) | copy-start | bytes 589828
  1.9 19.9 %copy-start.1 = (bf16[8,128,128]{2,1,0:T(8,128)(2,1)S(1)}, bf16[8,128,128]{2,1,0:T(8,128)(2,1)}, u32[]{:S(2)}) copy-start(bf16[8,128,128]{2,1,0:T(8,128)(2,1)} %b0.1) | copy-start | bytes 786436
  1.9 19.9 %copy-start.2 = (bf16[256,128]{1,0:T(8,128)(2,1)S(1)}, bf16[256,128]{1,0:T(8,128)(2,1)}, u32[]{:S(2)}) copy-start(bf16[256,128]{1,0:T(8,128)(2,1)} %constant.33.clone.y_bands) | copy-start | bytes 196612
  1.9 10.6 %collective-permute-start = (bf16[17,128,128]{2,1,0:T(8,128)(2,1)S(1)}, bf16[17,128,128]{2,1,0:T(8,128)(2,1)S(1)}, u32[]{:S(2)}, u32[]{:S(2)}) collective-permute-start(bf16[17,128,128]{2,1,0:T(8,128)(2,1)S(1)} %get-tuple-element.26.near), channel_id=1, source_target_pairs={{0,4},{4,0},{8,12},{12,8},{16,20},{20,16},{24,28},{28,24},{1,5},{5... | collective-permute-start | bytes 1671176 | tf_op jit(solution)/shard_map/ppermute | solution.py:572
  2.0 15.6 %collective-permute-start.2 = (bf16[8,128,128]{2,1,0:T(8,128)(2,1)}, bf16[8,128,128]{2,1,0:T(8,128)(2,1)S(1)}, u32[]{:S(2)}, u32[]{:S(2)}) collective-permute-start(bf16[8,128,128]{2,1,0:T(8,128)(2,1)} %b0.1), channel_id=1, source_target_pairs={{0,2},{1,3},{2,0},{3,1},{4,6},{5,7},{6,4},{7,5},{8,10},{9,11},{10,... | collective-permute-start | bytes 786440 | tf_op jit(solution)/shard_map/ppermute | solution.py:569
  4.7 13.6 %collective-permute-start.1 = (bf16[9,128,128]{2,1,0:T(8,128)(2,1)S(1)}, bf16[9,128,128]{2,1,0:T(8,128)(2,1)S(1)}, u32[]{:S(2)}, u32[]{:S(2)}) collective-permute-start(bf16[9,128,128]{2,1,0:T(8,128)(2,1)S(1)} %get-tuple-element.27.far), channel_id=1, source_target_pairs={{4,8},{8,4},{12,16},{16,12},{20,24},{24,20},{5,9},{9,5},{13,17},{1... | collective-permute-start | bytes 884744 | tf_op jit(solution)/shard_map/ppermute | solution.py:573
  7.8 13.9 %collective-permute-start.4 = (bf16[8,128,128]{2,1,0:T(8,128)(2,1)}, bf16[8,128,128]{2,1,0:T(8,128)(2,1)S(1)}, u32[]{:S(2)}, u32[]{:S(2)}) collective-permute-start(bf16[8,128,128]{2,1,0:T(8,128)(2,1)} %b0.1), channel_id=1, source_target_pairs={{0,1},{1,0},{2,3},{3,2},{4,5},{5,4},{6,7},{7,6},{8,9},{9,8},{10,11... | collective-permute-start | bytes 786440 | tf_op jit(solution)/shard_map/ppermute | solution.py:576
  9.4 12.3 %collective-permute-start.3 = (bf16[8,128,128]{2,1,0:T(8,128)(2,1)S(1)}, bf16[8,128,128]{2,1,0:T(8,128)(2,1)S(1)}, u32[]{:S(2)}, u32[]{:S(2)}) collective-permute-start(bf16[8,128,128]{2,1,0:T(8,128)(2,1)S(1)} %get-tuple-element.28.far_end), channel_id=1, source_target_pairs={{4,8},{8,4},{12,16},{16,12},{20,24},{24,20},{5,9},{9,5},{13,17},{1... | collective-permute-start | bytes 786440 | tf_op jit(solution)/shard_map/ppermute | solution.py:574
  17.6 9.2 %collective-permute-start.5 = (bf16[8,128,128]{2,1,0:T(8,128)(2,1)S(1)}, bf16[8,128,128]{2,1,0:T(8,128)(2,1)S(1)}, u32[]{:S(2)}, u32[]{:S(2)}) collective-permute-start(bf16[8,128,128]{2,1,0:T(8,128)(2,1)S(1)} %collective-permute-done.2.b2), channel_id=1, source_target_pairs={{0,1},{1,0},{2,3},{3,2},{4,5},{5,4},{6,7},{7,6},{8,9},{9,8},{10,11... | collective-permute-start | bytes 786440 | tf_op jit(solution)/shard_map/ppermute | solution.py:580
  26.9 6.4 %collective-permute-start.6 = (bf16[3,128,128]{2,1,0:T(8,128)(2,1)S(1)}, bf16[3,128,128]{2,1,0:T(8,128)(2,1)S(1)}, u32[]{:S(2)}, u32[]{:S(2)}) collective-permute-start(bf16[3,128,128]{2,1,0:T(8,128)(2,1)S(1)} %broadcast_select_fusion.1), channel_id=1, source_target_pairs={{0,4},{4,0},{8,12},{12,8},{16,20},{20,16},{24,28},{28,24},{1,5},{5... | collective-permute-start | bytes 294920 | tf_op jit(solution)/shard_map/ppermute | solution.py:598
  27.0 6.8 %collective-permute-start.7 = (bf16[3,128,128]{2,1,0:T(8,128)(2,1)S(1)}, bf16[3,128,128]{2,1,0:T(8,128)(2,1)S(1)}, u32[]{:S(2)}, u32[]{:S(2)}) collective-permute-start(bf16[3,128,128]{2,1,0:T(8,128)(2,1)S(1)} %get-tuple-element.44), channel_id=1, source_target_pairs={{4,8},{8,4},{12,16},{16,12},{20,24},{24,20},{5,9},{9,5},{13,17},{1... | collective-permute-start | bytes 294920 | tf_op jit(solution)/shard_map/ppermute | solution.py:598
  30.0 3.8 %copy-start.3 = (bf16[640,128]{1,0:T(8,128)(2,1)S(1)}, bf16[640,128]{1,0:T(8,128)(2,1)}, u32[]{:S(2)}) copy-start(bf16[640,128]{1,0:T(8,128)(2,1)} %constant.34.clone.hats) | copy-start | bytes 491524
  35.3 5.8 %collective-permute-start.8 = (f32[3,1,25]{2,1,0:T(1,128)S(1)}, f32[3,1,25]{2,1,0:T(1,128)S(1)}, u32[]{:S(2)}, u32[]{:S(2)}) collective-permute-start(f32[3,1,25]{2,1,0:T(1,128)S(1)} %get-tuple-element.49), channel_id=1, source_target_pairs={{0,4},{4,8},{8,12},{12,16},{16,20},{20,24},{24,28},{1,5},{5,9},{9,... | collective-permute-start | bytes 908 | tf_op jit(solution)/shard_map/ppermute | solution.py:601

commit v5 on v4

--- a/solution.py
+++ b/solution.py
@@ -355,6 +355,7 @@
     return call(first_kernel, "first_half", outs, planes, scratch, 16, hbm=samples)
 
 
+EDGES = pltpu.VMEM((3, RADIUS + 1, N, N), jnp.float32)
 ROUNDED = [pltpu.VMEM((HALF, N, N), jnp.bfloat16), pltpu.SemaphoreType.DMA]
 
 
@@ -418,20 +419,18 @@
     return out
 
 
-def add_up(sums, odd, y, misfit, edges, ranges):
+def add_up(sums, y, misfit, edges, begin, end):
     smooth = [float(SMOOTH[RADIUS + t] / SMOOTH[RADIUS]) for t in range(RADIUS + 1)]
     slope = [float(SLOPE[RADIUS + t] / SLOPE[RADIUS + 1]) for t in range(RADIUS + 1)]
-    below = RADIUS * (1 - odd)
-    above = RADIUS * odd
 
     def plane(k, z, rows):
         if z < 0:
-            return edges[k, below + RADIUS + z, rows]
+            return edges[k, RADIUS + z, rows]
         if z >= E:
-            return edges[k, above + z - E, rows]
+            return edges[k, z - E, rows]
         return y[z // HALF][k, z % HALF, rows]
 
-    def planes_of(rows, begin, end):
+    def planes_of(rows):
         window = [[plane(k, begin + t, rows) for t in range(-RADIUS, RADIUS)] for k in range(3)]
         zero = jnp.zeros((8, N), jnp.float32)
         plain = [zero] * 3
@@ -459,13 +458,11 @@
     def rows_of(r, carry):
         rows = pl.ds(pl.multiple_of(r * 8, 8), 8)
         ey = r // (E // 8)
-        parts = [planes_of(rows, begin, end) for begin, end in ranges]
+        plains, uppers = planes_of(rows)
         row = lax.broadcasted_iota(jnp.int32, (8, N), 0) + (r % (E // 8)) * 8
         py = (row.astype(jnp.float32) + 0.5) * (1.0 / E)
         for k in range(3):
-            plain = sum(p[0][k] for p in parts[1:]) + parts[0][0][k]
-            upper = sum(p[1][k] for p in parts[1:]) + parts[0][1][k]
-            for iz, part in enumerate((plain - upper, upper)):
+            for iz, part in enumerate((plains[k] - uppers[k], uppers[k])):
                 right = part * py
                 sums[ey, iz * 3 + k] += part - right
                 sums[ey + 1, iz * 3 + k] += right
@@ -474,34 +471,48 @@
     lax.fori_loop(0, N // 8, rows_of, 0)
 
 
+def in_each_case(add, low, high, near_end):
+    me, odd = position()
+    for first_low in (True, False):
+        for start in (True, False):
+            parts = (low, high) if first_low else (high, low)
+            case = ((me < 2) == first_low) & ((odd == 1) == (start == near_end))
+            inner = (0, E - RADIUS) if start else (RADIUS, E)
+            outer = (0, RADIUS) if start else (E - RADIUS, E)
+            pl.when(case)(
+                lambda parts=parts, planes=inner if near_end else outer: add(*zip(*parts), *planes)
+            )
+
+
 def inner_kernel(
-    warp_a, warp_b, b2, b3, y_a, misfit_a, x_bands, y_bands, residual_in,
-    residual, y, misfit, sums, rounded, sem,
+    warp_a, warp_b, b2, b3, edge, y_a, misfit_a, x_bands, y_bands, residual_in,
+    residual, y, misfit, sums, rounded, sem, edges,
 ):
-    me, odd = position()
     out = filter_half(
         (2, 3), warp_a, warp_b, (b2, b3), x_bands, y_bands,
         residual, y, misfit, rounded, sem,
     )
     sums[...] = jnp.zeros_like(sums)
-    inner = (None, [(RADIUS, E - RADIUS)])
-    pl.when(me < 2)(lambda: add_up(sums, odd, (y_a, y), (misfit_a, misfit), *inner))
-    pl.when(me >= 2)(lambda: add_up(sums, odd, (y, y_a), (misfit, misfit_a), *inner))
+    planes = [edge[i] for i in (0, 1, 2, 2)]
+    filter_into(edges, planes, 0, x_bands, y_bands)
+    in_each_case(
+        lambda ys, misfits, begin, end: add_up(sums, ys, misfits, edges, begin, end),
+        (y_a, misfit_a), (y, misfit), True,
+    )
     out.wait()
 
 
 def outer_kernel(
-    edge_a, edge_b, y_a, misfit_a, y_b, misfit_b, earlier, x_bands, y_bands, hats,
+    edge, y_a, misfit_a, y_b, misfit_b, earlier, x_bands, y_bands, hats,
     bottom, top, edges, sums,
 ):
-    me, odd = position()
-    planes = [edge[i] for edge in (edge_a, edge_b) for i in range(RADIUS)]
+    planes = [edge[i] for i in (0, 1, 2, 2)]
     filter_into(edges, planes, 0, x_bands, y_bands)
     sums[...] = earlier[...]
-
-    outer = (edges, [(0, RADIUS), (E - RADIUS, E)])
-    pl.when(me < 2)(lambda: add_up(sums, odd, (y_a, y_b), (misfit_a, misfit_b), *outer))
-    pl.when(me >= 2)(lambda: add_up(sums, odd, (y_b, y_a), (misfit_b, misfit_a), *outer))
+    in_each_case(
+        lambda ys, misfits, begin, end: add_up(sums, ys, misfits, edges, begin, end),
+        (y_a, misfit_a), (y_b, misfit_b), False,
+    )
     pieces = []
     for iy in range(ROW + 1):
         rest = sums[iy].reshape(48, N)
@@ -524,32 +535,32 @@
 SUMS = jax.ShapeDtypeStruct((ROW + 1, 6, 8, N), jnp.float32)
 
 
-def inner(halves, blocks, lower, residual):
+def inner(halves, blocks, edge, lower, residual):
     return call(
         inner_kernel,
         "inner",
         (RESIDUAL, FILTERED, HALF_VOLUME, SUMS),
-        [*halves, *blocks, *lower, *bands()],
-        ROUNDED,
+        [*halves, *blocks, edge, *lower, *bands()],
+        ROUNDED + [EDGES],
         32,
         hbm=[residual],
         hbm_outs=(0,),
-        alias={8: 0},
-    )
-
-
-def assemble(edges, halves, earlier):
+        alias={9: 0},
+    )
+
+
+def assemble(edge, halves, earlier):
     return call(
         outer_kernel,
         "outer",
         (SMALL, SMALL),
         [
-            *edges, *halves, earlier,
+            edge, *halves, earlier,
             *bands(),
             jnp.asarray(RHS_HATS.reshape(-1, N), jnp.bfloat16),
         ],
         [
-            pltpu.VMEM((3, 2 * RADIUS, N, N), jnp.float32),
+            EDGES,
             pltpu.VMEM(SUMS.shape, jnp.float32),
         ],
         24,
@@ -595,9 +606,10 @@
     send_a, send_b, lower[0] = lax.optimization_barrier(
         (jnp.where(odd == 1, head, tail), jnp.where(odd == 1, tail, head), lower[0])
     )
-    edges = (lax.ppermute(send_a, "brick", inside), lax.ppermute(send_b, "brick", outside))
-    residual, y, misfit, sums = inner(halves, blocks[2:], lower, residual)
-    bottom, top = assemble(edges, (*lower, y, misfit), sums)
+    edge_a = lax.ppermute(send_a, "brick", inside)
+    edge_b = lax.ppermute(send_b, "brick", outside)
+    residual, y, misfit, sums = inner(halves, blocks[2:], edge_a, lower, residual)
+    bottom, top = assemble(edge_b, (*lower, y, misfit), sums)
     node_rhs = bottom + lax.ppermute(top, "brick", up)
     return residual[None], node_rhs[None]
 

time: 42 us -> 41.6 us (level)
  waiting for transfers between devices: 9.06 us -> 8.6 us
  transfers between devices with their start and end apart: 9 -> 9, of which waited for: 6 -> 6; matrix products, arithmetic and copies ran while one was open for 0% -> 0% of each run, Pallas kernels for 29% -> 30%
where the time goes in v5:
time: 41.6 us; the launch traced here: 41.4 us
  starting transfers between devices  16.3 us (39%)
  Pallas kernels  15 us (36%)
  waiting for transfers between devices  8.6 us (21%)
  between operations  0.79 us (2%)
  other arithmetic  0.62 us (1%)
    pallas_call x6, Pallas kernels, call(): pl.pallas_call(kernel, out_shape=outs, in_specs=specs + [HBM] * len(hbm),...  15 us
    ppermute x1, waiting for transfers between devices, body(): node_rhs = bottom + lax.ppermute(top, 'brick', up)  3.87 us
    ppermute x1, starting transfers between devices, body(): halo_b = lax.ppermute(far, 'brick', outside)  3.1 us
    ppermute x1, starting transfers between devices, body(): edge_b = lax.ppermute(send_b, 'brick', outside)  3.07 us
    ppermute x1, starting transfers between devices, body(): halo_c = lax.ppermute(far_end, 'brick', outside)  3.06 us
    ppermute x1, starting transfers between devices, body(): across = lax.ppermute(tomogram, 'scan', [(0, 2), (1, 3), (2, 0), (3, 1)])  2.65 us
    ppermute x1, waiting for transfers between devices, body(): across = lax.ppermute(tomogram, 'scan', [(0, 2), (1, 3), (2, 0), (3, 1)])  1.97 us
    ppermute x1, starting transfers between devices, body(): node_rhs = bottom + lax.ppermute(top, 'brick', up)  1.92 us
  transfers between devices with their start and end apart: 9, of which 6 were waited for; matrix products, arithmetic and copies ran while one was open for 0% of the time, Pallas kernels for 30%

profile of v5, /device:TPU:4, one launch (start us, length us, event | category | flops | bytes accessed | tf_op | source)
XLA Modules:
  0.0 41.4 jit_solution(17220038753428956189)
XLA Ops:
  0.6 1.3 %split.1 = (bf16[17,128,128]{2,1,0:T(8,128)(2,1)S(1)}, bf16[9,128,128]{2,1,0:T(8,128)(2,1)S(1)}, bf16[8,128,128]{2,1,0:T(8,128)(2,1)S(1)}) custom-call(f32[1,3,1,25]{3,2,1,0:T(1,128)} %nodes_in.1, bf16[1,32,128,128]{3,2,1,0:T(8,128)(2,1)} %slab.1), custom_call_target="tpu_custom_call" | custom-call | tf_op jit(solution)/shard_map/split/pallas_call | solution.py:304
  1.9 0.0 copy-start
  1.9 0.0 copy-start.2
  1.9 0.1 collective-permute-start
  2.0 2.7 %collective-permute-start.2 = (bf16[8,128,128]{2,1,0:T(8,128)(2,1)}, bf16[8,128,128]{2,1,0:T(8,128)(2,1)S(1)}, u32[]{:S(2)}, u32[]{:S(2)}) collective-permute-start(bf16[8,128,128]{2,1,0:T(8,128)(2,1)} %b0.1), channel_id=1, source_target_pairs={{0,2},{1,3},{2,0},{3,1},{4,6},{5,7},{6,4},{7,5},{8,10},{9,11},{10,... | collective-permute-start | bytes 786440 | tf_op jit(solution)/shard_map/ppermute | solution.py:580
  4.7 3.1 %collective-permute-start.1 = (bf16[9,128,128]{2,1,0:T(8,128)(2,1)S(1)}, bf16[9,128,128]{2,1,0:T(8,128)(2,1)S(1)}, u32[]{:S(2)}, u32[]{:S(2)}) collective-permute-start(bf16[9,128,128]{2,1,0:T(8,128)(2,1)S(1)} %get-tuple-element.27.far), channel_id=1, source_target_pairs={{4,8},{8,4},{12,16},{16,12},{20,24},{24,20},{5,9},{9,5},{13,17},{1... | collective-permute-start | bytes 884744 | tf_op jit(solution)/shard_map/ppermute | solution.py:584
  7.8 1.6 %collective-permute-start.4 = (bf16[8,128,128]{2,1,0:T(8,128)(2,1)}, bf16[8,128,128]{2,1,0:T(8,128)(2,1)S(1)}, u32[]{:S(2)}, u32[]{:S(2)}) collective-permute-start(bf16[8,128,128]{2,1,0:T(8,128)(2,1)} %b0.1), channel_id=1, source_target_pairs={{0,1},{1,0},{2,3},{3,2},{4,5},{5,4},{6,7},{7,6},{8,9},{9,8},{10,11... | collective-permute-start | bytes 786440 | tf_op jit(solution)/shard_map/ppermute | solution.py:587
  9.4 3.1 %collective-permute-start.3 = (bf16[8,128,128]{2,1,0:T(8,128)(2,1)S(1)}, bf16[8,128,128]{2,1,0:T(8,128)(2,1)S(1)}, u32[]{:S(2)}, u32[]{:S(2)}) collective-permute-start(bf16[8,128,128]{2,1,0:T(8,128)(2,1)S(1)} %get-tuple-element.28.far_end), channel_id=1, source_target_pairs={{4,8},{8,4},{12,16},{16,12},{20,24},{24,20},{5,9},{9,5},{13,17},{1... | collective-permute-start | bytes 786440 | tf_op jit(solution)/shard_map/ppermute | solution.py:585
  12.5 3.1 %windows.1 = (f32[4,17,40,128]{3,2,1,0:T(8,128)}, f32[4,17,40,128]{3,2,1,0:T(8,128)}) custom-call(bf16[17,128,128]{2,1,0:T(8,128)(2,1)S(1)} %get-tuple-element.26.near, bf16[9,128,128]{2,1,0:T(8,128)(2,1)S(1)} %get-tuple-element.27.far, bf16[8,128,128]{2,1,0:T(8,128)(2,1)S(1)} %get-tuple-element.28.far_end, ...), custom_call_target="tpu_custom_call" | custom-call | tf_op jit(solution)/shard_map/windows/pallas_call | solution.py:304
  15.6 2.0 %collective-permute-done.2.b2 = bf16[8,128,128]{2,1,0:T(8,128)(2,1)S(1)} collective-permute-done((bf16[8,128,128]{2,1,0:T(8,128)(2,1)}, bf16[8,128,128]{2,1,0:T(8,128)(2,1)S(1)}, u32[]{:S(2)}, u32[]{:S(2)}) %collective-permute-start.2) | collective-permute-done | bytes 262176 | tf_op jit(solution)/shard_map/ppermute | solution.py:580
  17.6 0.7 %collective-permute-start.5 = (bf16[8,128,128]{2,1,0:T(8,128)(2,1)S(1)}, bf16[8,128,128]{2,1,0:T(8,128)(2,1)S(1)}, u32[]{:S(2)}, u32[]{:S(2)}) collective-permute-start(bf16[8,128,128]{2,1,0:T(8,128)(2,1)S(1)} %collective-permute-done.2.b2), channel_id=1, source_target_pairs={{0,1},{1,0},{2,3},{3,2},{4,5},{5,4},{6,7},{7,6},{8,9},{9,8},{10,11... | collective-permute-start | bytes 786440 | tf_op jit(solution)/shard_map/ppermute | solution.py:591
  18.3 2.0 %first_half.1 = (f32[16,128,128]{2,1,0:T(8,128)S(1)}, f32[3,128,128]{2,1,0:T(8,128)S(1)}, f32[3,128,128]{2,1,0:T(8,128)S(1)}) custom-call(bf16[17,128,128]{2,1,0:T(8,128)(2,1)S(1)} %get-tuple-element.26.near, bf16[17,128,128]{2,1,0:T(8,128)(2,1)S(1)} %collective-permute-done.near_halo, bf16[9,128,128]{2,1,0:T(8,128)(2,1)S(1)} %collective-permute-done.1.far_halo, ...), custom_call_target="tpu_custom_call" | custom-call | tf_op jit(solution)/shard_map/first_half/pallas_call | solution.py:304
  20.3 1.4 %collective-permute-done.4.b1 = bf16[8,128,128]{2,1,0:T(8,128)(2,1)S(1)} collective-permute-done((bf16[8,128,128]{2,1,0:T(8,128)(2,1)}, bf16[8,128,128]{2,1,0:T(8,128)(2,1)S(1)}, u32[]{:S(2)}, u32[]{:S(2)}) %collective-permute-start.4) | collective-permute-done | bytes 262176 | tf_op jit(solution)/shard_map/ppermute | solution.py:587
  21.7 0.1 collective-permute-done.3.far_halo_end
  21.8 3.8 %second_half.1 = (f32[16,128,128]{2,1,0:T(8,128)S(1)}, bf16[32,128,128]{2,1,0:T(8,128)(2,1)}, f32[3,16,128,128]{3,2,1,0:T(8,128)S(1)}, f32[16,128,128]{2,1,0:T(8,128)S(1)}) custom-call(bf16[17,128,128]{2,1,0:T(8,128)(2,1)S(1)} %get-tuple-element.26.near, bf16[9,128,128]{2,1,0:T(8,128)(2,1)S(1)} %get-tuple-element.27.far, ...), custom_call_target="tpu_custom_call" | custom-call | tf_op jit(solution)/shard_map/second_half/pallas_call | solution.py:304
  25.6 1.2 %collective-permute-done.5.b3 = bf16[8,128,128]{2,1,0:T(8,128)(2,1)S(1)} collective-permute-done((bf16[8,128,128]{2,1,0:T(8,128)(2,1)S(1)}, bf16[8,128,128]{2,1,0:T(8,128)(2,1)S(1)}, u32[]{:S(2)}, u32[]{:S(2)}) %collective-permute-start.5) | collective-permute-done | bytes 262176 | tf_op jit(solution)/shard_map/ppermute | solution.py:591
  26.9 0.1 collective-permute-start.6
  27.0 3.1 %collective-permute-start.7 = (bf16[3,128,128]{2,1,0:T(8,128)(2,1)S(1)}, bf16[3,128,128]{2,1,0:T(8,128)(2,1)S(1)}, u32[]{:S(2)}, u32[]{:S(2)}) collective-permute-start(bf16[3,128,128]{2,1,0:T(8,128)(2,1)S(1)} %get-tuple-element.44), channel_id=1, source_target_pairs={{4,8},{8,4},{12,16},{16,12},{20,24},{24,20},{5,9},{9,5},{13,17},{1... | collective-permute-start | bytes 294920 | tf_op jit(solution)/shard_map/ppermute | solution.py:610
  30.1 3.6 %inner.1 = (bf16[32,128,128]{2,1,0:T(8,128)(2,1)}, f32[3,16,128,128]{3,2,1,0:T(8,128)S(1)}, f32[16,128,128]{2,1,0:T(8,128)S(1)}, f32[5,6,8,128]{3,2,1,0:T(8,128)S(1)}) custom-call(f32[16,128,128]{2,1,0:T(8,128)S(1)} %get-tuple-element.33.warp_a, f32[16,128,128]{2,1,0:T(8,128)S(1)} %get-tuple-element.36.warp_b, ...), custom_call_target="tpu_custom_call", output_to_operand_aliasing={{0}: (9, {})} | custom-call | tf_op jit(solution)/shard_map/inner/pallas_call | solution.py:304
  33.7 0.1 collective-permute-done.7.edge
  33.8 1.2 %outer.1 = (f32[3,1,25]{2,1,0:T(1,128)S(1)}, f32[3,1,25]{2,1,0:T(1,128)S(1)}) custom-call(bf16[3,128,128]{2,1,0:T(8,128)(2,1)S(1)} %collective-permute-done.7.edge, f32[3,16,128,128]{3,2,1,0:T(8,128)S(1)} %get-tuple-element.40.y_a, f32[16,128,128]{2,1,0:T(8,128)S(1)} %get-tuple-element.41.misfit_a, f32[3,16,128,128]{3,2,1,0:T(8,128)S(1)} %get-tuple-element.45.y_b, ...), custom_call_target="tpu_custom_call" | custom-call | tf_op jit(solution)/shard_map/outer/pallas_call | solution.py:304
  35.0 1.9 %collective-permute-start.8 = (f32[3,1,25]{2,1,0:T(1,128)S(1)}, f32[3,1,25]{2,1,0:T(1,128)S(1)}, u32[]{:S(2)}, u32[]{:S(2)}) collective-permute-start(f32[3,1,25]{2,1,0:T(1,128)S(1)} %get-tuple-element.49), channel_id=1, source_target_pairs={{0,4},{4,8},{8,12},{12,16},{16,20},{20,24},{24,28},{1,5},{5,9},{9,... | collective-permute-start | bytes 908 | tf_op jit(solution)/shard_map/ppermute | solution.py:613
  36.9 3.9 %collective-permute-done.8 = f32[3,1,25]{2,1,0:T(1,128)S(1)} collective-permute-done((f32[3,1,25]{2,1,0:T(1,128)S(1)}, f32[3,1,25]{2,1,0:T(1,128)S(1)}, u32[]{:S(2)}, u32[]{:S(2)}) %collective-permute-start.8) | collective-permute-done | bytes 332 | tf_op jit(solution)/shard_map/ppermute | solution.py:613
  40.8 0.6 %add_bitcast_fusion = f32[1,3,1,25]{3,2,1,0:T(1,128)} fusion(f32[3,1,25]{2,1,0:T(1,128)S(1)} %get-tuple-element.48, f32[3,1,25]{2,1,0:T(1,128)S(1)} %collective-permute-done.8), kind=kLoop, calls=%fused_computation.8 | loop fusion | flops 75 | bytes 900
  (11 shorter events, 0.1 us)
Async XLA Ops:
  1.9 19.9 %copy-start = (bf16[384,256]{1,0:T(8,128)(2,1)S(1)}, bf16[384,256]{1,0:T(8,128)(2,1)}, u32[]{:S(2)}) copy-start(bf16[384,256]{1,0:T(8,128)(2,1)} %constant.32.clone.x_bands) | copy-start | bytes 589828
  1.9 19.9 %copy-start.1 = (bf16[8,128,128]{2,1,0:T(8,128)(2,1)S(1)}, bf16[8,128,128]{2,1,0:T(8,128)(2,1)}, u32[]{:S(2)}) copy-start(bf16[8,128,128]{2,1,0:T(8,128)(2,1)} %b0.1) | copy-start | bytes 786436
  1.9 19.9 %copy-start.2 = (bf16[256,128]{1,0:T(8,128)(2,1)S(1)}, bf16[256,128]{1,0:T(8,128)(2,1)}, u32[]{:S(2)}) copy-start(bf16[256,128]{1,0:T(8,128)(2,1)} %constant.33.clone.y_bands) | copy-start | bytes 196612
  1.9 10.6 %collective-permute-start = (bf16[17,128,128]{2,1,0:T(8,128)(2,1)S(1)}, bf16[17,128,128]{2,1,0:T(8,128)(2,1)S(1)}, u32[]{:S(2)}, u32[]{:S(2)}) collective-permute-start(bf16[17,128,128]{2,1,0:T(8,128)(2,1)S(1)} %get-tuple-element.26.near), channel_id=1, source_target_pairs={{0,4},{4,0},{8,12},{12,8},{16,20},{20,16},{24,28},{28,24},{1,5},{5... | collective-permute-start | bytes 1671176 | tf_op jit(solution)/shard_map/ppermute | solution.py:583
  2.0 15.6 %collective-permute-start.2 = (bf16[8,128,128]{2,1,0:T(8,128)(2,1)}, bf16[8,128,128]{2,1,0:T(8,128)(2,1)S(1)}, u32[]{:S(2)}, u32[]{:S(2)}) collective-permute-start(bf16[8,128,128]{2,1,0:T(8,128)(2,1)} %b0.1), channel_id=1, source_target_pairs={{0,2},{1,3},{2,0},{3,1},{4,6},{5,7},{6,4},{7,5},{8,10},{9,11},{10,... | collective-permute-start | bytes 786440 | tf_op jit(solution)/shard_map/ppermute | solution.py:580
  4.7 13.6 %collective-permute-start.1 = (bf16[9,128,128]{2,1,0:T(8,128)(2,1)S(1)}, bf16[9,128,128]{2,1,0:T(8,128)(2,1)S(1)}, u32[]{:S(2)}, u32[]{:S(2)}) collective-permute-start(bf16[9,128,128]{2,1,0:T(8,128)(2,1)S(1)} %get-tuple-element.27.far), channel_id=1, source_target_pairs={{4,8},{8,4},{12,16},{16,12},{20,24},{24,20},{5,9},{9,5},{13,17},{1... | collective-permute-start | bytes 884744 | tf_op jit(solution)/shard_map/ppermute | solution.py:584
  7.8 13.9 %collective-permute-start.4 = (bf16[8,128,128]{2,1,0:T(8,128)(2,1)}, bf16[8,128,128]{2,1,0:T(8,128)(2,1)S(1)}, u32[]{:S(2)}, u32[]{:S(2)}) collective-permute-start(bf16[8,128,128]{2,1,0:T(8,128)(2,1)} %b0.1), channel_id=1, source_target_pairs={{0,1},{1,0},{2,3},{3,2},{4,5},{5,4},{6,7},{7,6},{8,9},{9,8},{10,11... | collective-permute-start | bytes 786440 | tf_op jit(solution)/shard_map/ppermute | solution.py:587
  9.4 12.3 %collective-permute-start.3 = (bf16[8,128,128]{2,1,0:T(8,128)(2,1)S(1)}, bf16[8,128,128]{2,1,0:T(8,128)(2,1)S(1)}, u32[]{:S(2)}, u32[]{:S(2)}) collective-permute-start(bf16[8,128,128]{2,1,0:T(8,128)(2,1)S(1)} %get-tuple-element.28.far_end), channel_id=1, source_target_pairs={{4,8},{8,4},{12,16},{16,12},{20,24},{24,20},{5,9},{9,5},{13,17},{1... | collective-permute-start | bytes 786440 | tf_op jit(solution)/shard_map/ppermute | solution.py:585
  17.6 9.2 %collective-permute-start.5 = (bf16[8,128,128]{2,1,0:T(8,128)(2,1)S(1)}, bf16[8,128,128]{2,1,0:T(8,128)(2,1)S(1)}, u32[]{:S(2)}, u32[]{:S(2)}) collective-permute-start(bf16[8,128,128]{2,1,0:T(8,128)(2,1)S(1)} %collective-permute-done.2.b2), channel_id=1, source_target_pairs={{0,1},{1,0},{2,3},{3,2},{4,5},{5,4},{6,7},{7,6},{8,9},{9,8},{10,11... | collective-permute-start | bytes 786440 | tf_op jit(solution)/shard_map/ppermute | solution.py:591
  26.9 3.2 %collective-permute-start.6 = (bf16[3,128,128]{2,1,0:T(8,128)(2,1)S(1)}, bf16[3,128,128]{2,1,0:T(8,128)(2,1)S(1)}, u32[]{:S(2)}, u32[]{:S(2)}) collective-permute-start(bf16[3,128,128]{2,1,0:T(8,128)(2,1)S(1)} %broadcast_select_fusion.1), channel_id=1, source_target_pairs={{0,4},{4,0},{8,12},{12,8},{16,20},{20,16},{24,28},{28,24},{1,5},{5... | collective-permute-start | bytes 294920 | tf_op jit(solution)/shard_map/ppermute | solution.py:609
  27.0 6.8 %collective-permute-start.7 = (bf16[3,128,128]{2,1,0:T(8,128)(2,1)S(1)}, bf16[3,128,128]{2,1,0:T(8,128)(2,1)S(1)}, u32[]{:S(2)}, u32[]{:S(2)}) collective-permute-start(bf16[3,128,128]{2,1,0:T(8,128)(2,1)S(1)} %get-tuple-element.44), channel_id=1, source_target_pairs={{4,8},{8,4},{12,16},{16,12},{20,24},{24,20},{5,9},{9,5},{13,17},{1... | collective-permute-start | bytes 294920 | tf_op jit(solution)/shard_map/ppermute | solution.py:610
  30.0 3.7 %copy-start.3 = (bf16[640,128]{1,0:T(8,128)(2,1)S(1)}, bf16[640,128]{1,0:T(8,128)(2,1)}, u32[]{:S(2)}) copy-start(bf16[640,128]{1,0:T(8,128)(2,1)} %constant.34.clone.hats) | copy-start | bytes 491524
  35.0 5.8 %collective-permute-start.8 = (f32[3,1,25]{2,1,0:T(1,128)S(1)}, f32[3,1,25]{2,1,0:T(1,128)S(1)}, u32[]{:S(2)}, u32[]{:S(2)}) collective-permute-start(f32[3,1,25]{2,1,0:T(1,128)S(1)} %get-tuple-element.49), channel_id=1, source_target_pairs={{0,4},{4,8},{8,12},{12,16},{16,20},{20,24},{24,28},{1,5},{5,9},{9,... | collective-permute-start | bytes 908 | tf_op jit(solution)/shard_map/ppermute | solution.py:613

commit v6 on v5

--- a/solution.py
+++ b/solution.py
@@ -77,9 +77,9 @@
         for i, (first, skip, count, out) in enumerate(parts)
     ]
     fetch = pltpu.make_async_copy(nodes_in, nodes, sems.at[len(parts)])
-    fetch.start()
     for c in copies:
         c.start()
+    fetch.start()
     fetch.wait()
     wide[...] = jnp.zeros_like(wide)
     for c in range(3):
@@ -468,7 +468,7 @@
                 sums[ey + 1, iz * 3 + k] += right
         return carry
 
-    lax.fori_loop(0, N // 8, rows_of, 0)
+    lax.fori_loop(0, N // 8, rows_of, 0, unroll=4 if end - begin == RADIUS else 1)
 
 
 def in_each_case(add, low, high, near_end):

time: 41.6 us -> 41.5 us (level)
  no operation moved by 1% of the time
where the time goes in v6:
time: 41.5 us; the launch traced here: 41.2 us
  starting transfers between devices  16.3 us (39%)
  Pallas kernels  14.8 us (36%)
  waiting for transfers between devices  8.67 us (21%)
  between operations  0.79 us (2%)
  other arithmetic  0.62 us (1%)
    pallas_call x6, Pallas kernels, call(): pl.pallas_call(kernel, out_shape=outs, in_specs=specs + [HBM] * len(hbm),...  14.8 us
    ppermute x1, waiting for transfers between devices, body(): node_rhs = bottom + lax.ppermute(top, 'brick', up)  3.87 us
    ppermute x1, starting transfers between devices, body(): halo_b = lax.ppermute(far, 'brick', outside)  3.1 us
    ppermute x1, starting transfers between devices, body(): edge_b = lax.ppermute(send_b, 'brick', outside)  3.07 us
    ppermute x1, starting transfers between devices, body(): halo_c = lax.ppermute(far_end, 'brick', outside)  3.06 us
    ppermute x1, starting transfers between devices, body(): across = lax.ppermute(tomogram, 'scan', [(0, 2), (1, 3), (2, 0), (3, 1)])  2.65 us
    ppermute x1, waiting for transfers between devices, body(): across = lax.ppermute(tomogram, 'scan', [(0, 2), (1, 3), (2, 0), (3, 1)])  2 us
    ppermute x1, starting transfers between devices, body(): node_rhs = bottom + lax.ppermute(top, 'brick', up)  1.92 us
  transfers between devices with their start and end apart: 9, of which 6 were waited for; matrix products, arithmetic and copies ran while one was open for 0% of the time, Pallas kernels for 30%

profile of v6, /device:TPU:4, one launch (start us, length us, event | category | flops | bytes accessed | tf_op | source)
XLA Modules:
  0.0 41.2 jit_solution(14313251701659900385)
XLA Ops:
  0.6 1.3 %split.1 = (bf16[17,128,128]{2,1,0:T(8,128)(2,1)S(1)}, bf16[9,128,128]{2,1,0:T(8,128)(2,1)S(1)}, bf16[8,128,128]{2,1,0:T(8,128)(2,1)S(1)}) custom-call(f32[1,3,1,25]{3,2,1,0:T(1,128)} %nodes_in.1, bf16[1,32,128,128]{3,2,1,0:T(8,128)(2,1)} %slab.1), custom_call_target="tpu_custom_call" | custom-call | tf_op jit(solution)/shard_map/split/pallas_call | solution.py:304
  1.9 0.0 copy-start
  1.9 0.0 copy-start.2
  1.9 0.1 collective-permute-start
  2.0 2.7 %collective-permute-start.2 = (bf16[8,128,128]{2,1,0:T(8,128)(2,1)}, bf16[8,128,128]{2,1,0:T(8,128)(2,1)S(1)}, u32[]{:S(2)}, u32[]{:S(2)}) collective-permute-start(bf16[8,128,128]{2,1,0:T(8,128)(2,1)} %b0.1), channel_id=1, source_target_pairs={{0,2},{1,3},{2,0},{3,1},{4,6},{5,7},{6,4},{7,5},{8,10},{9,11},{10,... | collective-permute-start | bytes 786440 | tf_op jit(solution)/shard_map/ppermute | solution.py:580
  4.7 3.1 %collective-permute-start.1 = (bf16[9,128,128]{2,1,0:T(8,128)(2,1)S(1)}, bf16[9,128,128]{2,1,0:T(8,128)(2,1)S(1)}, u32[]{:S(2)}, u32[]{:S(2)}) collective-permute-start(bf16[9,128,128]{2,1,0:T(8,128)(2,1)S(1)} %get-tuple-element.27.far), channel_id=1, source_target_pairs={{4,8},{8,4},{12,16},{16,12},{20,24},{24,20},{5,9},{9,5},{13,17},{1... | collective-permute-start | bytes 884744 | tf_op jit(solution)/shard_map/ppermute | solution.py:584
  7.8 1.6 %collective-permute-start.4 = (bf16[8,128,128]{2,1,0:T(8,128)(2,1)}, bf16[8,128,128]{2,1,0:T(8,128)(2,1)S(1)}, u32[]{:S(2)}, u32[]{:S(2)}) collective-permute-start(bf16[8,128,128]{2,1,0:T(8,128)(2,1)} %b0.1), channel_id=1, source_target_pairs={{0,1},{1,0},{2,3},{3,2},{4,5},{5,4},{6,7},{7,6},{8,9},{9,8},{10,11... | collective-permute-start | bytes 786440 | tf_op jit(solution)/shard_map/ppermute | solution.py:587
  9.4 3.1 %collective-permute-start.3 = (bf16[8,128,128]{2,1,0:T(8,128)(2,1)S(1)}, bf16[8,128,128]{2,1,0:T(8,128)(2,1)S(1)}, u32[]{:S(2)}, u32[]{:S(2)}) collective-permute-start(bf16[8,128,128]{2,1,0:T(8,128)(2,1)S(1)} %get-tuple-element.28.far_end), channel_id=1, source_target_pairs={{4,8},{8,4},{12,16},{16,12},{20,24},{24,20},{5,9},{9,5},{13,17},{1... | collective-permute-start | bytes 786440 | tf_op jit(solution)/shard_map/ppermute | solution.py:585
  12.5 3.1 %windows.1 = (f32[4,17,40,128]{3,2,1,0:T(8,128)}, f32[4,17,40,128]{3,2,1,0:T(8,128)}) custom-call(bf16[17,128,128]{2,1,0:T(8,128)(2,1)S(1)} %get-tuple-element.26.near, bf16[9,128,128]{2,1,0:T(8,128)(2,1)S(1)} %get-tuple-element.27.far, bf16[8,128,128]{2,1,0:T(8,128)(2,1)S(1)} %get-tuple-element.28.far_end, ...), custom_call_target="tpu_custom_call" | custom-call | tf_op jit(solution)/shard_map/windows/pallas_call | solution.py:304
  15.6 2.0 %collective-permute-done.2.b2 = bf16[8,128,128]{2,1,0:T(8,128)(2,1)S(1)} collective-permute-done((bf16[8,128,128]{2,1,0:T(8,128)(2,1)}, bf16[8,128,128]{2,1,0:T(8,128)(2,1)S(1)}, u32[]{:S(2)}, u32[]{:S(2)}) %collective-permute-start.2) | collective-permute-done | bytes 262176 | tf_op jit(solution)/shard_map/ppermute | solution.py:580
  17.6 0.7 %collective-permute-start.5 = (bf16[8,128,128]{2,1,0:T(8,128)(2,1)S(1)}, bf16[8,128,128]{2,1,0:T(8,128)(2,1)S(1)}, u32[]{:S(2)}, u32[]{:S(2)}) collective-permute-start(bf16[8,128,128]{2,1,0:T(8,128)(2,1)S(1)} %collective-permute-done.2.b2), channel_id=1, source_target_pairs={{0,1},{1,0},{2,3},{3,2},{4,5},{5,4},{6,7},{7,6},{8,9},{9,8},{10,11... | collective-permute-start | bytes 786440 | tf_op jit(solution)/shard_map/ppermute | solution.py:591
  18.3 2.0 %first_half.1 = (f32[16,128,128]{2,1,0:T(8,128)S(1)}, f32[3,128,128]{2,1,0:T(8,128)S(1)}, f32[3,128,128]{2,1,0:T(8,128)S(1)}) custom-call(bf16[17,128,128]{2,1,0:T(8,128)(2,1)S(1)} %get-tuple-element.26.near, bf16[17,128,128]{2,1,0:T(8,128)(2,1)S(1)} %collective-permute-done.near_halo, bf16[9,128,128]{2,1,0:T(8,128)(2,1)S(1)} %collective-permute-done.1.far_halo, ...), custom_call_target="tpu_custom_call" | custom-call | tf_op jit(solution)/shard_map/first_half/pallas_call | solution.py:304
  20.3 1.4 %collective-permute-done.4.b1 = bf16[8,128,128]{2,1,0:T(8,128)(2,1)S(1)} collective-permute-done((bf16[8,128,128]{2,1,0:T(8,128)(2,1)}, bf16[8,128,128]{2,1,0:T(8,128)(2,1)S(1)}, u32[]{:S(2)}, u32[]{:S(2)}) %collective-permute-start.4) | collective-permute-done | bytes 262176 | tf_op jit(solution)/shard_map/ppermute | solution.py:587
  21.7 0.1 collective-permute-done.3.far_halo_end
  21.8 3.8 %second_half.1 = (f32[16,128,128]{2,1,0:T(8,128)S(1)}, bf16[32,128,128]{2,1,0:T(8,128)(2,1)}, f32[3,16,128,128]{3,2,1,0:T(8,128)S(1)}, f32[16,128,128]{2,1,0:T(8,128)S(1)}) custom-call(bf16[17,128,128]{2,1,0:T(8,128)(2,1)S(1)} %get-tuple-element.26.near, bf16[9,128,128]{2,1,0:T(8,128)(2,1)S(1)} %get-tuple-element.27.far, ...), custom_call_target="tpu_custom_call" | custom-call | tf_op jit(solution)/shard_map/second_half/pallas_call | solution.py:304
  25.6 1.2 %collective-permute-done.5.b3 = bf16[8,128,128]{2,1,0:T(8,128)(2,1)S(1)} collective-permute-done((bf16[8,128,128]{2,1,0:T(8,128)(2,1)S(1)}, bf16[8,128,128]{2,1,0:T(8,128)(2,1)S(1)}, u32[]{:S(2)}, u32[]{:S(2)}) %collective-permute-start.5) | collective-permute-done | bytes 262176 | tf_op jit(solution)/shard_map/ppermute | solution.py:591
  26.9 0.1 collective-permute-start.6
  27.0 3.1 %collective-permute-start.7 = (bf16[3,128,128]{2,1,0:T(8,128)(2,1)S(1)}, bf16[3,128,128]{2,1,0:T(8,128)(2,1)S(1)}, u32[]{:S(2)}, u32[]{:S(2)}) collective-permute-start(bf16[3,128,128]{2,1,0:T(8,128)(2,1)S(1)} %get-tuple-element.44), channel_id=1, source_target_pairs={{4,8},{8,4},{12,16},{16,12},{20,24},{24,20},{5,9},{9,5},{13,17},{1... | collective-permute-start | bytes 294920 | tf_op jit(solution)/shard_map/ppermute | solution.py:610
  30.1 3.6 %inner.1 = (bf16[32,128,128]{2,1,0:T(8,128)(2,1)}, f32[3,16,128,128]{3,2,1,0:T(8,128)S(1)}, f32[16,128,128]{2,1,0:T(8,128)S(1)}, f32[5,6,8,128]{3,2,1,0:T(8,128)S(1)}) custom-call(f32[16,128,128]{2,1,0:T(8,128)S(1)} %get-tuple-element.33.warp_a, f32[16,128,128]{2,1,0:T(8,128)S(1)} %get-tuple-element.36.warp_b, ...), custom_call_target="tpu_custom_call", output_to_operand_aliasing={{0}: (9, {})} | custom-call | tf_op jit(solution)/shard_map/inner/pallas_call | solution.py:304
  33.7 0.1 collective-permute-done.7.edge
  33.8 1.0 %outer.1 = (f32[3,1,25]{2,1,0:T(1,128)S(1)}, f32[3,1,25]{2,1,0:T(1,128)S(1)}) custom-call(bf16[3,128,128]{2,1,0:T(8,128)(2,1)S(1)} %collective-permute-done.7.edge, f32[3,16,128,128]{3,2,1,0:T(8,128)S(1)} %get-tuple-element.40.y_a, f32[16,128,128]{2,1,0:T(8,128)S(1)} %get-tuple-element.41.misfit_a, f32[3,16,128,128]{3,2,1,0:T(8,128)S(1)} %get-tuple-element.45.y_b, ...), custom_call_target="tpu_custom_call" | custom-call | tf_op jit(solution)/shard_map/outer/pallas_call | solution.py:304
  34.8 1.9 %collective-permute-start.8 = (f32[3,1,25]{2,1,0:T(1,128)S(1)}, f32[3,1,25]{2,1,0:T(1,128)S(1)}, u32[]{:S(2)}, u32[]{:S(2)}) collective-permute-start(f32[3,1,25]{2,1,0:T(1,128)S(1)} %get-tuple-element.49), channel_id=1, source_target_pairs={{0,4},{4,8},{8,12},{12,16},{16,20},{20,24},{24,28},{1,5},{5,9},{9,... | collective-permute-start | bytes 908 | tf_op jit(solution)/shard_map/ppermute | solution.py:613
  36.7 3.9 %collective-permute-done.8 = f32[3,1,25]{2,1,0:T(1,128)S(1)} collective-permute-done((f32[3,1,25]{2,1,0:T(1,128)S(1)}, f32[3,1,25]{2,1,0:T(1,128)S(1)}, u32[]{:S(2)}, u32[]{:S(2)}) %collective-permute-start.8) | collective-permute-done | bytes 332 | tf_op jit(solution)/shard_map/ppermute | solution.py:613
  40.6 0.6 %add_bitcast_fusion = f32[1,3,1,25]{3,2,1,0:T(1,128)} fusion(f32[3,1,25]{2,1,0:T(1,128)S(1)} %get-tuple-element.48, f32[3,1,25]{2,1,0:T(1,128)S(1)} %collective-permute-done.8), kind=kLoop, calls=%fused_computation.8 | loop fusion | flops 75 | bytes 900
  (11 shorter events, 0.1 us)
Async XLA Ops:
  1.9 19.9 %copy-start = (bf16[384,256]{1,0:T(8,128)(2,1)S(1)}, bf16[384,256]{1,0:T(8,128)(2,1)}, u32[]{:S(2)}) copy-start(bf16[384,256]{1,0:T(8,128)(2,1)} %constant.32.clone.x_bands) | copy-start | bytes 589828
  1.9 19.9 %copy-start.1 = (bf16[8,128,128]{2,1,0:T(8,128)(2,1)S(1)}, bf16[8,128,128]{2,1,0:T(8,128)(2,1)}, u32[]{:S(2)}) copy-start(bf16[8,128,128]{2,1,0:T(8,128)(2,1)} %b0.1) | copy-start | bytes 786436
  1.9 19.9 %copy-start.2 = (bf16[256,128]{1,0:T(8,128)(2,1)S(1)}, bf16[256,128]{1,0:T(8,128)(2,1)}, u32[]{:S(2)}) copy-start(bf16[256,128]{1,0:T(8,128)(2,1)} %constant.33.clone.y_bands) | copy-start | bytes 196612
  1.9 10.6 %collective-permute-start = (bf16[17,128,128]{2,1,0:T(8,128)(2,1)S(1)}, bf16[17,128,128]{2,1,0:T(8,128)(2,1)S(1)}, u32[]{:S(2)}, u32[]{:S(2)}) collective-permute-start(bf16[17,128,128]{2,1,0:T(8,128)(2,1)S(1)} %get-tuple-element.26.near), channel_id=1, source_target_pairs={{0,4},{4,0},{8,12},{12,8},{16,20},{20,16},{24,28},{28,24},{1,5},{5... | collective-permute-start | bytes 1671176 | tf_op jit(solution)/shard_map/ppermute | solution.py:583
  2.0 15.6 %collective-permute-start.2 = (bf16[8,128,128]{2,1,0:T(8,128)(2,1)}, bf16[8,128,128]{2,1,0:T(8,128)(2,1)S(1)}, u32[]{:S(2)}, u32[]{:S(2)}) collective-permute-start(bf16[8,128,128]{2,1,0:T(8,128)(2,1)} %b0.1), channel_id=1, source_target_pairs={{0,2},{1,3},{2,0},{3,1},{4,6},{5,7},{6,4},{7,5},{8,10},{9,11},{10,... | collective-permute-start | bytes 786440 | tf_op jit(solution)/shard_map/ppermute | solution.py:580
  4.7 13.6 %collective-permute-start.1 = (bf16[9,128,128]{2,1,0:T(8,128)(2,1)S(1)}, bf16[9,128,128]{2,1,0:T(8,128)(2,1)S(1)}, u32[]{:S(2)}, u32[]{:S(2)}) collective-permute-start(bf16[9,128,128]{2,1,0:T(8,128)(2,1)S(1)} %get-tuple-element.27.far), channel_id=1, source_target_pairs={{4,8},{8,4},{12,16},{16,12},{20,24},{24,20},{5,9},{9,5},{13,17},{1... | collective-permute-start | bytes 884744 | tf_op jit(solution)/shard_map/ppermute | solution.py:584
  7.8 13.9 %collective-permute-start.4 = (bf16[8,128,128]{2,1,0:T(8,128)(2,1)}, bf16[8,128,128]{2,1,0:T(8,128)(2,1)S(1)}, u32[]{:S(2)}, u32[]{:S(2)}) collective-permute-start(bf16[8,128,128]{2,1,0:T(8,128)(2,1)} %b0.1), channel_id=1, source_target_pairs={{0,1},{1,0},{2,3},{3,2},{4,5},{5,4},{6,7},{7,6},{8,9},{9,8},{10,11... | collective-permute-start | bytes 786440 | tf_op jit(solution)/shard_map/ppermute | solution.py:587
  9.4 12.3 %collective-permute-start.3 = (bf16[8,128,128]{2,1,0:T(8,128)(2,1)S(1)}, bf16[8,128,128]{2,1,0:T(8,128)(2,1)S(1)}, u32[]{:S(2)}, u32[]{:S(2)}) collective-permute-start(bf16[8,128,128]{2,1,0:T(8,128)(2,1)S(1)} %get-tuple-element.28.far_end), channel_id=1, source_target_pairs={{4,8},{8,4},{12,16},{16,12},{20,24},{24,20},{5,9},{9,5},{13,17},{1... | collective-permute-start | bytes 786440 | tf_op jit(solution)/shard_map/ppermute | solution.py:585
  17.6 9.2 %collective-permute-start.5 = (bf16[8,128,128]{2,1,0:T(8,128)(2,1)S(1)}, bf16[8,128,128]{2,1,0:T(8,128)(2,1)S(1)}, u32[]{:S(2)}, u32[]{:S(2)}) collective-permute-start(bf16[8,128,128]{2,1,0:T(8,128)(2,1)S(1)} %collective-permute-done.2.b2), channel_id=1, source_target_pairs={{0,1},{1,0},{2,3},{3,2},{4,5},{5,4},{6,7},{7,6},{8,9},{9,8},{10,11... | collective-permute-start | bytes 786440 | tf_op jit(solution)/shard_map/ppermute | solution.py:591
  26.9 3.2 %collective-permute-start.6 = (bf16[3,128,128]{2,1,0:T(8,128)(2,1)S(1)}, bf16[3,128,128]{2,1,0:T(8,128)(2,1)S(1)}, u32[]{:S(2)}, u32[]{:S(2)}) collective-permute-start(bf16[3,128,128]{2,1,0:T(8,128)(2,1)S(1)} %broadcast_select_fusion.1), channel_id=1, source_target_pairs={{0,4},{4,0},{8,12},{12,8},{16,20},{20,16},{24,28},{28,24},{1,5},{5... | collective-permute-start | bytes 294920 | tf_op jit(solution)/shard_map/ppermute | solution.py:609
  27.0 6.8 %collective-permute-start.7 = (bf16[3,128,128]{2,1,0:T(8,128)(2,1)S(1)}, bf16[3,128,128]{2,1,0:T(8,128)(2,1)S(1)}, u32[]{:S(2)}, u32[]{:S(2)}) collective-permute-start(bf16[3,128,128]{2,1,0:T(8,128)(2,1)S(1)} %get-tuple-element.44), channel_id=1, source_target_pairs={{4,8},{8,4},{12,16},{16,12},{20,24},{24,20},{5,9},{9,5},{13,17},{1... | collective-permute-start | bytes 294920 | tf_op jit(solution)/shard_map/ppermute | solution.py:610
  30.0 3.7 %copy-start.3 = (bf16[640,128]{1,0:T(8,128)(2,1)S(1)}, bf16[640,128]{1,0:T(8,128)(2,1)}, u32[]{:S(2)}) copy-start(bf16[640,128]{1,0:T(8,128)(2,1)} %constant.34.clone.hats) | copy-start | bytes 491524
  34.8 5.8 %collective-permute-start.8 = (f32[3,1,25]{2,1,0:T(1,128)S(1)}, f32[3,1,25]{2,1,0:T(1,128)S(1)}, u32[]{:S(2)}, u32[]{:S(2)}) collective-permute-start(f32[3,1,25]{2,1,0:T(1,128)S(1)} %get-tuple-element.49), channel_id=1, source_target_pairs={{0,4},{4,8},{8,12},{12,16},{16,20},{20,24},{24,28},{1,5},{5,9},{9,... | collective-permute-start | bytes 908 | tf_op jit(solution)/shard_map/ppermute | solution.py:613
